TPU v7x, 32 devices: a whole 2x2x4 slice. The times are simulated.
32 devices in a mesh: ctx: 8 (over z, y), ws: 4 (over x, core).
Axes of the slice: x: 2, y: 2, z: 4, core: 2. Of those that a mesh axis runs over, the one named last changes fastest.
Arguments:
- inputs: bfloat16 [4, 1024, 2048], P('ws', 'ctx'), may hold values from -6 to 6
- grad_output: bfloat16 [4, 1024, 2048], P('ws', 'ctx'), may hold values from -6 to 6
- routes: int32 [4, 1024, 8], P('ws', 'ctx'), may hold values from 0 to 31, all different within a row; in each aligned block of 128 rows (0 to 127, 128 to 255, ..., all dimensions but the last counted through in order) at most 48 rows name the same one
- doc_lengths: int32 [4, 4], P('ws'), may hold values from 32 to 576, as said below
- norm_attn: bfloat16 [2048], P(('ctx', 'ws')), may hold values from 0.099609375 to 1.8984375
- w_query: bfloat16 [2048, 4096], P(('ctx', 'ws')), may hold values from -0.125 to 0.125
- key_projection: bfloat16 [2048, 512], P(('ctx', 'ws')), may hold values from -0.125 to 0.125
- value_projection: bfloat16 [2048, 512], P(('ctx', 'ws')), may hold values from -0.125 to 0.125
- query_norm: bfloat16 [128], P(('ctx', 'ws')), may hold values from 0.099609375 to 1.8984375
- key_norm: bfloat16 [128], P(('ctx', 'ws')), may hold values from 0.099609375 to 1.8984375
- w_out: bfloat16 [4096, 2048], P(('ctx', 'ws')), may hold values from -0.5 to 0.5
- norm_ffn: bfloat16 [2048], P(('ctx', 'ws')), may hold values from 0.099609375 to 1.8984375
- w_router: bfloat16 [2048, 32], P(('ctx', 'ws')), may hold values from -0.0625 to 0.0625
- expert_gate: bfloat16 [32, 2048, 768], P(('ctx', 'ws')), may hold values from -0.125 to 0.125
- expert_up: bfloat16 [32, 2048, 768], P(('ctx', 'ws')), may hold values from -0.125 to 0.125
- expert_down: bfloat16 [32, 768, 2048], P(('ctx', 'ws')), may hold values from -1.25 to 1.25
Outputs:
- output: bfloat16 [4, 1024, 2048], P('ws', 'ctx')
- grad_input: float32 [4, 1024, 2048], P('ws', 'ctx')
- grad_norm_attn: float32 [2048], P(('ctx', 'ws'))
- grad_w_query: float32 [2048, 4096], P(('ctx', 'ws'))
- grad_w_key: float32 [2048, 512], P(('ctx', 'ws'))
- grad_w_value: float32 [2048, 512], P(('ctx', 'ws'))
- grad_query_norm: float32 [128], P(('ctx', 'ws'))
- grad_key_norm: float32 [128], P(('ctx', 'ws'))
- grad_w_out: float32 [4096, 2048], P(('ctx', 'ws'))
- grad_norm_ffn: float32 [2048], P(('ctx', 'ws'))
- grad_w_router: float32 [2048, 32], P(('ctx', 'ws'))
- grad_expert_gate: float32 [32, 2048, 768], P(('ctx', 'ws'))
- grad_expert_up: float32 [32, 2048, 768], P(('ctx', 'ws'))
- grad_expert_down: float32 [32, 768, 2048], P(('ctx', 'ws'))
Inputs may be any that keep to these rules, and one draw needn't show every extreme that they name: `routes`: each row names 8 different experts. Among the rows of one device no expert is named more than 48 times, and in every draw some expert is named exactly 48 times there. `doc_lengths`: the first document of each sequence has between 513 and 576 tokens, the others between 32 and 128; rows whose place lies past the sum are padding.
All inputs are finite; a program needn't handle non-finite values.
Results may differ from a plain program's by a relative error of at most 0.025.
Values may be sent and summed in bfloat16 or wider, within the bound.
A program may use at most 256 MiB of HBM per device.

v0:
```python
import jax
import jax.numpy as jnp
from jax import lax
from jax.sharding import PartitionSpec as P

QUERY_HEADS = 32
KEY_VALUE_HEADS = 4
HEAD_DIM = 128
TOPK = 8


EPS = 1e-06
THETA = 1000000.0
MASK_FILL = -1e30
TOP_PRECISION = lax.Precision.HIGHEST
SINGLE_FLOAT = jnp.float32
BRAIN_FLOAT_TYPE = jnp.bfloat16


def rms_scale(values, norm_gain):
    return values * lax.rsqrt(jnp.mean(values * values, axis=-1, keepdims=True) + EPS) * norm_gain


def rotate(values, positions):
    half_dim = values.shape[-1] // 2
    frequency = THETA ** (-2.0 * jnp.arange(half_dim, dtype=jnp.float32) / values.shape[-1])
    angle = positions.astype(jnp.float32)[:, None] * frequency[None, :]
    cosine = jnp.cos(angle)[:, None, :]
    sine_part = jnp.sin(angle)[:, None, :]
    first_half = values[..., :half_dim]
    second_half = values[..., half_dim:]
    return jnp.concatenate(
        [
            first_half * cosine - second_half * sine_part,
            second_half * cosine + first_half * sine_part,
        ],
        axis=-1,
    )


def head_prepare(raw_heads, norm_gain, positions):
    return rotate(rms_scale(raw_heads, norm_gain), positions)


def swiglu(gate_part, up_part):
    return jax.nn.silu(gate_part) * up_part


def stored_positions(row_index, tokens_per_shard, ctx_count):
    device_row = row_index // tokens_per_shard
    within = row_index % tokens_per_shard
    half_block = tokens_per_shard // 2
    block_index = jnp.where(within < half_block, device_row, 2 * ctx_count - 1 - device_row)
    return block_index * half_block + within % half_block


def segment_ids(doc_lengths, positions):
    doc_ends = jnp.cumsum(doc_lengths, dtype=jnp.int32)
    return jnp.sum(
        (positions[:, None] >= doc_ends[None, :]).astype(jnp.int32), axis=1, dtype=jnp.int32
    )


def slot_ranks(flat_routes, expert_count):
    expert_hits = (
        flat_routes[:, None] == jnp.arange(expert_count, dtype=jnp.int32)[None, :]
    ).astype(jnp.int32)
    running = jnp.cumsum(expert_hits, axis=0, dtype=jnp.int32) - 1
    return jnp.sum(expert_hits * running, axis=1, dtype=jnp.int32)


def send_inputs(flat_rows):
    moved = lax.all_to_all(flat_rows, ("ctx", "ws"), split_axis=0, concat_axis=0, tiled=True)
    return moved


def send_outputs(flat_rows):
    moved = lax.all_to_all(flat_rows, ("ctx", "ws"), split_axis=0, concat_axis=0, tiled=True)
    return moved


def send_out_grads(flat_rows):
    moved = lax.all_to_all(flat_rows, ("ctx", "ws"), split_axis=0, concat_axis=0, tiled=True)
    return moved


def send_in_grads(flat_rows):
    moved = lax.all_to_all(flat_rows, ("ctx", "ws"), split_axis=0, concat_axis=0, tiled=True)
    return moved


def flat_rows(grid_sum):
    return grid_sum.reshape((-1,) + grid_sum.shape[3:])


def to_expert_major(arrived, expert_local):
    device_count, row_span, model_width = arrived.shape
    capacity = row_span // expert_local
    shaped = arrived.reshape(device_count, expert_local, capacity, model_width)
    return shaped.transpose(1, 0, 2, 3).reshape(expert_local, device_count * capacity, model_width)


def to_device_major(expert_rows, device_count):
    expert_local, row_span, model_width = expert_rows.shape
    capacity = row_span // device_count
    shaped = expert_rows.reshape(expert_local, device_count, capacity, model_width)
    return shaped.transpose(1, 0, 2, 3).reshape(device_count, expert_local * capacity, model_width)


def body(
    inputs,
    grad_output,
    routes,
    doc_lengths,
    norm_attn,
    w_query,
    key_projection,
    value_projection,
    query_norm,
    key_norm,
    w_out,
    norm_ffn,
    w_router,
    expert_gate,
    expert_up,
    expert_down,
):
    ctx_count = lax.axis_size("ctx")
    device_count = ctx_count * lax.axis_size("ws")
    tokens_per_shard = inputs.shape[1]
    model_width = inputs.shape[2]
    sequence_tokens = tokens_per_shard * ctx_count
    expert_count = w_router.shape[1]
    expert_local = expert_gate.shape[0]
    capacity = max(2, tokens_per_shard * TOPK * 3 // (2 * device_count))
    query_group_size = QUERY_HEADS // KEY_VALUE_HEADS
    logit_scale = HEAD_DIM ** (-0.5)
    single_key_block = min(512, sequence_tokens)
    count_of_blocks = sequence_tokens // single_key_block
    ctx_index = lax.axis_index("ctx")
    positions_all = stored_positions(
        jnp.arange(sequence_tokens, dtype=jnp.int32), tokens_per_shard, ctx_count
    )
    segments_all = segment_ids(doc_lengths[0], positions_all)
    local_positions = lax.dynamic_slice_in_dim(
        positions_all, ctx_index * tokens_per_shard, tokens_per_shard
    )
    segments_own = lax.dynamic_slice_in_dim(
        segments_all, ctx_index * tokens_per_shard, tokens_per_shard
    )
    validity = (segments_own < doc_lengths.shape[1]).astype(SINGLE_FLOAT)
    shards = (
        norm_attn,
        w_query,
        key_projection,
        value_projection,
        query_norm,
        key_norm,
        w_out,
        norm_ffn,
        w_router,
    )
    gathered = (
        lax.all_gather(shards[0], ("ctx", "ws"), axis=0, tiled=True),
        lax.all_gather(shards[1], ("ctx", "ws"), axis=0, tiled=True),
        lax.all_gather(shards[2], ("ctx", "ws"), axis=0, tiled=True),
        lax.all_gather(shards[3], ("ctx", "ws"), axis=0, tiled=True),
        lax.all_gather(shards[4], ("ctx", "ws"), axis=0, tiled=True),
        lax.all_gather(shards[5], ("ctx", "ws"), axis=0, tiled=True),
        lax.all_gather(shards[6], ("ctx", "ws"), axis=0, tiled=True),
        lax.all_gather(shards[7], ("ctx", "ws"), axis=0, tiled=True),
        lax.all_gather(shards[8], ("ctx", "ws"), axis=0, tiled=True),
    )
    (
        attn_gain,
        query_matrix,
        key_matrix,
        value_matrix,
        query_gain,
        key_norm_gain,
        output_matrix,
        ffn_gain,
        router_matrix,
    ) = gathered
    attn_gain = attn_gain.astype(SINGLE_FLOAT)
    query_gain = query_gain.astype(SINGLE_FLOAT)
    key_norm_gain = key_norm_gain.astype(SINGLE_FLOAT)
    ffn_gain = ffn_gain.astype(SINGLE_FLOAT)
    layer_in = inputs[0].astype(SINGLE_FLOAT)
    normalized_rows = rms_scale(layer_in, attn_gain).astype(BRAIN_FLOAT_TYPE)
    unnormed_queries = jnp.dot(
        normalized_rows, query_matrix, preferred_element_type=SINGLE_FLOAT
    ).reshape(tokens_per_shard, QUERY_HEADS, HEAD_DIM)
    unnormed_keys = jnp.dot(
        normalized_rows, key_matrix, preferred_element_type=SINGLE_FLOAT
    ).reshape(tokens_per_shard, KEY_VALUE_HEADS, HEAD_DIM)
    value_low = jnp.dot(normalized_rows, value_matrix, preferred_element_type=SINGLE_FLOAT).astype(
        BRAIN_FLOAT_TYPE
    )
    query_rows = head_prepare(unnormed_queries, query_gain, local_positions).astype(
        BRAIN_FLOAT_TYPE
    )
    key_low = (
        head_prepare(unnormed_keys, key_norm_gain, local_positions)
        .astype(BRAIN_FLOAT_TYPE)
        .reshape(tokens_per_shard, KEY_VALUE_HEADS * HEAD_DIM)
    )
    every_key, every_value = (
        lax.all_gather(key_low, "ctx", axis=0, tiled=True),
        lax.all_gather(value_low, "ctx", axis=0, tiled=True),
    )
    grouped_queries = query_rows.reshape(
        tokens_per_shard, KEY_VALUE_HEADS, query_group_size, HEAD_DIM
    )
    blocked_keys = every_key.reshape(count_of_blocks, single_key_block, KEY_VALUE_HEADS, HEAD_DIM)
    blocked_values = every_value.reshape(
        count_of_blocks, single_key_block, KEY_VALUE_HEADS, HEAD_DIM
    )
    position_blocks = positions_all.reshape(count_of_blocks, single_key_block)
    segment_blocks = segments_all.reshape(count_of_blocks, single_key_block)

    def scores_for(block_keys, block_positions, block_segments):
        raw_scores = (
            jnp.einsum(
                "tkgd,jkd->kgtj", grouped_queries, block_keys, preferred_element_type=SINGLE_FLOAT
            )
            * logit_scale
        )
        allowed = (segments_own[:, None] == block_segments[None, :]) & (
            block_positions[None, :] <= local_positions[:, None]
        )
        return (raw_scores, allowed[None, None])

    def stats_step(running, pieces):
        maximum, denominator = running
        block_keys, block_positions, block_segments = pieces
        raw_scores, allowed = scores_for(block_keys, block_positions, block_segments)
        masked = jnp.where(allowed, raw_scores, MASK_FILL)
        new_maximum = jnp.maximum(maximum, jnp.max(masked, axis=-1))
        weights = jnp.where(allowed, jnp.exp(masked - new_maximum[..., None]), 0.0)
        denominator = denominator * jnp.exp(maximum - new_maximum) + jnp.sum(weights, axis=-1)
        return ((new_maximum, denominator), None)

    stats_init = (
        jnp.full((KEY_VALUE_HEADS, query_group_size, tokens_per_shard), MASK_FILL, SINGLE_FLOAT),
        jnp.zeros((KEY_VALUE_HEADS, query_group_size, tokens_per_shard), SINGLE_FLOAT),
    )
    (maximum, denominator), _ = lax.scan(
        stats_step, stats_init, (blocked_keys, position_blocks, segment_blocks)
    )

    def probs_for(raw_scores, allowed):
        return (
            jnp.where(allowed, jnp.exp(raw_scores - maximum[..., None]), 0.0)
            / denominator[..., None]
        )

    def value_update(running, pieces):
        block_keys, block_values, block_positions, block_segments = pieces
        raw_scores, allowed = scores_for(block_keys, block_positions, block_segments)
        softmaxed = probs_for(raw_scores, allowed).astype(BRAIN_FLOAT_TYPE)
        running = running + jnp.einsum(
            "kgtj,jkd->tkgd", softmaxed, block_values, preferred_element_type=SINGLE_FLOAT
        )
        return (running, None)

    inputs_per_block = (blocked_keys, blocked_values, position_blocks, segment_blocks)
    attended, _ = lax.scan(
        value_update,
        jnp.zeros((tokens_per_shard, KEY_VALUE_HEADS, query_group_size, HEAD_DIM), SINGLE_FLOAT),
        inputs_per_block,
    )
    attn_low = attended.reshape(tokens_per_shard, QUERY_HEADS * HEAD_DIM).astype(BRAIN_FLOAT_TYPE)
    hidden_state = layer_in + jnp.dot(attn_low, output_matrix, preferred_element_type=SINGLE_FLOAT)
    combined_rows = rms_scale(hidden_state, ffn_gain).astype(BRAIN_FLOAT_TYPE)
    router_scores = jnp.dot(combined_rows, router_matrix, preferred_element_type=SINGLE_FLOAT)
    own_routes = routes[0]
    route_mask = (
        own_routes[:, :, None] == jnp.arange(expert_count, dtype=jnp.int32)[None, None, :]
    ).astype(SINGLE_FLOAT)
    chosen = jnp.einsum("tke,te->tk", route_mask, router_scores, precision=TOP_PRECISION)
    gate_share = jax.nn.softmax(chosen, axis=-1)
    flat_routes = own_routes.reshape(-1)
    slot_index = flat_routes * capacity + slot_ranks(flat_routes, expert_count)
    entries = tokens_per_shard * TOPK
    source_slot = (
        jnp.full((expert_count * capacity,), entries, jnp.int32)
        .at[slot_index]
        .set(jnp.arange(entries, dtype=jnp.int32))
    )
    padded_in = jnp.concatenate(
        [combined_rows, jnp.zeros((1, model_width), BRAIN_FLOAT_TYPE)], axis=0
    )
    outgoing = padded_in[source_slot // TOPK].reshape(device_count, -1, model_width)
    expert_in = to_expert_major(send_inputs(outgoing), expert_local)
    gate_hidden = jnp.einsum(
        "erd,edf->erf", expert_in, expert_gate, preferred_element_type=SINGLE_FLOAT
    )
    up_hidden = jnp.einsum(
        "erd,edf->erf", expert_in, expert_up, preferred_element_type=SINGLE_FLOAT
    )
    hidden = swiglu(gate_hidden, up_hidden).astype(BRAIN_FLOAT_TYPE)
    expert_out = jnp.einsum(
        "erf,efd->erd", hidden, expert_down, preferred_element_type=SINGLE_FLOAT
    ).astype(BRAIN_FLOAT_TYPE)
    returned = send_outputs(to_device_major(expert_out, device_count)).reshape(
        expert_count * capacity, model_width
    )
    picked = returned[slot_index].reshape(tokens_per_shard, TOPK, model_width)
    moe_sum = jnp.sum(gate_share[:, :, None] * picked.astype(SINGLE_FLOAT), axis=1)
    output = (hidden_state + moe_sum).astype(BRAIN_FLOAT_TYPE)
    d_layer = grad_output[0].astype(SINGLE_FLOAT) * validity[:, None]
    d_gate_share = jnp.sum(d_layer[:, None, :] * picked.astype(SINGLE_FLOAT), axis=-1)
    d_chosen = gate_share * (
        d_gate_share - jnp.sum(gate_share * d_gate_share, axis=-1, keepdims=True)
    )
    d_logits = jnp.einsum("tke,tk->te", route_mask, d_chosen, precision=TOP_PRECISION).astype(
        BRAIN_FLOAT_TYPE
    )
    d_copies = (
        (gate_share[:, :, None] * d_layer[:, None, :])
        .astype(BRAIN_FLOAT_TYPE)
        .reshape(entries, model_width)
    )
    d_padded = jnp.concatenate([d_copies, jnp.zeros((1, model_width), BRAIN_FLOAT_TYPE)], axis=0)
    d_outgoing = d_padded[source_slot].reshape(device_count, -1, model_width)
    d_expert_out = to_expert_major(send_out_grads(d_outgoing), expert_local)
    d_hidden = jnp.einsum(
        "erd,efd->erf", d_expert_out, expert_down, preferred_element_type=SINGLE_FLOAT
    )
    grad_down = jnp.einsum(
        "erf,erd->efd", hidden, d_expert_out, preferred_element_type=SINGLE_FLOAT
    )
    _, swiglu_back = jax.vjp(swiglu, gate_hidden, up_hidden)
    d_gate_hidden, d_up_hidden = swiglu_back(d_hidden)
    d_gate_low = d_gate_hidden.astype(BRAIN_FLOAT_TYPE)
    d_up_low = d_up_hidden.astype(BRAIN_FLOAT_TYPE)
    grad_gate = jnp.einsum(
        "erd,erf->edf", expert_in, d_gate_low, preferred_element_type=SINGLE_FLOAT
    )
    grad_up = jnp.einsum("erd,erf->edf", expert_in, d_up_low, preferred_element_type=SINGLE_FLOAT)
    d_expert_in = jnp.einsum(
        "erf,edf->erd", d_gate_low, expert_gate, preferred_element_type=SINGLE_FLOAT
    )
    d_expert_in = (
        d_expert_in
        + jnp.einsum("erf,edf->erd", d_up_low, expert_up, preferred_element_type=SINGLE_FLOAT)
    ).astype(BRAIN_FLOAT_TYPE)
    d_returned = send_in_grads(to_device_major(d_expert_in, device_count)).reshape(
        expert_count * capacity, model_width
    )
    d_slots = d_returned[slot_index].reshape(tokens_per_shard, TOPK, model_width)
    d_mixed = jnp.sum(d_slots.astype(SINGLE_FLOAT), axis=1) + jnp.einsum(
        "te,de->td", d_logits, router_matrix, preferred_element_type=SINGLE_FLOAT
    )
    grad_router = jnp.einsum(
        "td,te->de", combined_rows, d_logits, preferred_element_type=SINGLE_FLOAT
    )
    _, ffn_norm_back = jax.vjp(rms_scale, hidden_state, ffn_gain)
    d_state_norm, grad_ffn_gain = ffn_norm_back(d_mixed)
    d_state = d_layer + d_state_norm
    d_state_low = d_state.astype(BRAIN_FLOAT_TYPE)
    grad_out_weight = jnp.einsum(
        "tc,td->cd", attn_low, d_state_low, preferred_element_type=SINGLE_FLOAT
    )
    attention_gradient = jnp.einsum(
        "td,cd->tc", d_state_low, output_matrix, preferred_element_type=SINGLE_FLOAT
    ).astype(BRAIN_FLOAT_TYPE)
    attention_gradient = attention_gradient.reshape(
        tokens_per_shard, KEY_VALUE_HEADS, query_group_size, HEAD_DIM
    )
    row_delta = jnp.sum(attention_gradient.astype(SINGLE_FLOAT) * attended, axis=-1).transpose(
        1, 2, 0
    )

    def backward_step(d_query_acc, pieces):
        block_keys, block_values, block_positions, block_segments = pieces
        raw_scores, allowed = scores_for(block_keys, block_positions, block_segments)
        softmaxed = probs_for(raw_scores, allowed)
        d_probs = jnp.einsum(
            "tkgd,jkd->kgtj", attention_gradient, block_values, preferred_element_type=SINGLE_FLOAT
        )
        d_scores = (softmaxed * (d_probs - row_delta[..., None])).astype(BRAIN_FLOAT_TYPE)
        d_query_acc = d_query_acc + jnp.einsum(
            "kgtj,jkd->tkgd", d_scores, block_keys, preferred_element_type=SINGLE_FLOAT
        )
        d_key_block = jnp.einsum(
            "kgtj,tkgd->jkd", d_scores, grouped_queries, preferred_element_type=SINGLE_FLOAT
        )
        d_value_block = jnp.einsum(
            "kgtj,tkgd->jkd",
            softmaxed.astype(BRAIN_FLOAT_TYPE),
            attention_gradient,
            preferred_element_type=SINGLE_FLOAT,
        )
        return (d_query_acc, (d_key_block, d_value_block))

    d_query_acc, (key_block_gradients, value_block_gradients) = lax.scan(
        backward_step,
        jnp.zeros((tokens_per_shard, KEY_VALUE_HEADS, query_group_size, HEAD_DIM), SINGLE_FLOAT),
        inputs_per_block,
    )
    every_key_gradient = (key_block_gradients * logit_scale).reshape(
        sequence_tokens, KEY_VALUE_HEADS * HEAD_DIM
    )
    every_value_gradient = value_block_gradients.reshape(
        sequence_tokens, KEY_VALUE_HEADS * HEAD_DIM
    )
    key_gradients, d_values = (
        lax.psum_scatter(
            every_key_gradient.astype(jnp.bfloat16), "ctx", scatter_dimension=0, tiled=True
        ).astype(jnp.float32),
        lax.psum_scatter(
            every_value_gradient.astype(jnp.bfloat16), "ctx", scatter_dimension=0, tiled=True
        ).astype(jnp.float32),
    )
    _, query_back = jax.vjp(
        lambda raw_heads, norm_gain: head_prepare(raw_heads, norm_gain, local_positions),
        unnormed_queries,
        query_gain,
    )
    d_query_raw, grad_query_gain = query_back(
        (d_query_acc * logit_scale).reshape(tokens_per_shard, QUERY_HEADS, HEAD_DIM)
    )
    _, key_backward = jax.vjp(
        lambda raw_heads, norm_gain: head_prepare(raw_heads, norm_gain, local_positions),
        unnormed_keys,
        key_norm_gain,
    )
    raw_key_gradient, key_gain_gradient = key_backward(
        key_gradients.reshape(tokens_per_shard, KEY_VALUE_HEADS, HEAD_DIM)
    )
    d_query_low = d_query_raw.reshape(tokens_per_shard, QUERY_HEADS * HEAD_DIM).astype(
        BRAIN_FLOAT_TYPE
    )
    key_gradient_lowprec = raw_key_gradient.reshape(
        tokens_per_shard, KEY_VALUE_HEADS * HEAD_DIM
    ).astype(BRAIN_FLOAT_TYPE)
    d_value_low = d_values.astype(BRAIN_FLOAT_TYPE)
    grad_query_weight = jnp.einsum(
        "td,tc->dc", normalized_rows, d_query_low, preferred_element_type=SINGLE_FLOAT
    )
    grad_key_weight = jnp.einsum(
        "td,tc->dc", normalized_rows, key_gradient_lowprec, preferred_element_type=SINGLE_FLOAT
    )
    grad_value_weight = jnp.einsum(
        "td,tc->dc", normalized_rows, d_value_low, preferred_element_type=SINGLE_FLOAT
    )
    d_normed = jnp.einsum(
        "tc,dc->td", d_query_low, query_matrix, preferred_element_type=SINGLE_FLOAT
    )
    d_normed = d_normed + jnp.einsum(
        "tc,dc->td", key_gradient_lowprec, key_matrix, preferred_element_type=SINGLE_FLOAT
    )
    d_normed = d_normed + jnp.einsum(
        "tc,dc->td", d_value_low, value_matrix, preferred_element_type=SINGLE_FLOAT
    )
    _, attn_norm_back = jax.vjp(rms_scale, layer_in, attn_gain)
    d_input_norm, grad_attn_gain = attn_norm_back(d_normed)
    grad_input = d_state + d_input_norm
    reduced = (
        lax.psum_scatter(grad_attn_gain, ("ctx", "ws"), scatter_dimension=0, tiled=True),
        lax.psum_scatter(grad_query_weight, ("ctx", "ws"), scatter_dimension=0, tiled=True),
        lax.psum_scatter(grad_key_weight, ("ctx", "ws"), scatter_dimension=0, tiled=True),
        lax.psum_scatter(grad_value_weight, ("ctx", "ws"), scatter_dimension=0, tiled=True),
        lax.psum_scatter(grad_query_gain, ("ctx", "ws"), scatter_dimension=0, tiled=True),
        lax.psum_scatter(key_gain_gradient, ("ctx", "ws"), scatter_dimension=0, tiled=True),
        lax.psum_scatter(grad_out_weight, ("ctx", "ws"), scatter_dimension=0, tiled=True),
        lax.psum_scatter(grad_ffn_gain, ("ctx", "ws"), scatter_dimension=0, tiled=True),
        lax.psum_scatter(grad_router, ("ctx", "ws"), scatter_dimension=0, tiled=True),
    )
    return (
        output[None],
        grad_input[None],
        reduced[0],
        reduced[1],
        reduced[2],
        reduced[3],
        reduced[4],
        reduced[5],
        reduced[6],
        reduced[7],
        reduced[8],
        grad_gate,
        grad_up,
        grad_down,
    )


def solution(mesh):
    placed = (
        P("ws", "ctx", None),
        P("ws", "ctx", None),
        P("ws", "ctx", None),
        P("ws", None),
        P(("ctx", "ws")),
        P(("ctx", "ws"), None),
        P(("ctx", "ws"), None),
        P(("ctx", "ws"), None),
        P(("ctx", "ws")),
        P(("ctx", "ws")),
        P(("ctx", "ws"), None),
        P(("ctx", "ws")),
        P(("ctx", "ws"), None),
        P(("ctx", "ws"), None, None),
        P(("ctx", "ws"), None, None),
        P(("ctx", "ws"), None, None),
    )
    return jax.shard_map(
        body,
        mesh=mesh,
        in_specs=placed,
        out_specs=(
            P("ws", "ctx", None),
            P("ws", "ctx", None),
            P(("ctx", "ws")),
            P(("ctx", "ws"), None),
            P(("ctx", "ws"), None),
            P(("ctx", "ws"), None),
            P(("ctx", "ws")),
            P(("ctx", "ws")),
            P(("ctx", "ws"), None),
            P(("ctx", "ws")),
            P(("ctx", "ws"), None),
            P(("ctx", "ws"), None, None),
            P(("ctx", "ws"), None, None),
            P(("ctx", "ws"), None, None),
        ),
        check_vma=False,
    )
```

profile of v0, /device:TPU:8, one launch (start us, length us, event | category | flops | bytes accessed | tf_op | source)
XLA Modules:
  0.0 2476.0 jit_solution(1910775020587805539)
XLA Ops:
  12.1 40.8 %all-reduce.15 = (bf16[2048]{0:T(1024)(128)(2,1)S(1)}, bf16[128]{0:T(256)(128)(2,1)S(1)}, bf16[128]{0:T(256)(128)(2,1)S(1)}, bf16[2048]{0:T(1024)(128)(2,1)S(1)}) all-reduce(bf16[2048]{0:T(1024)(128)(2,1)S(1)} %dynamic-update-slice, bf16[128]{0:T(256)(128)(2,1)S(1)} %dynamic-update-slice.1, ...), channel_id=1, replica_groups=mesh['ctx'=8,'ws'=4] {'ctx','ws'}, use_global_device_ids=true, to_apply=%add.6 | all-reduce | flops 4352 | bytes 17408
  54.7 12.9 all-gather.12.cloned.1.call-done
  75.8 49.9 %all-gather.8.cloned.1.call-done = bf16[2048,512]{1,0:T(8,128)(2,1)} async-done(((bf16[64,512]{1,0:T(8,128)(2,1)}), bf16[2048,512]{1,0:T(8,128)(2,1)}) %all-gather.8.cloned.1.call-update) | async-done | bytes 2097168 | tf_op jit(solution)/shard_map/all_gather | solution.py:167
  148.9 18.6 all-gather.14.cloned.1.call-done
  171.9 37.0 %all-gather.10.cloned.1.call-done = bf16[1024,512]{1,0:T(8,128)(2,1)} async-done(((bf16[128,512]{1,0:T(8,128)(2,1)}), bf16[1024,512]{1,0:T(8,128)(2,1)}) %all-gather.10.cloned.1.call-update) | async-done | bytes 1048592 | tf_op jit(solution)/shard_map/all_gather | solution.py:210
  211.1 114.1 %all-gather.16.cloned.1.call-done = bf16[2048,4096]{1,0:T(8,128)(2,1)} async-done(((bf16[64,4096]{1,0:T(8,128)(2,1)}), bf16[2048,4096]{1,0:T(8,128)(2,1)}) %all-gather.16.cloned.1.call-update) | async-done | bytes 16777232 | tf_op jit(solution)/shard_map/all_gather | solution.py:165
  325.2 22.7 copy.97
  367.0 21.6 while.39
  388.7 20.8 while.40
  412.3 28.7 %all-gather.18.cloned.1.call-done = bf16[4096,2048]{1,0:T(8,128)(2,1)} async-done(((bf16[128,2048]{1,0:T(8,128)(2,1)}), bf16[4096,2048]{1,0:T(8,128)(2,1)}) %all-gather.18.cloned.1.call-update) | async-done | bytes 16777232 | tf_op jit(solution)/shard_map/all_gather | solution.py:170
  452.4 13.8 gather_fusion
  471.2 163.5 %all-gather = bf16[32,64,32]{1,2,0:T(8,128)(2,1)S(1)} all-gather(bf16[1,64,32]{1,2,0:T(8,128)(2,1)S(1)} %bitcast.403), channel_id=1, replica_groups=mesh['ctx'=8,'ws'=4] {'ctx','ws'}, dimensions={0}, use_global_device_ids=true | all-gather | bytes 135168 | tf_op jit(solution)/shard_map/all_gather | solution.py:172
  645.8 15.4 gather_fusion.2
  684.5 117.4 %all-to-all-done.2 = bf16[32,48,2048]{2,1,0:T(8,128)(2,1)} async-done(((bf16[32,48,2048]{2,1,0:T(8,128)(2,1)}), bf16[32,48,2048]{2,1,0:T(8,128)(2,1)}, u32[]{:S(2)}, u32[]{:S(2)}) %all-to-all-start.2) | async-done | bytes 6291488 | tf_op jit(solution)/shard_map/all_to_all | solution.py:83
  801.8 12.3 multiply_convert_fusion
  849.5 127.1 %all-to-all-done.3 = bf16[32,48,2048]{2,1,0:T(8,128)(2,1)} async-done(((bf16[32,48,2048]{2,1,0:T(8,128)(2,1)}), bf16[32,48,2048]{2,1,0:T(8,128)(2,1)}, u32[]{:S(2)}, u32[]{:S(2)}) %all-to-all-start.3) | async-done | bytes 6291488 | tf_op jit(solution)/shard_map/all_to_all | solution.py:88
  984.5 12.4 gather_fusion.3
  1001.9 118.4 %all-to-all-done.1 = bf16[32,48,2048]{2,1,0:T(8,128)(2,1)} async-done(((bf16[32,48,2048]{2,1,0:T(8,128)(2,1)}), bf16[32,48,2048]{2,1,0:T(8,128)(2,1)}, u32[]{:S(2)}, u32[]{:S(2)}) %all-to-all-start.1) | async-done | bytes 6291488 | tf_op jit(solution)/shard_map/all_to_all | solution.py:78
  1120.3 12.5 gather_fusion.1
  1141.3 11.8 fusion.63
  1157.8 40.9 %while.41 = (s32[]{:T(128)}, f32[128,4,8,128]{0,3,2,1:T(8,128)}, f32[2,512,4,128]{3,1,2,0:T(8,128)}, bf16[2,512,4,128]{3,1,2,0:T(8,128)(2,1)}, bf16[2,512,4,128]...) while((s32[]{:T(128)}, f32[128,4,8,128]{0,3,2,1:T(8,128)}, ...), condition=%wide.region_25.26_spmd.clone, body=%wide.region_24.25_spmd.clone.sunk | while | flops 2702376960 | bytes 147518832 | solution.py:398
  1207.4 60.6 %reduce-scatter.10.cloned.1.call-done = bf16[128,512]{1,0:T(8,128)(2,1)} async-done(((bf16[1024,512]{1,0:T(8,128)(2,1)}), bf16[128,512]{1,0:T(8,128)(2,1)}) %reduce-scatter.10.cloned.1.call-update) | async-done | bytes 131088 | tf_op jit(solution)/shard_map/reduce_scatter | solution.py:410
  1272.4 62.6 %reduce-scatter.12.cloned.1.call-done = bf16[128,512]{1,0:T(8,128)(2,1)} async-done(((bf16[1024,512]{1,0:T(8,128)(2,1)}), bf16[128,512]{1,0:T(8,128)(2,1)}) %reduce-scatter.12.cloned.1.call-update) | async-done | bytes 131088 | tf_op jit(solution)/shard_map/reduce_scatter | solution.py:413
  1342.0 13.4 fusion.86
  1356.9 13.5 fusion.91
  1402.3 12.5 fusion.135
  1414.8 37.7 %reduce-scatter.22.cloned.1.call-done = f32[64,32]{1,0:T(8,128)} async-done(((f32[2048,32]{1,0:T(8,128)}), f32[64,32]{1,0:T(8,128)}) %reduce-scatter.22.cloned.1.call-update) | async-done | bytes 8208
  1460.4 57.7 %all-reduce.14 = (f32[2048]{0:T(1024)S(1)}, f32[128]{0:T(128)S(1)}, f32[128]{0:T(128)S(1)}, f32[2048]{0:T(1024)S(1)}) all-reduce(f32[2048]{0:T(1024)S(1)} %get-tuple-element.455, f32[128]{0:T(128)S(1)} %get-tuple-element.449, f32[128]{0:T(128)S(1)} %get-tuple-element.457, ...), channel_id=4, replica_groups=mesh['ctx'=8,'ws'=4] {'ctx','ws'}, use_global_device_ids=true, to_apply=%region_32.33.clone | all-reduce | flops 4352 | bytes 34816
  1523.4 68.3 %reduce-scatter.16.cloned.1.call-done = f32[64,512]{1,0:T(8,128)} async-done(((f32[2048,512]{1,0:T(8,128)}), f32[64,512]{1,0:T(8,128)}) %reduce-scatter.16.cloned.1.call-update) | async-done | bytes 131088 | tf_op jit(solution)/shard_map/reduce_scatter | solution.py:464
  1591.7 140.3 %reduce-scatter.18.cloned.1.call-done = f32[64,512]{1,0:T(8,128)} async-done(((f32[2048,512]{1,0:T(8,128)}), f32[64,512]{1,0:T(8,128)}) %reduce-scatter.18.cloned.1.call-update) | async-done | bytes 131088 | tf_op jit(solution)/shard_map/reduce_scatter | solution.py:465
  1732.0 372.0 %reduce-scatter.14.cloned.1.call-done = f32[64,4096]{1,0:T(8,128)} async-done(((f32[2048,4096]{1,0:T(8,128)}), f32[64,4096]{1,0:T(8,128)}) %reduce-scatter.14.cloned.1.call-update) | async-done | bytes 1048592 | tf_op jit(solution)/shard_map/reduce_scatter | solution.py:463
  2104.0 365.0 %reduce-scatter.20.cloned.1.call-done = f32[128,2048]{1,0:T(8,128)} async-done(((f32[4096,2048]{1,0:T(8,128)}), f32[128,2048]{1,0:T(8,128)}) %reduce-scatter.20.cloned.1.call-update) | async-done | bytes 1048592 | tf_op jit(solution)/shard_map/reduce_scatter | solution.py:468
  (371 shorter events, 326.9 us)
Async XLA Ops:
  7.2 794.7 %copy-start = (bf16[1,768,2048]{2,1,0:T(8,128)(2,1)S(1)}, bf16[1,768,2048]{2,1,0:T(8,128)(2,1)}, u32[]{:S(2)}) copy-start(bf16[1,768,2048]{2,1,0:T(8,128)(2,1)} %param.37) | copy-start | bytes 9437188
  7.2 60.4 %all-gather.12.cloned.1.call-start = ((), (), s32[]{:S(2)}) async-start(), calls=%async_computation.13 | async-start | bytes 2162688 | tf_op jit(solution)/shard_map/all_gather | solution.py:166
  7.9 117.8 %all-gather.8.cloned.1.call-start = ((), (), s32[]{:S(2)}) async-start(), calls=%async_computation.11 | async-start | bytes 2162688 | tf_op jit(solution)/shard_map/all_gather | solution.py:167
  8.7 158.8 %all-gather.14.cloned.1.call-start = ((), (), s32[]{:S(2)}) async-start(), calls=%async_computation.14 | async-start | bytes 1179648 | tf_op jit(solution)/shard_map/all_gather | solution.py:209
  52.9 294.9 %copy-start.32 = (f32[2048]{0:T(1024)}, f32[2048]{0:T(1024)S(1)}, u32[]{:S(2)}) copy-start(f32[2048]{0:T(1024)S(1)} %convert_element_type.178) | copy-start | bytes 24580
  54.4 293.4 %copy-start.55 = (f32[128]{0:T(128)}, f32[128]{0:T(128)S(1)}, u32[]{:S(2)}) copy-start(f32[128]{0:T(128)S(1)} %fusion.127) | copy-start | bytes 1540
  54.6 303.2 %copy-start.28 = (f32[128,64]{0,1:T(8,128)}, f32[128,64]{0,1:T(8,128)S(1)}, u32[]{:S(2)}) copy-start(f32[128,64]{0,1:T(8,128)S(1)} %get-tuple-element.564) | copy-start | bytes 98308
  54.7 303.2 %copy-start.30 = (f32[128,64]{0,1:T(8,128)}, f32[128,64]{0,1:T(8,128)S(1)}, u32[]{:S(2)}) copy-start(f32[128,64]{0,1:T(8,128)S(1)} %get-tuple-element.565) | copy-start | bytes 98308
  75.8 133.2 %all-gather.10.cloned.1.call-start = ((), (), s32[]{:S(2)}) async-start(), calls=%async_computation.12 | async-start | bytes 1179648 | tf_op jit(solution)/shard_map/all_gather | solution.py:210
  128.7 196.5 %all-gather.16.cloned.1.call-start = ((), (), s32[]{:S(2)}) async-start(), calls=%async_computation.15 | async-start | bytes 17301504 | tf_op jit(solution)/shard_map/all_gather | solution.py:165
  129.2 311.7 %all-gather.18.cloned.1.call-start = ((), (), s32[]{:S(2)}) async-start(), calls=%async_computation.16 | async-start | bytes 17301504 | tf_op jit(solution)/shard_map/all_gather | solution.py:170
  466.2 195.0 %all-to-all-start = ((bf16[32,48,2048]{2,1,0:T(8,128)(2,1)}), bf16[32,48,2048]{2,1,0:T(8,128)(2,1)}, u32[]{:S(2)}, u32[]{:S(2)}) async-start(bf16[32,48,2048]{2,1,0:T(8,128)(2,1)} %bitcast.358), calls=%async_computation | async-start | bytes 12582912 | tf_op jit(solution)/shard_map/all_to_all | solution.py:73
  661.2 140.6 %all-to-all-start.2 = ((bf16[32,48,2048]{2,1,0:T(8,128)(2,1)}), bf16[32,48,2048]{2,1,0:T(8,128)(2,1)}, u32[]{:S(2)}, u32[]{:S(2)}) async-start(bf16[32,48,2048]{2,1,0:T(8,128)(2,1)} %bitcast.359), calls=%async_computation.2 | async-start | bytes 12582912 | tf_op jit(solution)/shard_map/all_to_all | solution.py:83
  832.3 144.3 %all-to-all-start.3 = ((bf16[32,48,2048]{2,1,0:T(8,128)(2,1)}), bf16[32,48,2048]{2,1,0:T(8,128)(2,1)}, u32[]{:S(2)}, u32[]{:S(2)}) async-start(bf16[32,48,2048]{2,1,0:T(8,128)(2,1)} %bitcast.369), calls=%async_computation.3 | async-start | bytes 12582912 | tf_op jit(solution)/shard_map/all_to_all | solution.py:88
  976.6 143.8 %all-to-all-start.1 = ((bf16[32,48,2048]{2,1,0:T(8,128)(2,1)}), bf16[32,48,2048]{2,1,0:T(8,128)(2,1)}, u32[]{:S(2)}, u32[]{:S(2)}) async-start(bf16[32,48,2048]{2,1,0:T(8,128)(2,1)} %bitcast.368), calls=%async_computation.1 | async-start | bytes 12582912 | tf_op jit(solution)/shard_map/all_to_all | solution.py:78
  984.4 283.7 %reduce-scatter.10.cloned.1.call-start = ((), (), s32[]{:S(2)}) async-start(), calls=%async_computation.17 | async-start | bytes 1179648 | tf_op jit(solution)/shard_map/reduce_scatter | solution.py:410
  1202.6 66.5 %copy-start.29 = (f32[128,64]{0,1:T(8,128)S(1)}, f32[128,64]{0,1:T(8,128)}, u32[]{:S(2)}) copy-start(f32[128,64]{0,1:T(8,128)} %copy-done.28) | copy-start | bytes 98308
  1202.6 66.5 %copy-start.31 = (f32[128,64]{0,1:T(8,128)S(1)}, f32[128,64]{0,1:T(8,128)}, u32[]{:S(2)}) copy-start(f32[128,64]{0,1:T(8,128)} %copy-done.30) | copy-start | bytes 98308
  1202.6 132.4 %reduce-scatter.12.cloned.1.call-start = ((), (), s32[]{:S(2)}) async-start(), calls=%async_computation.18 | async-start | bytes 1179648 | tf_op jit(solution)/shard_map/reduce_scatter | solution.py:413
  1202.6 66.5 %copy-start.22 = (f32[128,4,128]{0,2,1:T(8,128)S(1)}, f32[128,4,128]{0,2,1:T(8,128)}, u32[]{:S(2)}) copy-start(f32[128,4,128]{0,2,1:T(8,128)} %copy-done.21) | copy-start | bytes 786436
  1202.6 66.5 %copy-start.53 = (f32[128,4]{0,1:T(4,128)S(1)}, f32[128,4]{0,1:T(4,128)}, u32[]{:S(2)}) copy-start(f32[128,4]{0,1:T(4,128)} %copy-done.52) | copy-start | bytes 6148
  1202.7 66.5 %copy-start.64 = (f32[128]{0:T(128)S(1)}, f32[128]{0:T(128)}, u32[]{:S(2)}) copy-start(f32[128]{0:T(128)} %copy-done.63) | copy-start | bytes 1540
  1204.7 64.7 %copy-start.10 = (bf16[1,128,2048]{2,1,0:T(8,128)(2,1)S(1)}, bf16[1,128,2048]{2,1,0:T(8,128)(2,1)}, u32[]{:S(2)}) copy-start(bf16[1,128,2048]{2,1,0:T(8,128)(2,1)} %param.22) | copy-start | bytes 1572868
  1204.8 64.7 %copy-start.33 = (f32[2048]{0:T(1024)S(1)}, f32[2048]{0:T(1024)}, u32[]{:S(2)}) copy-start(f32[2048]{0:T(1024)} %copy-done.32) | copy-start | bytes 24580
  1206.0 246.6 %reduce-scatter.22.cloned.1.call-start = ((), (), s32[]{:S(2)}) async-start(), calls=%async_computation.23 | async-start | bytes 1081344
  1207.4 384.3 %reduce-scatter.16.cloned.1.call-start = ((), (), s32[]{:S(2)}) async-start(), calls=%async_computation.20 | async-start | bytes 4325376 | tf_op jit(solution)/shard_map/reduce_scatter | solution.py:464
  1272.3 66.4 %copy-start.6 = (f32[128,4,8,128]{0,3,2,1:T(8,128)S(1)}, f32[128,4,8,128]{0,3,2,1:T(8,128)}, u32[]{:S(2)}) copy-start(f32[128,4,8,128]{0,3,2,1:T(8,128)} %get-tuple-element.201) | copy-start | bytes 6291460
  1272.3 459.7 %reduce-scatter.18.cloned.1.call-start = ((), (), s32[]{:S(2)}) async-start(), calls=%async_computation.21 | async-start | bytes 4325376 | tf_op jit(solution)/shard_map/reduce_scatter | solution.py:465
  1338.7 765.4 %reduce-scatter.14.cloned.1.call-start = ((), (), s32[]{:S(2)}) async-start(), calls=%async_computation.19 | async-start | bytes 34603008 | tf_op jit(solution)/shard_map/reduce_scatter | solution.py:463
  1355.4 1113.6 %reduce-scatter.20.cloned.1.call-start = ((), (), s32[]{:S(2)}) async-start(), calls=%async_computation.22 | async-start | bytes 34603008 | tf_op jit(solution)/shard_map/reduce_scatter | solution.py:468
  1454.0 66.5 %copy-start.68 = (f32[128]{0:T(128)S(1)}, f32[128]{0:T(128)}, u32[]{:S(2)}) copy-start(f32[128]{0:T(128)} %copy-done.67) | copy-start | bytes 1540
  1454.0 1015.0 %copy-start.1 = (bf16[1,768,2048]{2,1,0:T(8,128)(2,1)S(1)}, bf16[1,768,2048]{2,1,0:T(8,128)(2,1)}, u32[]{:S(2)}) copy-start(bf16[1,768,2048]{2,1,0:T(8,128)(2,1)} %param.37) | copy-start | bytes 9437188
  (69 other events, 957.3 us)
Sparse Core Ops, SparseCore 0:
  10.9 56.6 all-gather.11
  70.4 55.2 all-gather.7
  128.4 38.9 all-gather.13
  170.0 38.8 all-gather.9
  211.6 113.4 all-gather.15
  327.9 113.0 all-gather.17
  1202.7 65.3 reduce-scatter.9
  1272.4 62.4 reduce-scatter.11
  1337.2 115.2 reduce-scatter.21
  1455.3 136.3 reduce-scatter.15
  1594.6 137.3 reduce-scatter.17
  1734.8 369.1 reduce-scatter.13
  2107.0 361.9 reduce-scatter.19
where the time goes:
time: 2490 us; the launch traced here: 2480 us
  waiting for transfers between devices  1730 us (69%)
  blocking collectives  262 us (11%)
  matrix products  233 us (9%)
  local copies, waits for them, and re-layouts  147 us (6%)
  other arithmetic  57.6 us (2%)
  starting transfers between devices  26.9 us (1%)
    reduce_scatter x1, waiting for transfers between devices, body(): lax.psum_scatter(grad_query_weight, ('ctx', 'ws'), scatter_dimension=0, t...  372 us
    reduce_scatter x1, waiting for transfers between devices, body(): lax.psum_scatter(grad_out_weight, ('ctx', 'ws'), scatter_dimension=0, til...  365 us
    all_gather x1, blocking collectives, body(): lax.all_gather(shards[8], ('ctx', 'ws'), axis=0, tiled=True)  164 us
    reduce_scatter x1, waiting for transfers between devices, body(): lax.psum_scatter(grad_value_weight, ('ctx', 'ws'), scatter_dimension=0, t...  140 us
    all_to_all x1, waiting for transfers between devices, send_in_grads(): lax.all_to_all(flat_rows, ('ctx', 'ws'), split_axis=0, concat_axis=0, til...  127 us
    all_to_all x1, waiting for transfers between devices, send_outputs(): lax.all_to_all(flat_rows, ('ctx', 'ws'), split_axis=0, concat_axis=0, til...  118 us
    all_to_all x1, waiting for transfers between devices, send_out_grads(): lax.all_to_all(flat_rows, ('ctx', 'ws'), split_axis=0, concat_axis=0, til...  117 us
    all_gather x1, waiting for transfers between devices, body(): lax.all_gather(shards[1], ('ctx', 'ws'), axis=0, tiled=True)  114 us
  transfers between devices with their start and end apart: 17, of which 16 were waited for; matrix products, arithmetic and copies ran while one was open for 12% of the time, Pallas kernels for 0%

commit v1 on v0

--- a/solution.py
+++ b/solution.py
@@ -1,6 +1,8 @@
 import jax
 import jax.numpy as jnp
 from jax import lax
+from jax.experimental import pallas as pl
+from jax.experimental.pallas import tpu as pltpu
 from jax.sharding import PartitionSpec as P
 
 QUERY_HEADS = 32
@@ -107,7 +109,7 @@
     return shaped.transpose(1, 0, 2, 3).reshape(device_count, expert_local * capacity, model_width)
 
 
-def body(
+def general_body(
     inputs,
     grad_output,
     routes,
@@ -487,6 +489,655 @@
     )
 
 
+VMEM_WHOLE = pl.BlockSpec(memory_space=pltpu.VMEM)
+VMEM_BYTES = 60 * 2**20
+EXTRA = 128
+
+
+def compiler_params():
+    return pltpu.CompilerParams(vmem_limit_bytes=VMEM_BYTES)
+
+
+def dot_rows(left, right):
+    return lax.dot_general(
+        left, right, (((1,), (0,)), ((), ())), preferred_element_type=SINGLE_FLOAT
+    )
+
+
+def dot_right_transposed(left, right):
+    return lax.dot_general(
+        left, right, (((1,), (1,)), ((), ())), preferred_element_type=SINGLE_FLOAT
+    )
+
+
+def dot_left_transposed(left, right):
+    return lax.dot_general(
+        left, right, (((0,), (0,)), ((), ())), preferred_element_type=SINGLE_FLOAT
+    )
+
+
+def key_range(tile, tile_rows, sequence_tokens, slack):
+    half = sequence_tokens // 2
+    first_row = tile * tile_rows
+    low = 0 if first_row < half + slack else half
+    return low, first_row + tile_rows
+
+
+def stacked_heads(ref, rows, heads):
+    return jnp.concatenate(
+        [ref[rows, h * HEAD_DIM : (h + 1) * HEAD_DIM] for h in range(heads)], axis=0
+    )
+
+
+def tile_scores(q4, k_ref, segc_ref, segr_ref, low, high, first_row, tile_rows, heads):
+    scale = HEAD_DIM ** (-0.5)
+    scores = dot_right_transposed(q4, k_ref[low:high, :]) * scale
+    span = high - low
+    query_place = first_row + lax.broadcasted_iota(jnp.int32, (tile_rows, span), 0)
+    key_place = low + lax.broadcasted_iota(jnp.int32, (tile_rows, span), 1)
+    allowed = (segc_ref[first_row : first_row + tile_rows, :] == segr_ref[:, low:high]) & (
+        key_place <= query_place
+    )
+    fill = jnp.where(allowed, 0.0, MASK_FILL)
+    scores = scores + jnp.concatenate([fill] * heads, axis=0)
+    exponent = jnp.exp(scores - jnp.max(scores, axis=-1, keepdims=True))
+    return exponent * (1.0 / jnp.sum(exponent, axis=-1, keepdims=True))
+
+
+def attention_forward_kernel(
+    slack,
+    x_ref,
+    gain_ref,
+    w_ref,
+    qg_ref,
+    kg_ref,
+    cos_ref,
+    sin_ref,
+    segc_ref,
+    segr_ref,
+    wo_ref,
+    normed_ref,
+    raw_ref,
+    q_ref,
+    k_ref,
+    v_ref,
+    attn_ref,
+    part_ref,
+):
+    tokens = x_ref.shape[0]
+    heads = q_ref.shape[1] // HEAD_DIM
+    rows_step = 256
+
+    def project(i, carry):
+        rows = pl.ds(pl.multiple_of(i * rows_step, rows_step), rows_step)
+        x = x_ref[rows, :].astype(SINGLE_FLOAT)
+        inverse = lax.rsqrt(jnp.mean(x * x, axis=-1, keepdims=True) + EPS)
+        normed = (x * inverse * gain_ref[...]).astype(BRAIN_FLOAT_TYPE)
+        normed_ref[rows, :] = normed
+        raw = dot_rows(normed, w_ref[...])
+        raw_ref[rows, :] = raw[:, : (heads + 1) * HEAD_DIM]
+        v_ref[rows, :] = raw[:, (heads + 1) * HEAD_DIM :].astype(BRAIN_FLOAT_TYPE)
+        cosine, sine = cos_ref[rows, :], sin_ref[rows, :]
+        for h in range(heads + 1):
+            part = raw[:, h * HEAD_DIM : (h + 1) * HEAD_DIM]
+            gain = qg_ref[...] if h < heads else kg_ref[...]
+            scaled = (
+                part * lax.rsqrt(jnp.mean(part * part, axis=-1, keepdims=True) + EPS) * gain
+            )
+            turned = scaled * cosine + pltpu.roll(scaled, HEAD_DIM // 2, 1) * sine
+            turned = turned.astype(BRAIN_FLOAT_TYPE)
+            if h < heads:
+                q_ref[rows, h * HEAD_DIM : (h + 1) * HEAD_DIM] = turned
+            else:
+                k_ref[rows, :] = turned
+        return carry
+
+    lax.fori_loop(0, tokens // rows_step, project, 0)
+    tile_rows = 128
+    for tile in range(tokens // tile_rows):
+        first_row = tile * tile_rows
+        rows = slice(first_row, first_row + tile_rows)
+        low, high = key_range(tile, tile_rows, tokens, slack)
+        probs = tile_scores(
+            stacked_heads(q_ref, rows, heads),
+            k_ref,
+            segc_ref,
+            segr_ref,
+            low,
+            high,
+            first_row,
+            tile_rows,
+            heads,
+        )
+        attended = dot_rows(probs.astype(BRAIN_FLOAT_TYPE), v_ref[low:high, :])
+        for h in range(heads):
+            attn_ref[rows, h * HEAD_DIM : (h + 1) * HEAD_DIM] = attended[
+                h * tile_rows : (h + 1) * tile_rows
+            ].astype(BRAIN_FLOAT_TYPE)
+
+    def project_out(i, carry):
+        rows = pl.ds(pl.multiple_of(i * rows_step, rows_step), rows_step)
+        part_ref[rows, :] = dot_rows(attn_ref[rows, :], wo_ref[...]).astype(BRAIN_FLOAT_TYPE)
+        return carry
+
+    lax.fori_loop(0, tokens // rows_step, project_out, 0)
+
+
+def attention_forward(slack, x, gain, w, qg, kg, cosine, sine, segc, segr, wo):
+    tokens, width = x.shape
+    channels = w.shape[1] - 2 * HEAD_DIM
+    low = BRAIN_FLOAT_TYPE
+    shapes = (
+        jax.ShapeDtypeStruct((tokens, width), low),
+        jax.ShapeDtypeStruct((tokens, channels + HEAD_DIM), SINGLE_FLOAT),
+        jax.ShapeDtypeStruct((tokens, channels), low),
+        jax.ShapeDtypeStruct((tokens, HEAD_DIM), low),
+        jax.ShapeDtypeStruct((tokens, HEAD_DIM), low),
+        jax.ShapeDtypeStruct((tokens, channels), low),
+        jax.ShapeDtypeStruct((tokens, width), low),
+    )
+
+    def kernel(*refs):
+        attention_forward_kernel(slack, *refs)
+
+    return pl.pallas_call(
+        kernel,
+        out_shape=shapes,
+        in_specs=[VMEM_WHOLE] * 10,
+        out_specs=[VMEM_WHOLE] * 7,
+        compiler_params=compiler_params(),
+        name="attention_forward",
+    )(x, gain, w, qg, kg, cosine, sine, segc, segr, wo)
+
+
+def head_backward(turned_gradient, part, gain, cosine, sine):
+    scaled_gradient = turned_gradient * cosine - (
+        pltpu.roll(turned_gradient, HEAD_DIM // 2, 1) * sine
+    )
+    inverse = lax.rsqrt(jnp.mean(part * part, axis=-1, keepdims=True) + EPS)
+    unit = part * inverse
+    gain_gradient = jnp.sum(scaled_gradient * unit, axis=0, keepdims=True)
+    unit_gradient = scaled_gradient * gain
+    raw_gradient = inverse * (
+        unit_gradient - unit * jnp.mean(unit * unit_gradient, axis=-1, keepdims=True)
+    )
+    return raw_gradient, gain_gradient
+
+
+def attention_backward_kernel(
+    slack,
+    dh_ref,
+    wo_ref,
+    attn_ref,
+    q_ref,
+    k_ref,
+    v_ref,
+    raw_ref,
+    normed_ref,
+    x_ref,
+    w_ref,
+    qg_ref,
+    kg_ref,
+    cos_ref,
+    sin_ref,
+    segc_ref,
+    segr_ref,
+    gwo_ref,
+    gw_ref,
+    dpart_ref,
+    ggain_ref,
+    gheads_ref,
+    da_ref,
+    draw_ref,
+    dk_ref,
+    dv_ref,
+):
+    tokens = x_ref.shape[0]
+    heads = q_ref.shape[1] // HEAD_DIM
+    scale = HEAD_DIM ** (-0.5)
+    rows_step = 256
+
+    def attended_gradient(i, carry):
+        rows = pl.ds(pl.multiple_of(i * rows_step, rows_step), rows_step)
+        da_ref[rows, :] = dot_right_transposed(dh_ref[rows, :], wo_ref[...]).astype(
+            BRAIN_FLOAT_TYPE
+        )
+        return carry
+
+    lax.fori_loop(0, tokens // rows_step, attended_gradient, 0)
+
+    def out_weight(i, carry):
+        columns = pl.ds(pl.multiple_of(i * 512, 512), 512)
+        gwo_ref[:, columns] = dot_left_transposed(attn_ref[...], dh_ref[:, columns]).astype(
+            gwo_ref.dtype
+        )
+        return carry
+
+    lax.fori_loop(0, dh_ref.shape[1] // 512, out_weight, 0)
+    dk_ref[...] = jnp.zeros_like(dk_ref)
+    dv_ref[...] = jnp.zeros_like(dv_ref)
+    query_gain_gradient = jnp.zeros((1, HEAD_DIM), SINGLE_FLOAT)
+    tile_rows = 128
+    for tile in range(tokens // tile_rows):
+        first_row = tile * tile_rows
+        rows = slice(first_row, first_row + tile_rows)
+        low, high = key_range(tile, tile_rows, tokens, slack)
+        q4 = stacked_heads(q_ref, rows, heads)
+        da4 = stacked_heads(da_ref, rows, heads)
+        probs = tile_scores(
+            q4, k_ref, segc_ref, segr_ref, low, high, first_row, tile_rows, heads
+        )
+        d_probs = dot_right_transposed(da4, v_ref[low:high, :])
+        delta = jnp.sum(probs * d_probs, axis=-1, keepdims=True)
+        d_scores = (probs * (d_probs - delta)).astype(BRAIN_FLOAT_TYPE)
+        dq4 = dot_rows(d_scores, k_ref[low:high, :]) * scale
+        dk_ref[low:high, :] += dot_left_transposed(d_scores, q4)
+        dv_ref[low:high, :] += dot_left_transposed(probs.astype(BRAIN_FLOAT_TYPE), da4)
+        for h in range(heads):
+            columns = slice(h * HEAD_DIM, (h + 1) * HEAD_DIM)
+            raw_gradient, gain_gradient = head_backward(
+                dq4[h * tile_rows : (h + 1) * tile_rows],
+                raw_ref[rows, columns],
+                qg_ref[...],
+                cos_ref[rows, :],
+                sin_ref[rows, :],
+            )
+            draw_ref[rows, columns] = raw_gradient.astype(BRAIN_FLOAT_TYPE)
+            query_gain_gradient = query_gain_gradient + gain_gradient
+    key_columns = slice(heads * HEAD_DIM, (heads + 1) * HEAD_DIM)
+    raw_gradient, key_gain_gradient = head_backward(
+        dk_ref[...] * scale, raw_ref[:, key_columns], kg_ref[...], cos_ref[...], sin_ref[...]
+    )
+    draw_ref[:, key_columns] = raw_gradient.astype(BRAIN_FLOAT_TYPE)
+    draw_ref[:, (heads + 1) * HEAD_DIM :] = dv_ref[...].astype(BRAIN_FLOAT_TYPE)
+    gheads_ref[...] = jnp.concatenate(
+        [query_gain_gradient, key_gain_gradient, jnp.zeros((6, HEAD_DIM), SINGLE_FLOAT)], axis=0
+    )
+
+    def projection_weight(i, carry):
+        columns = pl.ds(pl.multiple_of(i * 256, 256), 256)
+        gw_ref[columns, :] = dot_left_transposed(normed_ref[:, columns], draw_ref[...]).astype(
+            gw_ref.dtype
+        )
+        return carry
+
+    lax.fori_loop(0, normed_ref.shape[1] // 256, projection_weight, 0)
+    ggain_ref[...] = jnp.zeros_like(ggain_ref)
+
+    def input_gradient(i, carry):
+        rows = pl.ds(pl.multiple_of(i * rows_step, rows_step), rows_step)
+        d_normed = dot_right_transposed(draw_ref[rows, :], w_ref[...])
+        dpart_ref[rows, :] = d_normed.astype(BRAIN_FLOAT_TYPE)
+        x = x_ref[rows, :].astype(SINGLE_FLOAT)
+        inverse = lax.rsqrt(jnp.mean(x * x, axis=-1, keepdims=True) + EPS)
+        ggain_ref[...] += jnp.sum(d_normed * (x * inverse), axis=0, keepdims=True)
+        return carry
+
+    lax.fori_loop(0, tokens // rows_step, input_gradient, 0)
+
+
+def attention_backward(
+    slack, dh, wo, attn, q, k, v, raw, normed, x, w, qg, kg, cosine, sine, segc, segr
+):
+    tokens, width = x.shape
+    channels = q.shape[1]
+    low = BRAIN_FLOAT_TYPE
+    shapes = (
+        jax.ShapeDtypeStruct((channels, width), low),
+        jax.ShapeDtypeStruct((width, channels + 2 * HEAD_DIM), low),
+        jax.ShapeDtypeStruct((tokens, width), low),
+        jax.ShapeDtypeStruct((1, width), SINGLE_FLOAT),
+        jax.ShapeDtypeStruct((8, HEAD_DIM), SINGLE_FLOAT),
+    )
+
+    def kernel(*refs):
+        attention_backward_kernel(slack, *refs)
+
+    return pl.pallas_call(
+        kernel,
+        out_shape=shapes,
+        in_specs=[VMEM_WHOLE] * 16,
+        out_specs=[VMEM_WHOLE] * 5,
+        scratch_shapes=[
+            pltpu.VMEM((tokens, channels), low),
+            pltpu.VMEM((tokens, channels + 2 * HEAD_DIM), low),
+            pltpu.VMEM((tokens, HEAD_DIM), SINGLE_FLOAT),
+            pltpu.VMEM((tokens, HEAD_DIM), SINGLE_FLOAT),
+        ],
+        compiler_params=compiler_params(),
+        name="attention_backward",
+    )(dh, wo, attn, q, k, v, raw, normed, x, w, qg, kg, cosine, sine, segc, segr)
+
+
+def expert_kernel(
+    capacity,
+    expert_ref,
+    pay_ref,
+    dout_ref,
+    wg_ref,
+    wu_ref,
+    wd_ref,
+    outp_ref,
+    dp_ref,
+    x_ref,
+    deo_ref,
+    hid_ref,
+    dgl_ref,
+    dul_ref,
+    d_ref,
+    g_ref,
+    st_ref,
+):
+    sources, tokens, payload = pay_ref.shape
+    width = wg_ref.shape[0]
+    experts = (payload - width) // 4
+    e = expert_ref[0]
+    lane = lax.broadcasted_iota(jnp.int32, (tokens, payload - width), 1)
+    slot_lane = lax.broadcasted_iota(jnp.int32, (tokens, capacity), 1).astype(SINGLE_FLOAT)
+    row_lane = lax.broadcasted_iota(jnp.int32, (capacity, payload - width), 1)
+    is_gate = (row_lane == e) | (row_lane == experts + e)
+    for s in range(sources):
+        rows = slice(s * capacity, (s + 1) * capacity)
+        table = pay_ref[s, :, width:].astype(SINGLE_FLOAT)
+        rank = jnp.sum(jnp.where(lane == 2 * experts + e, table, 0.0), axis=-1, keepdims=True)
+        pick = (rank == slot_lane).astype(BRAIN_FLOAT_TYPE)
+        st_ref[s] = pick
+        chosen = dot_left_transposed(pick, pay_ref[s])
+        x_ref[rows, :] = chosen[:, :width].astype(BRAIN_FLOAT_TYPE)
+        gate = jnp.sum(jnp.where(is_gate, chosen[:, width:], 0.0), axis=-1, keepdims=True)
+        g_ref[rows, :] = gate
+        d_rows = dot_left_transposed(pick, dout_ref[s])
+        d_ref[rows, :] = d_rows.astype(BRAIN_FLOAT_TYPE)
+        deo_ref[rows, :] = (gate * d_rows).astype(BRAIN_FLOAT_TYPE)
+    x = x_ref[...]
+    gate_hidden = dot_rows(x, wg_ref[...])
+    up_hidden = dot_rows(x, wu_ref[...])
+    sigmoid = 1.0 / (1.0 + jnp.exp(-gate_hidden))
+    silu = gate_hidden * sigmoid
+    hidden = (silu * up_hidden).astype(BRAIN_FLOAT_TYPE)
+    hid_ref[...] = hidden
+    d_hidden = dot_right_transposed(deo_ref[...], wd_ref[...])
+    d_gate = (d_hidden * up_hidden * sigmoid * (1.0 + gate_hidden * (1.0 - sigmoid))).astype(
+        BRAIN_FLOAT_TYPE
+    )
+    d_up = (d_hidden * silu).astype(BRAIN_FLOAT_TYPE)
+    dgl_ref[...] = d_gate
+    dul_ref[...] = d_up
+    expert_out = dot_rows(hidden, wd_ref[...]).astype(BRAIN_FLOAT_TYPE)
+    d_copy = (
+        dot_right_transposed(d_gate, wg_ref[...]) + dot_right_transposed(d_up, wu_ref[...])
+    ).astype(BRAIN_FLOAT_TYPE)
+    for s in range(sources):
+        rows = slice(s * capacity, (s + 1) * capacity)
+        pick = st_ref[s]
+        e_rows = expert_out[rows].astype(SINGLE_FLOAT)
+        gate = g_ref[rows, :]
+        d_gate_rows = jnp.sum(
+            d_ref[rows, :].astype(SINGLE_FLOAT) * e_rows, axis=-1, keepdims=True
+        )
+        high = d_gate_rows.astype(BRAIN_FLOAT_TYPE).astype(SINGLE_FLOAT)
+        extra = jnp.where(row_lane == e, high, 0.0) + jnp.where(
+            row_lane == experts + e, d_gate_rows - high, 0.0
+        )
+        outp_ref[s] = dot_rows(pick, (gate * e_rows).astype(BRAIN_FLOAT_TYPE)).astype(
+            BRAIN_FLOAT_TYPE
+        )
+        dp_ref[s, :, :width] = dot_rows(pick, d_copy[rows]).astype(BRAIN_FLOAT_TYPE)
+        dp_ref[s, :, width:] = dot_rows(pick, extra.astype(BRAIN_FLOAT_TYPE)).astype(
+            BRAIN_FLOAT_TYPE
+        )
+
+
+def expert_compute(capacity, step_sources, expert, pay, dout, wg, wu, wd):
+    sources, tokens, payload = pay.shape
+    width, ff = wg.shape
+    low = BRAIN_FLOAT_TYPE
+    rows = step_sources * capacity
+    total = sources * capacity
+    once = pl.Buffered(1)
+    grid_spec = pltpu.PrefetchScalarGridSpec(
+        num_scalar_prefetch=1,
+        grid=(sources // step_sources,),
+        in_specs=[
+            pl.BlockSpec((step_sources, tokens, payload), lambda i, e: (i, 0, 0)),
+            pl.BlockSpec((step_sources, tokens, width), lambda i, e: (i, 0, 0)),
+            pl.BlockSpec((width, ff), lambda i, e: (0, 0), pipeline_mode=once),
+            pl.BlockSpec((width, ff), lambda i, e: (0, 0), pipeline_mode=once),
+            pl.BlockSpec((ff, width), lambda i, e: (0, 0), pipeline_mode=once),
+        ],
+        out_specs=[
+            pl.BlockSpec((step_sources, tokens, width), lambda i, e: (i, 0, 0)),
+            pl.BlockSpec((step_sources, tokens, payload), lambda i, e: (i, 0, 0)),
+            pl.BlockSpec((rows, width), lambda i, e: (i, 0)),
+            pl.BlockSpec((rows, width), lambda i, e: (i, 0)),
+            pl.BlockSpec((rows, ff), lambda i, e: (i, 0)),
+            pl.BlockSpec((rows, ff), lambda i, e: (i, 0)),
+            pl.BlockSpec((rows, ff), lambda i, e: (i, 0)),
+        ],
+        scratch_shapes=[
+            pltpu.VMEM((rows, width), low),
+            pltpu.VMEM((rows, 1), SINGLE_FLOAT),
+            pltpu.VMEM((step_sources, tokens, capacity), low),
+        ],
+    )
+
+    def kernel(*refs):
+        expert_kernel(capacity, *refs)
+
+    return pl.pallas_call(
+        kernel,
+        grid_spec=grid_spec,
+        out_shape=(
+            jax.ShapeDtypeStruct((sources, tokens, width), low),
+            jax.ShapeDtypeStruct((sources, tokens, payload), low),
+            jax.ShapeDtypeStruct((total, width), low),
+            jax.ShapeDtypeStruct((total, width), low),
+            jax.ShapeDtypeStruct((total, ff), low),
+            jax.ShapeDtypeStruct((total, ff), low),
+            jax.ShapeDtypeStruct((total, ff), low),
+        ),
+        compiler_params=compiler_params(),
+        name="expert_compute",
+    )(expert, pay, dout, wg, wu, wd)
+
+
+def natural_order(blocks):
+    count, rows, width = blocks.shape
+    half = rows // 2
+    first = blocks[:, :half].reshape(count * half, width)
+    second = blocks[::-1, half:].reshape(count * half, width)
+    return jnp.concatenate([first, second], axis=0)
+
+
+def device_order(rows, count):
+    total, width = rows.shape
+    half = total // count // 2
+    first = rows[: total // 2].reshape(count, half, width)
+    second = rows[total // 2 :].reshape(count, half, width)[::-1]
+    return jnp.concatenate([first, second], axis=1)
+
+
+def norm_backward(gradient, values, gain):
+    inverse = lax.rsqrt(jnp.mean(values * values, axis=-1, keepdims=True) + EPS)
+    unit = values * inverse
+    scaled = gradient * gain
+    d_values = inverse * (scaled - unit * jnp.mean(unit * scaled, axis=-1, keepdims=True))
+    return d_values, jnp.sum(gradient * unit, axis=0)
+
+
+def tensor_body(
+    inputs,
+    grad_output,
+    routes,
+    doc_lengths,
+    norm_attn,
+    w_query,
+    key_projection,
+    value_projection,
+    query_norm,
+    key_norm,
+    w_out,
+    norm_ffn,
+    w_router,
+    expert_gate,
+    expert_up,
+    expert_down,
+):
+    ctx_count = lax.axis_size("ctx")
+    ws_count = lax.axis_size("ws")
+    device_count = ctx_count * ws_count
+    tokens = inputs.shape[1]
+    width = inputs.shape[2]
+    sequence_tokens = tokens * ctx_count
+    expert_count = w_router.shape[1]
+    capacity = tokens * TOPK * 3 // (2 * device_count)
+    heads = QUERY_HEADS // ctx_count
+    group = QUERY_HEADS // KEY_VALUE_HEADS
+    slack = tokens // 2
+    ctx_index = lax.axis_index("ctx")
+    both = ("ctx", "ws")
+    me = ctx_index * ws_count + lax.axis_index("ws")
+    slabs = []
+    for c in range(ctx_count):
+        kv = c * heads // group
+        slabs.append(
+            jnp.concatenate(
+                [
+                    w_query[:, c * heads * HEAD_DIM : (c + 1) * heads * HEAD_DIM],
+                    key_projection[:, kv * HEAD_DIM : (kv + 1) * HEAD_DIM],
+                    value_projection[:, kv * HEAD_DIM : (kv + 1) * HEAD_DIM],
+                ],
+                axis=1,
+            )
+        )
+    slabs = jnp.stack(slabs)
+    moved = lax.all_to_all(slabs, "ctx", split_axis=0, concat_axis=0)
+    w_all = lax.all_gather(moved, "ws", axis=1).reshape(width, (heads + 2) * HEAD_DIM)
+    wo_all = lax.all_gather(w_out, "ws", axis=0, tiled=True)
+    x_blocks = lax.all_gather(inputs[0], "ctx", axis=0)
+    x_all = natural_order(x_blocks)
+    attn_gain = lax.all_gather(norm_attn, both, tiled=True).astype(SINGLE_FLOAT)
+    ffn_gain = lax.all_gather(norm_ffn, both, tiled=True).astype(SINGLE_FLOAT)
+    query_gain = lax.all_gather(query_norm, both, tiled=True).astype(SINGLE_FLOAT)
+    key_gain = lax.all_gather(key_norm, both, tiled=True).astype(SINGLE_FLOAT)
+    router_matrix = lax.all_gather(w_router, both, axis=0, tiled=True)
+
+    places = jnp.arange(sequence_tokens, dtype=jnp.int32)
+    segments = segment_ids(doc_lengths[0], places)
+    half = HEAD_DIM // 2
+    frequency = THETA ** (-2.0 * jnp.arange(half, dtype=SINGLE_FLOAT) / HEAD_DIM)
+    angle = places.astype(SINGLE_FLOAT)[:, None] * frequency[None, :]
+    cosine, sine = jnp.cos(angle), jnp.sin(angle)
+    cosine = jnp.concatenate([cosine, cosine], axis=1)
+    sine = jnp.concatenate([-sine, sine], axis=1)
+    segc, segr = segments[:, None], segments[None, :]
+    qg, kg = query_gain[None, :], key_gain[None, :]
+    own_places = jnp.arange(tokens, dtype=jnp.int32)
+    own_places = jnp.where(
+        own_places < tokens // 2,
+        ctx_index * (tokens // 2) + own_places,
+        (2 * ctx_count - 2 - ctx_index) * (tokens // 2) + own_places,
+    )
+    own_segments = segment_ids(doc_lengths[0], own_places)
+    validity = own_segments < doc_lengths.shape[1]
+    d_layer = jnp.where(validity[:, None], grad_output[0], 0.0).astype(BRAIN_FLOAT_TYPE)
+    dout_all = lax.all_gather(d_layer, both, axis=0)
+
+    normed, raw, q, k, v, attn, part = attention_forward(
+        slack, x_all, attn_gain[None, :], w_all, qg, kg, cosine, sine, segc, segr, wo_all
+    )
+    branch = lax.psum_scatter(
+        device_order(part, ctx_count), "ctx", scatter_dimension=0, tiled=False
+    )
+    layer_in = inputs[0].astype(SINGLE_FLOAT)
+    hidden_state = layer_in + branch.astype(SINGLE_FLOAT)
+    mixed = rms_scale(hidden_state, ffn_gain).astype(BRAIN_FLOAT_TYPE)
+    logits = jnp.dot(mixed, router_matrix, preferred_element_type=SINGLE_FLOAT)
+    own_routes = routes[0]
+    hit = jnp.any(
+        own_routes[:, :, None] == jnp.arange(expert_count, dtype=jnp.int32)[None, None, :], axis=1
+    )
+    masked = jnp.where(hit, logits, MASK_FILL)
+    exponent = jnp.exp(masked - jnp.max(masked, axis=-1, keepdims=True))
+    gates = exponent / jnp.sum(exponent, axis=-1, keepdims=True)
+    hits = hit.astype(BRAIN_FLOAT_TYPE)
+    earlier = jnp.tril(jnp.ones((tokens, tokens), BRAIN_FLOAT_TYPE), -1)
+    rank = jnp.dot(earlier, hits, preferred_element_type=SINGLE_FLOAT)
+    rank = jnp.where(hit, rank, -1.0).astype(BRAIN_FLOAT_TYPE)
+    gate_high = gates.astype(BRAIN_FLOAT_TYPE)
+    gate_low = (gates - gate_high.astype(SINGLE_FLOAT)).astype(BRAIN_FLOAT_TYPE)
+    payload = jnp.concatenate(
+        [mixed, gate_high, gate_low, rank, jnp.zeros_like(rank)], axis=1
+    )
+    pay_all = lax.all_gather(payload, both, axis=0)
+    out_part, d_part, x_rows, d_rows, hidden, d_gate, d_up = expert_compute(
+        capacity, 4, me.astype(jnp.int32).reshape(1), pay_all, dout_all, expert_gate[0], expert_up[0], expert_down[0]
+    )
+    d_back = lax.psum_scatter(d_part, both, scatter_dimension=0, tiled=False)
+    moe_sum = lax.psum_scatter(out_part, both, scatter_dimension=0, tiled=False)
+    output = (hidden_state + moe_sum.astype(SINGLE_FLOAT)).astype(BRAIN_FLOAT_TYPE)
+    grad_gate = dot_left_transposed(x_rows, d_gate)[None]
+    grad_up = dot_left_transposed(x_rows, d_up)[None]
+    grad_down = dot_left_transposed(hidden, d_rows)[None]
+
+    table = d_back[:, width:].astype(SINGLE_FLOAT)
+    d_gates = table[:, :expert_count] + table[:, expert_count : 2 * expert_count]
+    d_chosen = gates * (d_gates - jnp.sum(gates * d_gates, axis=-1, keepdims=True))
+    d_logits = d_chosen.astype(BRAIN_FLOAT_TYPE)
+    d_mixed = d_back[:, :width].astype(SINGLE_FLOAT) + dot_right_transposed(
+        d_logits, router_matrix
+    )
+    grad_router = dot_left_transposed(mixed, d_logits)
+    d_state_norm, grad_ffn_gain = norm_backward(d_mixed, hidden_state, ffn_gain)
+    d_state = d_layer.astype(SINGLE_FLOAT) + d_state_norm
+    d_state_low = d_state.astype(BRAIN_FLOAT_TYPE)
+    dh_all = natural_order(lax.all_gather(d_state_low, "ctx", axis=0))
+    gwo, gw, dpart, ggain, gheads = attention_backward(
+        slack, dh_all, wo_all, attn, q, k, v, raw, normed, x_all, w_all, qg, kg, cosine, sine, segc, segr
+    )
+    d_normed = lax.psum_scatter(
+        device_order(dpart, ctx_count), "ctx", scatter_dimension=0, tiled=False
+    ).astype(SINGLE_FLOAT)
+    d_input_norm, _ = norm_backward(d_normed, layer_in, attn_gain)
+    grad_input = d_state + d_input_norm
+    grad_wo = lax.psum_scatter(gwo, "ws", scatter_dimension=0, tiled=True).astype(SINGLE_FLOAT)
+    owned = width // device_count
+    gw = gw.reshape(ctx_count, ws_count, owned, (heads + 2) * HEAD_DIM)
+    gw = lax.psum_scatter(gw, "ws", scatter_dimension=1, tiled=False)
+    gw = lax.all_to_all(gw, "ctx", split_axis=0, concat_axis=0).astype(SINGLE_FLOAT)
+    channels = heads * HEAD_DIM
+    grad_wq = gw[:, :, :channels].transpose(1, 0, 2).reshape(owned, ctx_count * channels)
+    shared = ctx_count // KEY_VALUE_HEADS
+    kv = gw[:, :, channels:].reshape(KEY_VALUE_HEADS, shared, owned, 2, HEAD_DIM).sum(1)
+    grad_wk = kv[:, :, 0].transpose(1, 0, 2).reshape(owned, KEY_VALUE_HEADS * HEAD_DIM)
+    grad_wv = kv[:, :, 1].transpose(1, 0, 2).reshape(owned, KEY_VALUE_HEADS * HEAD_DIM)
+    small = [ggain[0], gheads[0], gheads[1], grad_ffn_gain]
+    small = [lax.psum_scatter(g, both, scatter_dimension=0, tiled=True) for g in small]
+    grad_router = lax.psum_scatter(grad_router, both, scatter_dimension=0, tiled=True)
+    return (
+        output[None],
+        grad_input[None],
+        small[0],
+        grad_wq,
+        grad_wk,
+        grad_wv,
+        small[1],
+        small[2],
+        grad_wo,
+        small[3],
+        grad_router,
+        grad_gate,
+        grad_up,
+        grad_down,
+    )
+
+
+def planned_body(mesh):
+    if mesh.shape["ctx"] == 8 and mesh.shape["ws"] == 4:
+        return tensor_body
+    return general_body
+
+
 def solution(mesh):
     placed = (
         P("ws", "ctx", None),
@@ -507,7 +1158,7 @@
         P(("ctx", "ws"), None, None),
     )
     return jax.shard_map(
-        body,
+        planned_body(mesh),
         mesh=mesh,
         in_specs=placed,
         out_specs=(

time: 2490 us -> 1360 us (0.55)
  waiting for transfers between devices: 1730 us -> 908 us
  matrix products: 233 us -> 32.9 us
  Pallas kernels: 0 us -> 121 us
  local copies, waits for them, and re-layouts: 147 us -> 45.5 us
  blocking collectives: 262 us -> 176 us
    reduce_scatter x6 -> x5, waiting for transfers between devices: 1070 us -> 487 us  [the longest x1 189 us: tensor_body(): d_back = lax.psum_scatter(d_part, both, scatter_dimension=0, tiled=False)]
    all_to_all x4 -> x1, waiting for transfers between devices: 363 us -> 0.01 us  [tensor_body(): lax.all_to_all(gw, 'ctx', split_axis=0, concat_axis=0).astype(SINGLE_FLOAT)]
    dot_general x39 -> x6, matrix products: 231 us -> 31.6 us  [the longest x3 29.4 us: dot_left_transposed(): lax.dot_general(left, right, (((0,), (0,)), ((), ())), preferred_element_...]
    unnamed x14 -> x15, waiting for transfers between devices: 40.3 us -> 185 us
    all_gather x1, blocking collectives: 164 us -> 36 us  [tensor_body(): router_matrix = lax.all_gather(w_router, both, axis=0, tiled=True)]
    pallas_call x0 -> x3, Pallas kernels: none -> 121 us  [the longest x1 62.6 us: expert_compute(): pl.pallas_call(kernel, grid_spec=grid_spec, out_shape=(jax.ShapeDtypeStru...]
    gather x4 -> x0, local copies, waits for them, and re-layouts: 54.1 us -> none  [the longest x1 15.4 us: body(): d_outgoing = d_padded[source_slot].reshape(device_count, -1, model_width)]
    all_to_all x0 -> x1, blocking collectives: none -> 40.6 us  [tensor_body(): moved = lax.all_to_all(slabs, 'ctx', split_axis=0, concat_axis=0)]
  transfers between devices with their start and end apart: 17 -> 14, of which waited for: 16 -> 10; matrix products, arithmetic and copies ran while one was open for 12% -> 6% of each run, Pallas kernels for 0% -> 0%
where the time goes in v1:
time: 1360 us; the launch traced here: 1350 us
  waiting for transfers between devices  908 us (67%)
  blocking collectives  176 us (13%)
  Pallas kernels  121 us (9%)
  local copies, waits for them, and re-layouts  45.5 us (3%)
  other arithmetic  39.6 us (3%)
  matrix products  32.9 us (2%)
  between operations  16.3 us (1%)
    reduce_scatter x1, waiting for transfers between devices, tensor_body(): d_back = lax.psum_scatter(d_part, both, scatter_dimension=0, tiled=False)  189 us
    unnamed x15, waiting for transfers between devices  185 us
    all_gather x1, waiting for transfers between devices, tensor_body(): pay_all = lax.all_gather(payload, both, axis=0)  118 us
    reduce_scatter x1, waiting for transfers between devices, tensor_body(): moe_sum = lax.psum_scatter(out_part, both, scatter_dimension=0, tiled=False)  116 us
    reduce_scatter x1, waiting for transfers between devices, tensor_body(): lax.psum_scatter(device_order(part, ctx_count), 'ctx', scatter_dimension=...  111 us
    unnamed x2, blocking collectives  99.5 us
    all_gather x1, waiting for transfers between devices, tensor_body(): dh_all = natural_order(lax.all_gather(d_state_low, 'ctx', axis=0))  78.3 us
    reduce_scatter x1, waiting for transfers between devices, tensor_body(): lax.psum_scatter(device_order(dpart, ctx_count), 'ctx', scatter_dimension...  71.1 us
  transfers between devices with their start and end apart: 14, of which 10 were waited for; matrix products, arithmetic and copies ran while one was open for 6% of the time, Pallas kernels for 0%

profile of v1, /device:TPU:8, one launch (start us, length us, event | category | flops | bytes accessed | tf_op | source)
XLA Modules:
  0.0 1350.0 jit_solution(15821954718829254391)
XLA Ops:
  11.7 40.6 %all_to_all.10 = bf16[8,64,768]{2,1,0:T(8,128)(2,1)} all-to-all(bf16[8,64,768]{2,1,0:T(8,128)(2,1)S(1)} %fusion.20), channel_id=1, replica_groups=mesh['ctx'=8,'ws'=4] {'ctx'}, dimensions={0} | all-to-all | bytes 1572864 | tf_op jit(solution)/shard_map/all_to_all | solution.py:1014
  53.5 42.2 %all-reduce.10 = (bf16[2048]{0:T(1024)(128)(2,1)S(1)}, bf16[128]{0:T(256)(128)(2,1)S(1)}, bf16[128]{0:T(256)(128)(2,1)S(1)}, bf16[2048]{0:T(1024)(128)(2,1)S(1)}) all-reduce(bf16[2048]{0:T(1024)(128)(2,1)S(1)} %dynamic-update-slice, bf16[128]{0:T(256)(128)(2,1)S(1)} %dynamic-update-slice.1, ...), channel_id=1, replica_groups=mesh['ctx'=8,'ws'=4] {'ctx','ws'}, use_global_device_ids=true, to_apply=%add | all-reduce | flops 4352 | bytes 17408
  101.4 4.0 fusion.47
  106.8 5.1 pad_maximum_fusion.refs_0_.refs_8_
  112.0 9.8 all-gather.13.cloned.1.call-done.refs_9_.refs_1_
  121.8 30.1 %all-gather.17.cloned.1.call-done = bf16[8,256,768]{2,1,0:T(8,128)(2,1)} async-done(((bf16[8,64,768]{2,1,0:T(8,128)(2,1)}), bf16[8,256,768]{2,1,0:T(8,128)(2,1)}) %all-gather.17.cloned.1.call-update) | async-done | bytes 3145744 | tf_op jit(solution)/shard_map/all_gather | solution.py:1015
  152.0 21.8 %attention_forward.1 = (bf16[1024,2048]{1,0:T(8,128)(2,1)}, f32[1024,640]{1,0:T(8,128)}, bf16[1024,512]{1,0:T(8,128)(2,1)}, bf16[1024,128]{1,0:T(8,128)(2,1)}, b...) custom-call(bf16[1024,2048]{1,0:T(8,128)(2,1)} %pad_maximum_fusion.refs_0_.refs_8_, ...), custom_call_target="tpu_custom_call" | custom-call | tf_op jit(solution)/shard_map/attention_forward/pallas_call | solution.py:643
  173.8 4.0 fusion.46
  179.2 4.8 pad_maximum_fusion.1
  186.3 36.0 %all-gather.3 = bf16[32,64,32]{1,2,0:T(8,128)(2,1)S(1)} all-gather(bf16[1,64,32]{1,2,0:T(8,128)(2,1)S(1)} %bitcast.219), channel_id=1, replica_groups=mesh['ctx'=8,'ws'=4] {'ctx','ws'}, dimensions={0}, use_global_device_ids=true | all-gather | bytes 135168 | tf_op jit(solution)/shard_map/all_gather | solution.py:1023
  222.9 111.1 %reduce-scatter.12.cloned.1.call-done = bf16[1,128,2048]{2,1,0:T(8,128)(2,1)} async-done(((bf16[8,128,2048]{2,1,0:T(8,128)(2,1)}), bf16[1,128,2048]{2,1,0:T(8,128)(2,1)}) %reduce-scatter.12.cloned.1.call-update) | async-done | bytes 524304 | tf_op jit(solution)/shard_map/reduce_scatter | solution.py:1049
  338.4 117.8 %all-gather.19.cloned.1.call-done = bf16[4096,2176]{1,0:T(8,128)(2,1)} async-done(((bf16[128,2176]{1,0:T(8,128)(2,1)}), bf16[4096,2176]{1,0:T(8,128)(2,1)}) %all-gather.19.cloned.1.call-update) | async-done | bytes 17825808 | tf_op jit(solution)/shard_map/all_gather | solution.py:1072
  456.2 62.6 %expert_compute.1 = (bf16[32,128,2048]{2,1,0:T(8,128)(2,1)}, bf16[32,128,2176]{2,1,0:T(8,128)(2,1)}, bf16[1536,2048]{1,0:T(8,128)(2,1)}, bf16[1536,2048]{1,0:T(8...) custom-call(s32[1]{0:T(128)} %bitcast.20.refs_0_, ...), custom_call_target="tpu_custom_call" | custom-call | tf_op jit(solution)/shard_map/expert_compute/pallas_call | solution.py:927
  518.9 189.1 %reduce-scatter.16.cloned.1.call-done = bf16[1,128,2176]{2,1,0:T(8,128)(2,1)} async-done(((bf16[32,128,2176]{2,1,0:T(8,128)(2,1)}), bf16[1,128,2176]{2,1,0:T(8,128)(2,1)}) %reduce-scatter.16.cloned.1.call-update) | async-done | bytes 557072 | tf_op jit(solution)/shard_map/reduce_scatter | solution.py:1076
  713.1 78.3 %all-gather.21.cloned.1.call-done = bf16[1024,2048]{1,0:T(8,128)(2,1)} async-done(((bf16[128,2048]{1,0:T(8,128)(2,1)}), bf16[1024,2048]{1,0:T(8,128)(2,1)}) %all-gather.21.cloned.1.call-update) | async-done | bytes 4194320 | tf_op jit(solution)/shard_map/all_gather | solution.py:1094
  791.4 4.8 fusion.45
  796.2 3.2 rev.14
  799.4 4.8 pad_maximum_fusion.2.refs_0_
  804.2 36.6 %attention_backward.1 = (bf16[512,2048]{1,0:T(8,128)(2,1)}, bf16[2048,768]{1,0:T(8,128)(2,1)}, bf16[1024,2048]{1,0:T(8,128)(2,1)}, f32[1,2048]{1,0:T(1,128)}, f32[8,128]{1,0:T(8,128)}) custom-call(bf16[1024,2048]{1,0:T(8,128)(2,1)} %pad_maximum_fusion.2.refs_0_, bf16[512,2048]{1,0:T(8,128)(2,1)} %all-gather.13.cloned.1.call-done.refs_9_.refs_1_, ...), custom_call_target="tpu_custom_call" | custom-call | tf_op jit(solution)/shard_map/attention_backward/pallas_call | solution.py:796
  844.0 4.5 fusion.44
  849.9 4.8 pad_maximum_fusion.3
  856.0 9.8 convolution_bitcast_fusion.1
  865.8 9.9 convolution_bitcast_fusion.2
  875.7 62.8 %all-reduce.13.cloned.1.call-done = bf16[8,4,64,768]{3,2,1,0:T(8,128)(2,1)} async-done(((bf16[8,4,64,768]{3,2,1,0:T(8,128)(2,1)}), bf16[8,4,64,768]{3,2,1,0:T(8,128)(2,1)}) %all-reduce.13.cloned.1.call-update) | async-done | bytes 3145744
  938.5 2.7 dynamic-slice_bitcast_fusion
  941.3 9.3 all-to-all-start.1
  950.6 9.7 convolution_bitcast_fusion
  960.2 115.5 %reduce-scatter.14.cloned.1.call-done = bf16[1,128,2048]{2,1,0:T(8,128)(2,1)} async-done(((bf16[32,128,2048]{2,1,0:T(8,128)(2,1)}), bf16[1,128,2048]{2,1,0:T(8,128)(2,1)}) %reduce-scatter.14.cloned.1.call-update) | async-done | bytes 524304 | tf_op jit(solution)/shard_map/reduce_scatter | solution.py:1077
  1077.8 119.7 %reduce-scatter.22.cloned.1.call-done = f32[64,32]{1,0:T(8,128)} async-done(((f32[2048,32]{1,0:T(8,128)}), f32[64,32]{1,0:T(8,128)}) %reduce-scatter.22.cloned.1.call-update) | async-done | bytes 8208
  1199.8 57.3 %all-reduce.9 = (f32[2048]{0:T(1024)S(1)}, f32[128]{0:T(128)S(1)}, f32[128]{0:T(128)S(1)}, f32[2048]{0:T(1024)S(1)}) all-reduce(f32[2048]{0:T(1024)S(1)} %bitcast.220, f32[128]{0:T(128)S(1)} %get-tuple-element.95, f32[128]{0:T(128)S(1)} %get-tuple-element.94, ...), channel_id=9, replica_groups=mesh['ctx'=8,'ws'=4] {'ctx','ws'}, use_global_device_ids=true, to_apply=%region_15.16.clone | all-reduce | flops 4352 | bytes 34816
  1267.0 71.1 %reduce-scatter.18.cloned.1.call-done = bf16[1,128,2048]{2,1,0:T(8,128)(2,1)} async-done(((bf16[8,128,2048]{2,1,0:T(8,128)(2,1)}), bf16[1,128,2048]{2,1,0:T(8,128)(2,1)}) %reduce-scatter.18.cloned.1.call-update) | async-done | bytes 524304 | tf_op jit(solution)/shard_map/reduce_scatter | solution.py:1098
  1339.5 2.8 fusion.10
  (143 shorter events, 46.6 us)
Async XLA Ops:
  8.0 44.4 %copy-start.12 = (bf16[64]{0:T(256)(128)(2,1)S(1)}, bf16[64]{0:T(256)(128)(2,1)}, u32[]{:S(2)}) copy-start(bf16[64]{0:T(256)(128)(2,1)} %param.20) | copy-start | bytes 388
  8.0 44.7 %copy-start.13 = (bf16[64]{0:T(256)(128)(2,1)S(1)}, bf16[64]{0:T(256)(128)(2,1)}, u32[]{:S(2)}) copy-start(bf16[64]{0:T(256)(128)(2,1)} %param.27) | copy-start | bytes 388
  8.0 44.9 %copy-start.14 = (bf16[4]{0:T(256)(128)(2,1)S(1)}, bf16[4]{0:T(256)(128)(2,1)}, u32[]{:S(2)}) copy-start(bf16[4]{0:T(256)(128)(2,1)} %param.24) | copy-start | bytes 28
  8.0 45.2 %copy-start.15 = (bf16[4]{0:T(256)(128)(2,1)S(1)}, bf16[4]{0:T(256)(128)(2,1)}, u32[]{:S(2)}) copy-start(bf16[4]{0:T(256)(128)(2,1)} %param.25) | copy-start | bytes 28
  8.1 88.2 %copy-start.16 = (s32[1,4]{1,0:T(1,128)S(1)}, s32[1,4]{1,0:T(1,128)}, u32[]{:S(2)}) copy-start(s32[1,4]{1,0:T(1,128)} %param.19) | copy-start | bytes 52
  8.1 93.3 %all-gather.11.cloned.1.call-start = ((), (), s32[]{:S(2)}) async-start(), calls=%async_computation.8 | async-start | bytes 4718592 | tf_op jit(solution)/shard_map/all_gather | solution.py:1017
  8.8 113.0 %all-gather.13.cloned.1.call-start = ((), (), s32[]{:S(2)}) async-start(), calls=%async_computation.9 | async-start | bytes 2621440 | tf_op jit(solution)/shard_map/all_gather | solution.py:1016
  9.5 142.4 %all-gather.17.cloned.1.call-start = ((), (), s32[]{:S(2)}) async-start(), calls=%async_computation.16 | async-start | bytes 3932160 | tf_op jit(solution)/shard_map/all_gather | solution.py:1015
  52.4 281.6 %reduce-scatter.12.cloned.1.call-start = ((), (), s32[]{:S(2)}) async-start(), calls=%async_computation.10 | async-start | bytes 4718592 | tf_op jit(solution)/shard_map/reduce_scatter | solution.py:1049
  96.6 8.8 copy-start.7
  184.1 1.0 copy-start.2
  184.1 2.0 copy-start.10
  184.1 2.2 copy-start.8
  184.1 149.9 %copy-start = (bf16[1,128,2048]{2,1,0:T(8,128)(2,1)S(1)}, bf16[1,128,2048]{2,1,0:T(8,128)(2,1)}, u32[]{:S(2)}) copy-start(bf16[1,128,2048]{2,1,0:T(8,128)(2,1)} %param.16) | copy-start | bytes 1572868
  184.1 154.3 %all-gather.15.cloned.1.call-start = ((), (), s32[]{:S(2)}) async-start(), calls=%async_computation.11 | async-start | bytes 17301504 | tf_op jit(solution)/shard_map/all_gather | solution.py:1044
  186.0 270.1 %all-gather.19.cloned.1.call-start = ((), (), s32[]{:S(2)}) async-start(), calls=%async_computation.17 | async-start | bytes 18382848 | tf_op jit(solution)/shard_map/all_gather | solution.py:1072
  338.3 369.6 %reduce-scatter.16.cloned.1.call-start = ((), (), s32[]{:S(2)}) async-start(), calls=%async_computation.13 | async-start | bytes 18382848 | tf_op jit(solution)/shard_map/reduce_scatter | solution.py:1076
  518.8 190.3 %copy-start.1 = (bf16[1,128,2048]{2,1,0:T(8,128)(2,1)S(1)}, bf16[1,128,2048]{2,1,0:T(8,128)(2,1)}, u32[]{:S(2)}) copy-start(bf16[1,128,2048]{2,1,0:T(8,128)(2,1)} %reduce-scatter.12.cloned.1.call-done) | copy-start | bytes 1572868
  518.8 272.6 %all-gather.21.cloned.1.call-start = ((), (), s32[]{:S(2)}) async-start(), calls=%async_computation.18 | async-start | bytes 4718592 | tf_op jit(solution)/shard_map/all_gather | solution.py:1094
  710.7 1.0 copy-start.4
  713.0 225.5 %all-reduce.13.cloned.1.call-start = ((), (), s32[]{:S(2)}) async-start(), calls=%async_computation.20 | async-start | bytes 6291456
  840.9 234.9 %reduce-scatter.14.cloned.1.call-start = ((), (), s32[]{:S(2)}) async-start(), calls=%async_computation.12 | async-start | bytes 17301504 | tf_op jit(solution)/shard_map/reduce_scatter | solution.py:1077
  841.6 355.9 %reduce-scatter.22.cloned.1.call-start = ((), (), s32[]{:S(2)}) async-start(), calls=%async_computation.19 | async-start | bytes 1081344
  843.2 421.7 %reduce-scatter.20.cloned.1.call-start = ((), (), s32[]{:S(2)}) async-start(), calls=%async_computation.15 | async-start | bytes 2621440 | tf_op jit(solution)/shard_map/reduce_scatter | solution.py:1103
  843.9 494.2 %reduce-scatter.18.cloned.1.call-start = ((), (), s32[]{:S(2)}) async-start(), calls=%async_computation.14 | async-start | bytes 4718592 | tf_op jit(solution)/shard_map/reduce_scatter | solution.py:1098
  854.7 0.7 copy-start.17
  856.0 9.8 copy-start.11
  941.3 318.2 %all-to-all-start.1 = ((bf16[8,64,768]{2,1,0:T(8,128)(2,1)}), bf16[8,64,768]{2,1,0:T(8,128)(2,1)S(1)}, u32[]{:S(2)}, u32[]{:S(2)}) async-start(bf16[8,64,768]{2,1,0:T(8,128)(2,1)} %dynamic-slice_bitcast_fusion), calls=%async_computation.5 | async-start | bytes 1572864 | tf_op jit(solution)/shard_map/all_to_all | solution.py:1107
  950.6 249.2 %copy-start.9 = (f32[1,2048]{1,0:T(1,128)S(1)}, f32[1,2048]{1,0:T(1,128)}, u32[]{:S(2)}) copy-start(f32[1,2048]{1,0:T(1,128)} %get-tuple-element.43) | copy-start | bytes 24580
  1259.7 78.4 %copy-start.6 = (f32[2048]{0:T(1024)S(1)}, f32[2048]{0:T(1024)}, u32[]{:S(2)}) copy-start(f32[2048]{0:T(1024)} %convert_element_type.99) | copy-start | bytes 24580
  1259.7 79.8 %copy-start.3 = (bf16[1,128,2048]{2,1,0:T(8,128)(2,1)S(1)}, bf16[1,128,2048]{2,1,0:T(8,128)(2,1)}, u32[]{:S(2)}) copy-start(bf16[1,128,2048]{2,1,0:T(8,128)(2,1)} %param.17) | copy-start | bytes 1572868
  1259.7 79.8 %copy-start.5 = (f32[128,2048]{1,0:T(8,128)S(1)}, f32[128,2048]{1,0:T(8,128)}, u32[]{:S(2)}) copy-start(f32[128,2048]{1,0:T(8,128)} %copy-done.4) | copy-start | bytes 3145732
Sparse Core Ops, SparseCore 0:
  11.0 87.3 all-gather.10
  100.0 21.8 all-gather.12
  123.4 28.5 all-gather.16
  184.2 149.7 reduce-scatter.11
  713.2 78.2 all-gather.20
  841.0 97.4 all-reduce.12
Sparse Core Ops, SparseCore 1:
  187.9 140.4 all-gather.14
  338.4 117.8 all-gather.18
  518.9 189.0 reduce-scatter.15
  844.1 231.6 reduce-scatter.13
  1078.7 118.8 reduce-scatter.21
  1200.1 46.0 reduce-scatter.19
  1250.1 88.0 reduce-scatter.17

commit v2 on v1

--- a/solution.py
+++ b/solution.py
@@ -941,6 +941,740 @@
     )(expert, pay, dout, wg, wu, wd)
 
 
+MESH = pl.DeviceIdType.MESH
+ANYWHERE = pl.BlockSpec(memory_space=pl.ANY)
+LINE = 4
+
+
+def place():
+    c, w = lax.axis_index("ctx"), lax.axis_index("ws")
+    return c // 2, c % 2, w // 2, w % 2
+
+
+def device_at(z, y, x, k):
+    return (z * 2 + y, x * 2 + k)
+
+
+def slot_of(z, y, x, k):
+    return ((z * 2 + y) * 2 + x) * 2 + k
+
+
+def line_order(z):
+    upper = z // 2
+    return [z, z + 1 - 2 * upper, 2 - 2 * (z % 2) + upper, 3 - 3 * upper]
+
+
+def remote(source, target, send, recv, device):
+    return pltpu.make_async_remote_copy(
+        src_ref=source,
+        dst_ref=target,
+        send_sem=send,
+        recv_sem=recv,
+        device_id=device,
+        device_id_type=MESH,
+    )
+
+
+def meet(z, y, x, k, around):
+    barrier = pltpu.get_barrier_semaphore()
+
+    def greet(device):
+        pl.semaphore_signal(barrier, inc=1, device_id=device, device_id_type=MESH)
+
+    @pl.when(z < LINE - 1)
+    def _():
+        greet(device_at(z + 1, y, x, k))
+
+    @pl.when(z > 0)
+    def _():
+        greet(device_at(z - 1, y, x, k))
+
+    for device in around:
+        greet(device)
+    pl.semaphore_wait(barrier, len(around) + 1 + z * (LINE - 1 - z) // 2)
+
+
+class Sends:
+    def __init__(self, semaphores):
+        self.semaphores = semaphores
+        self.started = []
+
+    def start(self, source, target, recv, device, condition=None):
+        copy = remote(source, target, self.semaphores.at[len(self.started)], recv, device)
+        if condition is None:
+            copy.start()
+        else:
+            pl.when(condition)(copy.start)
+        self.started.append((condition, copy))
+
+    def finish(self):
+        for condition, copy in self.started:
+            if condition is None:
+                copy.wait_send()
+            else:
+                pl.when(condition)(copy.wait_send)
+
+
+def arrived(target, recv, device):
+    remote(target, target, recv, recv, device).wait_recv()
+
+
+def along_line(z, y, x, k, block, i, order, start):
+    if i == 0:
+        up, down = z < LINE - 1, z > 0
+    else:
+        below = order[i] < z
+        up, down = below & (z < LINE - 1), jnp.logical_not(below) & (z > 0)
+    start(block, device_at(z + 1, y, x, k), up)
+    start(block, device_at(z - 1, y, x, k), down)
+
+
+def gather_all_kernel(source, out, local, send_sems, recv_sems):
+    z, y, x, k = place()
+    order = line_order(z)
+    along_x, along_y = device_at(z, y, 1 - x, k), device_at(z, 1 - y, x, k)
+    sibling = device_at(z, y, x, 1 - k)
+    meet(z, y, x, k, (along_x, along_y, sibling))
+    sends = Sends(send_sems)
+    mine = slot_of(z, y, x, k)
+    own = pltpu.make_async_copy(source, out.at[mine], local)
+    own.start()
+
+    def pass_on(slot, device, condition=None):
+        block = source if slot is mine else out.at[slot]
+        sends.start(block, out.at[slot], recv_sems.at[slot], device, condition)
+
+    def wait(slot):
+        arrived(out.at[slot], recv_sems.at[slot], along_x)
+
+    def column(i):
+        slot = mine if i == 0 else slot_of(order[i], y, x, k)
+        if i > 0:
+            wait(slot)
+        along_line(z, y, x, k, slot, i, order, pass_on)
+        pass_on(slot, along_x)
+        pass_on(slot, along_y)
+        pass_on(slot, sibling)
+
+    def from_x(i):
+        slot = slot_of(order[i], y, 1 - x, k)
+        wait(slot)
+        pass_on(slot, sibling)
+        if i == 3:
+            for j in (0, 1):
+                pass_on(slot_of(order[j], y, 1 - x, k), along_y)
+
+    def from_y(i):
+        slot = slot_of(order[i], 1 - y, x, k)
+        wait(slot)
+        pass_on(slot, sibling)
+        if i == 3:
+            for j in (2, 3):
+                pass_on(slot_of(order[j], 1 - y, x, k), along_x)
+
+    def from_corner(i):
+        slot = slot_of(order[i], 1 - y, 1 - x, k)
+        wait(slot)
+        pass_on(slot, sibling)
+
+    column(0)
+    for i in (1, 2, 3):
+        column(i)
+        from_x(i - 1)
+        from_y(i - 1)
+    from_x(3)
+    from_y(3)
+    for i in range(4):
+        from_corner(i)
+    for i in range(4):
+        for dy in (y, 1 - y):
+            for dx in (x, 1 - x):
+                wait(slot_of(order[i], dy, dx, 1 - k))
+    own.wait()
+    sends.finish()
+
+
+def gather_all(block, collective_id):
+    return pl.pallas_call(
+        gather_all_kernel,
+        out_shape=jax.ShapeDtypeStruct((32,) + block.shape, block.dtype),
+        in_specs=[ANYWHERE],
+        out_specs=ANYWHERE,
+        scratch_shapes=[
+            pltpu.SemaphoreType.DMA,
+            pltpu.SemaphoreType.DMA((40,)),
+            pltpu.SemaphoreType.DMA((32,)),
+        ],
+        compiler_params=pltpu.CompilerParams(collective_id=collective_id, has_side_effects=True),
+        name="gather_all",
+    )(block)
+
+
+def add_blocks(target, *terms):
+    rows = target.shape[0]
+
+    def step(i, carry):
+        part = pl.ds(pl.multiple_of(i * 16, 16), 16)
+        total = terms[0][part, :].astype(SINGLE_FLOAT)
+        for term in terms[1:]:
+            total = total + term[part, :].astype(SINGLE_FLOAT)
+        target[part, :] = total.astype(target.dtype)
+        return carry
+
+    lax.fori_loop(0, rows // 16, step, 0)
+
+
+def scatter_line(z, y, x, k, order, total, owned, up_ref, down_ref, up_sems, down_sems, sends, out, after):
+    above, below = device_at(z + 1, y, x, k), device_at(z - 1, y, x, k)
+    for i in (3, 2, 1):
+        total(i)
+        chip = order[i]
+        upward = chip > z
+        block = owned(i)
+
+        @pl.when(upward & (z > 0))
+        def _():
+            arrived(up_ref.at[chip], up_sems.at[chip], below)
+            add_blocks(block, block, up_ref.at[chip])
+
+        @pl.when(jnp.logical_not(upward) & (z < LINE - 1))
+        def _():
+            arrived(down_ref.at[chip], down_sems.at[chip], above)
+            add_blocks(block, block, down_ref.at[chip])
+
+        sends.start(block, up_ref.at[chip], up_sems.at[chip], above, upward)
+        sends.start(
+            block, down_ref.at[chip], down_sems.at[chip], below, jnp.logical_not(upward)
+        )
+        after(i)
+    total(0)
+    block = owned(0)
+
+    @pl.when(z > 0)
+    def _():
+        arrived(up_ref.at[z], up_sems.at[z], below)
+
+    @pl.when(z < LINE - 1)
+    def _():
+        arrived(down_ref.at[z], down_sems.at[z], above)
+
+    @pl.when(z == 0)
+    def _():
+        add_blocks(out, block, down_ref.at[z])
+
+    @pl.when(z == LINE - 1)
+    def _():
+        add_blocks(out, block, up_ref.at[z])
+
+    @pl.when((z > 0) & (z < LINE - 1))
+    def _():
+        add_blocks(out, block, up_ref.at[z], down_ref.at[z])
+
+
+def scatter_all_kernel(
+    part,
+    out,
+    own_ref,
+    sibling_ref,
+    corner_ref,
+    x_ref,
+    y_ref,
+    up_ref,
+    down_ref,
+    load_sems,
+    sibling_sems,
+    corner_sems,
+    x_sems,
+    y_sems,
+    up_sems,
+    down_sems,
+    send_sems,
+):
+    z, y, x, k = place()
+    order = line_order(z)
+    along_x, along_y = device_at(z, y, 1 - x, k), device_at(z, 1 - y, x, k)
+    sibling = device_at(z, y, x, 1 - k)
+    meet(z, y, x, k, (along_x, along_y, sibling))
+    sends = Sends(send_sems)
+    home, on_x, on_y, corner = 0, 1, 2, 3
+    where = {home: (y, x), on_x: (y, 1 - x), on_y: (1 - y, x), corner: (1 - y, 1 - x)}
+    turn = [(i, corner) for i in (3, 2, 1, 0)]
+    for i in (3, 2, 1, 0):
+        turn += [(i, on_x), (i, on_y)]
+    turn += [(i, home) for i in (3, 2, 1, 0)]
+    loads = {}
+    for i, r in turn:
+        j = i * 4 + r
+        dy, dx = where[r]
+        sends.start(
+            part.at[slot_of(order[i], dy, dx, 1 - k)],
+            sibling_ref.at[j],
+            sibling_sems.at[j],
+            sibling,
+        )
+        loads[j] = pltpu.make_async_copy(
+            part.at[slot_of(order[i], dy, dx, k)], own_ref.at[j], load_sems.at[j]
+        )
+        loads[j].start()
+
+    def gather(i, r, *extra):
+        j = i * 4 + r
+        loads[j].wait()
+        arrived(sibling_ref.at[j], sibling_sems.at[j], sibling)
+        add_blocks(own_ref.at[j], own_ref.at[j], sibling_ref.at[j], *extra)
+        return own_ref.at[j]
+
+    for i in (3, 2, 1, 0):
+        sends.start(
+            gather(i, corner), corner_ref.at[i], corner_sems.at[i], along_y if i < 2 else along_x
+        )
+
+    def cross(i):
+        arrived(corner_ref.at[i], corner_sems.at[i], along_x)
+        extra = (corner_ref.at[i],)
+        for_x = gather(i, on_x, *(extra if i < 2 else ()))
+        for_y = gather(i, on_y, *(extra if i >= 2 else ()))
+        sends.start(for_x, x_ref.at[i], x_sems.at[i], along_x)
+        sends.start(for_y, y_ref.at[i], y_sems.at[i], along_y)
+
+    def total(i):
+        arrived(x_ref.at[i], x_sems.at[i], along_x)
+        arrived(y_ref.at[i], y_sems.at[i], along_y)
+        if i > 0:
+            cross(i - 1)
+        gather(i, home, x_ref.at[i], y_ref.at[i])
+
+    cross(3)
+    scatter_line(
+        z, y, x, k, order, total, lambda i: own_ref.at[i * 4 + home],
+        up_ref, down_ref, up_sems, down_sems, sends, out, lambda i: None,
+    )
+    sends.finish()
+
+
+def scatter_all(part, collective_id, dtype):
+    shape, low = part.shape[1:], part.dtype
+    dma = pltpu.SemaphoreType.DMA
+    return pl.pallas_call(
+        scatter_all_kernel,
+        out_shape=jax.ShapeDtypeStruct(shape, dtype),
+        in_specs=[ANYWHERE],
+        out_specs=VMEM_WHOLE,
+        scratch_shapes=[pltpu.VMEM((n,) + shape, low) for n in (16, 16, 4, 4, 4, 4, 4)]
+        + [dma((n,)) for n in (16, 16, 4, 4, 4, 4, 4)]
+        + [dma((40,))],
+        compiler_params=pltpu.CompilerParams(
+            collective_id=collective_id, has_side_effects=True, vmem_limit_bytes=VMEM_BYTES
+        ),
+        name="scatter_all",
+    )(part)
+
+
+def halves(ref, z, y):
+    half = ref.shape[0] // 16
+    c = z * 2 + y
+    return [
+        ref.at[pl.ds(pl.multiple_of(half * b, half), half), :] for b in (c, 15 - c)
+    ]
+
+
+def split_rows(ref):
+    half = ref.shape[0] // 2
+    return [ref.at[0:half, :], ref.at[half : 2 * half, :]]
+
+
+class RowGather:
+    def __init__(self, source, out, sends, locals_, semaphores, at, order, along_y):
+        self.source, self.out, self.sends, self.semaphores = source, out, sends, semaphores
+        self.at, self.order, self.along_y = at, order, along_y
+        z, y, x, k = at
+        self.own = [
+            pltpu.make_async_copy(a, b, locals_.at[n])
+            for n, (a, b) in enumerate(zip(split_rows(source), halves(out, z, y)))
+        ]
+        for copy in self.own:
+            copy.start()
+
+    def column(self, i):
+        z, y, x, k = self.at
+        chip = self.order[i]
+        pieces = halves(self.out, chip, y)
+        if i > 0:
+            self.wait(chip, y)
+        for n in (0, 1):
+            block = split_rows(self.source)[n] if i == 0 else pieces[n]
+            recv = self.semaphores.at[n, chip * 2 + y]
+
+            def start(_, device, condition=None):
+                self.sends.start(block, pieces[n], recv, device, condition)
+
+            along_line(z, y, x, k, None, i, self.order, start)
+            start(None, self.along_y)
+
+    def wait(self, chip, y):
+        for n, piece in enumerate(halves(self.out, chip, y)):
+            arrived(piece, self.semaphores.at[n, chip * 2 + y], self.along_y)
+
+    def finish(self):
+        y = self.at[1]
+        for i in range(4):
+            self.wait(self.order[i], 1 - y)
+        for copy in self.own:
+            copy.wait()
+
+
+def gather_rows_kernel(source, out, local_sems, send_sems, recv_sems):
+    at = place()
+    z, y, x, k = at
+    along_y = device_at(z, 1 - y, x, k)
+    meet(z, y, x, k, (along_y,))
+    sends = Sends(send_sems)
+    rows = RowGather(source, out, sends, local_sems, recv_sems, at, line_order(z), along_y)
+    for i in range(4):
+        rows.column(i)
+    rows.finish()
+    sends.finish()
+
+
+def gather_rows(block, collective_id):
+    rows, width = block.shape
+    dma = pltpu.SemaphoreType.DMA
+    return pl.pallas_call(
+        gather_rows_kernel,
+        out_shape=jax.ShapeDtypeStruct((8 * rows, width), block.dtype),
+        in_specs=[ANYWHERE],
+        out_specs=ANYWHERE,
+        scratch_shapes=[dma((2,)), dma((24,)), dma((2, 8))],
+        compiler_params=pltpu.CompilerParams(collective_id=collective_id, has_side_effects=True),
+        name="gather_rows",
+    )(block)
+
+
+class RowScatter:
+    def __init__(self, part, out, buffers, semaphores, sends, at, order, along_y):
+        self.part, self.out, self.sends, self.at, self.order = part, out, sends, at, order
+        self.along_y = along_y
+        self.own_ref, self.y_ref, self.up_ref, self.down_ref = buffers
+        self.load_sems, self.y_sems, self.up_sems, self.down_sems = semaphores
+        z, y, x, k = at
+        self.loads = {}
+        for i in (3, 2, 1, 0):
+            self.loads[i] = [
+                pltpu.make_async_copy(a, b, self.load_sems.at[n, i])
+                for n, (a, b) in enumerate(
+                    zip(halves(part, order[i], y), split_rows(self.own_ref.at[i]))
+                )
+            ]
+            for copy in self.loads[i]:
+                copy.start()
+        self.cross(3)
+
+    def cross(self, i):
+        y = self.at[1]
+        for n, (a, b) in enumerate(
+            zip(halves(self.part, self.order[i], 1 - y), split_rows(self.y_ref.at[i]))
+        ):
+            self.sends.start(a, b, self.y_sems.at[n, i], self.along_y)
+
+    def total(self, i):
+        for copy in self.loads[i]:
+            copy.wait()
+        for n, piece in enumerate(split_rows(self.y_ref.at[i])):
+            arrived(piece, self.y_sems.at[n, i], self.along_y)
+        if i > 0:
+            self.cross(i - 1)
+        add_blocks(self.own_ref.at[i], self.own_ref.at[i], self.y_ref.at[i])
+
+    def run(self, after=lambda i: None):
+        z, y, x, k = self.at
+        scatter_line(
+            z, y, x, k, self.order, self.total, lambda i: self.own_ref.at[i],
+            self.up_ref, self.down_ref, self.up_sems, self.down_sems, self.sends, self.out,
+            after,
+        )
+
+
+def row_scatter_scratch(rows, width, low):
+    dma = pltpu.SemaphoreType.DMA
+    return [pltpu.VMEM((4, rows, width), low)] * 4 + [
+        dma((2, 4)),
+        dma((2, 4)),
+        dma((4,)),
+        dma((4,)),
+    ]
+
+
+def scatter_rows_kernel(part, out, *scratch):
+    at = place()
+    z, y, x, k = at
+    along_y = device_at(z, 1 - y, x, k)
+    meet(z, y, x, k, (along_y,))
+    sends = Sends(scratch[8])
+    rows = RowScatter(part, out, scratch[:4], scratch[4:8], sends, at, line_order(z), along_y)
+    rows.run()
+    sends.finish()
+
+
+def scatter_rows(part, collective_id):
+    rows, width = part.shape[0] // 8, part.shape[1]
+    return pl.pallas_call(
+        scatter_rows_kernel,
+        out_shape=jax.ShapeDtypeStruct((rows, width), SINGLE_FLOAT),
+        in_specs=[ANYWHERE],
+        out_specs=VMEM_WHOLE,
+        scratch_shapes=row_scatter_scratch(rows, width, part.dtype)
+        + [pltpu.SemaphoreType.DMA((16,))],
+        compiler_params=pltpu.CompilerParams(
+            collective_id=collective_id, has_side_effects=True, vmem_limit_bytes=VMEM_BYTES
+        ),
+        name="scatter_rows",
+    )(part)
+
+
+def ring_of(c, w):
+    return [((c + t) % 8, w) for t in range(1, 8)]
+
+
+def gather_start_kernel(
+    x_in,
+    slab_in,
+    wo_in,
+    x_out,
+    slab_out,
+    wo_out,
+    local_sems,
+    send_sems,
+    x_sems,
+    slab_sems,
+    wo_sems,
+):
+    at = place()
+    z, y, x, k = at
+    c, w = z * 2 + y, x * 2 + k
+    along_x, along_y = device_at(z, y, 1 - x, k), device_at(z, 1 - y, x, k)
+    sibling = device_at(z, y, x, 1 - k)
+    others = ring_of(c, w)
+    barrier = pltpu.get_barrier_semaphore()
+    for device in others + [along_x, sibling]:
+        pl.semaphore_signal(barrier, inc=1, device_id=device, device_id_type=MESH)
+    pl.semaphore_wait(barrier, 9)
+    sends = Sends(send_sems)
+    rows = RowGather(
+        x_in, x_out, sends, local_sems.at[pl.ds(0, 2)], x_sems, at, line_order(z), along_y
+    )
+    wo_rows = wo_in.shape[0]
+
+    def wo_at(w):
+        return wo_out.at[pl.ds(pl.multiple_of(w * wo_rows, wo_rows), wo_rows), :]
+
+    mine = c * 4 + w
+    local = [
+        pltpu.make_async_copy(slab_in.at[c], slab_out.at[mine], local_sems.at[2]),
+        pltpu.make_async_copy(wo_in, wo_at(w), local_sems.at[3]),
+    ]
+    for copy in local:
+        copy.start()
+
+    def pass_on(slot, device, block=None):
+        block = slab_out.at[slot] if block is None else block
+        sends.start(block, slab_out.at[slot], slab_sems.at[slot], device)
+
+    def take(source, w):
+        slot = source * 4 + w
+        arrived(slab_out.at[slot], slab_sems.at[slot], along_x)
+        return slot
+
+    rows.column(0)
+    for device in (along_x, sibling):
+        sends.start(wo_in, wo_at(w), wo_sems.at[w], device)
+        pass_on(mine, device, slab_in.at[c])
+    for device in others:
+        sends.start(slab_in.at[device[0]], slab_out.at[mine], slab_sems.at[mine], device)
+
+    def onward():
+        for t in range(1, 8):
+            slot = take((c + 8 - t) % 8, w)
+            pass_on(slot, along_x)
+            pass_on(slot, sibling)
+
+    def across():
+        beside = (1 - x) * 2 + k
+        arrived(wo_at(beside), wo_sems.at[beside], along_x)
+        sends.start(wo_at(beside), wo_at(beside), wo_sems.at[beside], sibling)
+        for t in range(8):
+            pass_on(take((c + 8 - t) % 8, beside), sibling)
+
+    rows.column(1)
+    rows.column(2)
+    onward()
+    rows.column(3)
+    across()
+    for other in (x * 2 + 1 - k, (1 - x) * 2 + 1 - k):
+        for t in range(8):
+            take((c + 8 - t) % 8, other)
+        arrived(wo_at(other), wo_sems.at[other], along_x)
+    rows.finish()
+    for copy in local:
+        copy.wait()
+    sends.finish()
+
+
+def gather_start(x, slabs, wo, collective_id):
+    tokens, width = x.shape
+    low = BRAIN_FLOAT_TYPE
+    dma = pltpu.SemaphoreType.DMA
+    return pl.pallas_call(
+        gather_start_kernel,
+        out_shape=(
+            jax.ShapeDtypeStruct((8 * tokens, width), low),
+            jax.ShapeDtypeStruct((32,) + slabs.shape[1:], low),
+            jax.ShapeDtypeStruct((4 * wo.shape[0], width), low),
+        ),
+        in_specs=[ANYWHERE] * 3,
+        out_specs=[ANYWHERE] * 3,
+        scratch_shapes=[dma((4,)), dma((64,)), dma((2, 8)), dma((32,)), dma((4,))],
+        compiler_params=pltpu.CompilerParams(collective_id=collective_id, has_side_effects=True),
+        name="gather_start",
+    )(x, slabs, wo)
+
+
+def scatter_end_kernel(
+    part,
+    gw,
+    gwo,
+    small,
+    rows_out,
+    gw_out,
+    gwo_out,
+    small_out,
+    *scratch,
+):
+    row_scratch, row_sems = scratch[:4], scratch[4:8]
+    (
+        send_sems,
+        load_sems,
+        core_sems,
+        x_sems,
+        to_sems,
+        small_to_sems,
+        gw_own,
+        gw_core,
+        gw_x,
+        gwo_own,
+        gwo_core,
+        gwo_x,
+        small_own,
+        small_core,
+        small_x,
+        small_to,
+    ) = scratch[8:]
+    at = place()
+    z, y, x, k = at
+    c, w = z * 2 + y, x * 2 + k
+    along_x, along_y = device_at(z, y, 1 - x, k), device_at(z, 1 - y, x, k)
+    sibling = device_at(z, y, x, 1 - k)
+    others = ring_of(c, w)
+    barrier = pltpu.get_barrier_semaphore()
+    for device in others + [along_x, sibling]:
+        pl.semaphore_signal(barrier, inc=1, device_id=device, device_id_type=MESH)
+    pl.semaphore_wait(barrier, 9)
+    sends = Sends(send_sems)
+    rows = RowScatter(
+        part, rows_out, row_scratch, row_sems, sends, at, line_order(z), along_y
+    )
+    loads = []
+    for n, (source, core, own) in enumerate(
+        (
+            (small, small_core, small_own),
+            (gw, gw_core, gw_own),
+            (gwo, gwo_core, gwo_own),
+        )
+    ):
+        outer = (slice(None),) * (len(source.shape) - 3)
+        sends.start(source.at[(*outer, 1 - k)], core, core_sems.at[n], sibling)
+        loads.append(pltpu.make_async_copy(source.at[(*outer, k)], own, load_sems.at[n]))
+        loads[-1].start()
+
+    def fold(n, own, core):
+        loads[n].wait()
+        arrived(core, core_sems.at[n], sibling)
+        flat = [(i,) for i in range(own.shape[0])]
+        for extent in own.shape[1:-2]:
+            flat = [index + (j,) for index in flat for j in range(extent)]
+        for i in flat:
+            add_blocks(own.at[i], own.at[i], core.at[i])
+
+    fold(0, small_own, small_core)
+    sends.start(small_own.at[:, 1 - x], small_x, x_sems.at[0], along_x)
+    fold(1, gw_own, gw_core)
+    sends.start(gw_own.at[:, 1 - x], gw_x, x_sems.at[1], along_x)
+    fold(2, gwo_own, gwo_core)
+    keep = []
+
+    def weights(i):
+        if i == 2:
+            sends.start(gwo_own.at[1 - x], gwo_x, x_sems.at[2], along_x)
+            spread()
+
+    def spread():
+        for n, own, far in ((0, small_own, small_x), (1, gw_own, gw_x)):
+            arrived(far, x_sems.at[n], along_x)
+            for i in range(8):
+                add_blocks(own.at[i, x], own.at[i, x], far.at[i])
+            target, sems = (small_to, small_to_sems) if n == 0 else (gw_out, to_sems)
+            keep.append(
+                pltpu.make_async_copy(own.at[c, x], target.at[c], load_sems.at[3 + n])
+            )
+            keep[-1].start()
+            for device in others:
+                sends.start(own.at[device[0], x], target.at[c], sems.at[c], device)
+
+    rows.run(weights)
+    arrived(gwo_x, x_sems.at[2], along_x)
+    add_blocks(gwo_out, gwo_own.at[x], gwo_x)
+    for copy in keep:
+        copy.wait()
+    for t in range(1, 8):
+        source = (c + 8 - t) % 8
+        arrived(small_to.at[source], small_to_sems.at[source], along_x)
+        arrived(gw_out.at[source], to_sems.at[source], along_x)
+    total = small_to[0]
+    for i in range(1, 8):
+        total = total + small_to[i]
+    small_out[...] = total
+    sends.finish()
+
+
+def scatter_end(part, gw, gwo, small, collective_id):
+    rows, width = part.shape[0] // 8, part.shape[1]
+    low = part.dtype
+    dma, vmem = pltpu.SemaphoreType.DMA, pltpu.VMEM
+    r, n = gw.shape[3:]
+    ro, no = gwo.shape[2:]
+    rs, ns = small.shape[3:]
+    return pl.pallas_call(
+        scatter_end_kernel,
+        out_shape=(
+            jax.ShapeDtypeStruct((rows, width), SINGLE_FLOAT),
+            jax.ShapeDtypeStruct((8, r, n), low),
+            jax.ShapeDtypeStruct((ro, no), SINGLE_FLOAT),
+            jax.ShapeDtypeStruct((rs, ns), SINGLE_FLOAT),
+        ),
+        in_specs=[ANYWHERE] * 4,
+        out_specs=[VMEM_WHOLE, ANYWHERE, VMEM_WHOLE, VMEM_WHOLE],
+        scratch_shapes=row_scatter_scratch(rows, width, low)
+        + [dma((48,)), dma((5,)), dma((3,)), dma((3,)), dma((8,)), dma((8,))]
+        + [vmem((8, 2, r, n), low), vmem((8, 2, r, n), low), vmem((8, r, n), low)]
+        + [vmem((2, ro, no), low), vmem((2, ro, no), low), vmem((ro, no), low)]
+        + [vmem((8, 2, rs, ns), SINGLE_FLOAT), vmem((8, 2, rs, ns), SINGLE_FLOAT)]
+        + [vmem((8, rs, ns), SINGLE_FLOAT), vmem((8, rs, ns), SINGLE_FLOAT)],
+        compiler_params=pltpu.CompilerParams(
+            collective_id=collective_id, has_side_effects=True, vmem_limit_bytes=VMEM_BYTES
+        ),
+        name="scatter_end",
+    )(part, gw, gwo, small)
+
+
 def natural_order(blocks):
     count, rows, width = blocks.shape
     half = rows // 2
@@ -997,30 +1731,32 @@
     ctx_index = lax.axis_index("ctx")
     both = ("ctx", "ws")
     me = ctx_index * ws_count + lax.axis_index("ws")
+    small = jnp.concatenate([norm_attn, norm_ffn, query_norm, key_norm, w_router.reshape(-1)])
+    columns = (heads + 2) * HEAD_DIM
+    small = jnp.pad(small, (0, 16 * columns - small.shape[0])).reshape(16, columns)
     slabs = []
     for c in range(ctx_count):
         kv = c * heads // group
-        slabs.append(
-            jnp.concatenate(
-                [
-                    w_query[:, c * heads * HEAD_DIM : (c + 1) * heads * HEAD_DIM],
-                    key_projection[:, kv * HEAD_DIM : (kv + 1) * HEAD_DIM],
-                    value_projection[:, kv * HEAD_DIM : (kv + 1) * HEAD_DIM],
-                ],
-                axis=1,
-            )
-        )
-    slabs = jnp.stack(slabs)
-    moved = lax.all_to_all(slabs, "ctx", split_axis=0, concat_axis=0)
-    w_all = lax.all_gather(moved, "ws", axis=1).reshape(width, (heads + 2) * HEAD_DIM)
-    wo_all = lax.all_gather(w_out, "ws", axis=0, tiled=True)
-    x_blocks = lax.all_gather(inputs[0], "ctx", axis=0)
-    x_all = natural_order(x_blocks)
-    attn_gain = lax.all_gather(norm_attn, both, tiled=True).astype(SINGLE_FLOAT)
-    ffn_gain = lax.all_gather(norm_ffn, both, tiled=True).astype(SINGLE_FLOAT)
-    query_gain = lax.all_gather(query_norm, both, tiled=True).astype(SINGLE_FLOAT)
-    key_gain = lax.all_gather(key_norm, both, tiled=True).astype(SINGLE_FLOAT)
-    router_matrix = lax.all_gather(w_router, both, axis=0, tiled=True)
+        slab = jnp.concatenate(
+            [
+                w_query[:, c * heads * HEAD_DIM : (c + 1) * heads * HEAD_DIM],
+                key_projection[:, kv * HEAD_DIM : (kv + 1) * HEAD_DIM],
+                value_projection[:, kv * HEAD_DIM : (kv + 1) * HEAD_DIM],
+            ],
+            axis=1,
+        )
+        slabs.append(jnp.concatenate([slab, small], axis=0))
+    owned, few = width // device_count, query_norm.shape[0]
+    x_all, slabs, wo_all = gather_start(inputs[0], jnp.stack(slabs), w_out, 1)
+    w_all = slabs[:, :owned].reshape(width, columns)
+    small = slabs[:, owned:].reshape(device_count, 16 * columns)
+    attn_gain = small[:, :owned].reshape(width).astype(SINGLE_FLOAT)
+    ffn_gain = small[:, owned : 2 * owned].reshape(width).astype(SINGLE_FLOAT)
+    at = 2 * owned
+    query_gain = small[:, at : at + few].reshape(HEAD_DIM).astype(SINGLE_FLOAT)
+    key_gain = small[:, at + few : at + 2 * few].reshape(HEAD_DIM).astype(SINGLE_FLOAT)
+    at = at + 2 * few
+    router_matrix = small[:, at : at + owned * expert_count].reshape(width, expert_count)
 
     places = jnp.arange(sequence_tokens, dtype=jnp.int32)
     segments = segment_ids(doc_lengths[0], places)
@@ -1041,16 +1777,13 @@
     own_segments = segment_ids(doc_lengths[0], own_places)
     validity = own_segments < doc_lengths.shape[1]
     d_layer = jnp.where(validity[:, None], grad_output[0], 0.0).astype(BRAIN_FLOAT_TYPE)
-    dout_all = lax.all_gather(d_layer, both, axis=0)
 
     normed, raw, q, k, v, attn, part = attention_forward(
         slack, x_all, attn_gain[None, :], w_all, qg, kg, cosine, sine, segc, segr, wo_all
     )
-    branch = lax.psum_scatter(
-        device_order(part, ctx_count), "ctx", scatter_dimension=0, tiled=False
-    )
+    branch = scatter_rows(part, 2)
     layer_in = inputs[0].astype(SINGLE_FLOAT)
-    hidden_state = layer_in + branch.astype(SINGLE_FLOAT)
+    hidden_state = layer_in + branch
     mixed = rms_scale(hidden_state, ffn_gain).astype(BRAIN_FLOAT_TYPE)
     logits = jnp.dot(mixed, router_matrix, preferred_element_type=SINGLE_FLOAT)
     own_routes = routes[0]
@@ -1069,63 +1802,74 @@
     payload = jnp.concatenate(
         [mixed, gate_high, gate_low, rank, jnp.zeros_like(rank)], axis=1
     )
-    pay_all = lax.all_gather(payload, both, axis=0)
+    pay_all = gather_all(payload, 3)
+    dout_all = gather_all(d_layer, 7)
     out_part, d_part, x_rows, d_rows, hidden, d_gate, d_up = expert_compute(
         capacity, 4, me.astype(jnp.int32).reshape(1), pay_all, dout_all, expert_gate[0], expert_up[0], expert_down[0]
     )
-    d_back = lax.psum_scatter(d_part, both, scatter_dimension=0, tiled=False)
-    moe_sum = lax.psum_scatter(out_part, both, scatter_dimension=0, tiled=False)
-    output = (hidden_state + moe_sum.astype(SINGLE_FLOAT)).astype(BRAIN_FLOAT_TYPE)
+    d_back = scatter_all(d_part, 4, SINGLE_FLOAT)
+    moe_sum = scatter_all(out_part, 8, SINGLE_FLOAT)
+    output = (hidden_state + moe_sum).astype(BRAIN_FLOAT_TYPE)
     grad_gate = dot_left_transposed(x_rows, d_gate)[None]
     grad_up = dot_left_transposed(x_rows, d_up)[None]
     grad_down = dot_left_transposed(hidden, d_rows)[None]
 
-    table = d_back[:, width:].astype(SINGLE_FLOAT)
+    table = d_back[:, width:]
     d_gates = table[:, :expert_count] + table[:, expert_count : 2 * expert_count]
     d_chosen = gates * (d_gates - jnp.sum(gates * d_gates, axis=-1, keepdims=True))
     d_logits = d_chosen.astype(BRAIN_FLOAT_TYPE)
-    d_mixed = d_back[:, :width].astype(SINGLE_FLOAT) + dot_right_transposed(
+    d_mixed = d_back[:, :width] + dot_right_transposed(
         d_logits, router_matrix
     )
     grad_router = dot_left_transposed(mixed, d_logits)
     d_state_norm, grad_ffn_gain = norm_backward(d_mixed, hidden_state, ffn_gain)
     d_state = d_layer.astype(SINGLE_FLOAT) + d_state_norm
     d_state_low = d_state.astype(BRAIN_FLOAT_TYPE)
-    dh_all = natural_order(lax.all_gather(d_state_low, "ctx", axis=0))
+    dh_all = gather_rows(d_state_low, 5)
     gwo, gw, dpart, ggain, gheads = attention_backward(
         slack, dh_all, wo_all, attn, q, k, v, raw, normed, x_all, w_all, qg, kg, cosine, sine, segc, segr
     )
-    d_normed = lax.psum_scatter(
-        device_order(dpart, ctx_count), "ctx", scatter_dimension=0, tiled=False
-    ).astype(SINGLE_FLOAT)
+    blocks = (ctx_count, ws_count // 2, 2)
+    small = jnp.concatenate(
+        [
+            ggain.reshape(device_count, owned),
+            grad_ffn_gain.reshape(device_count, owned),
+            gheads[0].reshape(device_count, few),
+            gheads[1].reshape(device_count, few),
+            grad_router.reshape(device_count, owned * expert_count),
+        ],
+        axis=1,
+    )
+    small = jnp.pad(small, ((0, 0), (0, 32 * 128 - small.shape[1]))).reshape(*blocks, 32, 128)
+    d_normed, gw, grad_wo, small = scatter_end(
+        dpart,
+        gw.reshape(*blocks, owned, columns),
+        gwo.reshape(*blocks[1:], w_out.shape[0], width),
+        small,
+        6,
+    )
+    small = small.reshape(-1)
     d_input_norm, _ = norm_backward(d_normed, layer_in, attn_gain)
     grad_input = d_state + d_input_norm
-    grad_wo = lax.psum_scatter(gwo, "ws", scatter_dimension=0, tiled=True).astype(SINGLE_FLOAT)
-    owned = width // device_count
-    gw = gw.reshape(ctx_count, ws_count, owned, (heads + 2) * HEAD_DIM)
-    gw = lax.psum_scatter(gw, "ws", scatter_dimension=1, tiled=False)
-    gw = lax.all_to_all(gw, "ctx", split_axis=0, concat_axis=0).astype(SINGLE_FLOAT)
+    gw = gw.astype(SINGLE_FLOAT)
     channels = heads * HEAD_DIM
     grad_wq = gw[:, :, :channels].transpose(1, 0, 2).reshape(owned, ctx_count * channels)
     shared = ctx_count // KEY_VALUE_HEADS
     kv = gw[:, :, channels:].reshape(KEY_VALUE_HEADS, shared, owned, 2, HEAD_DIM).sum(1)
     grad_wk = kv[:, :, 0].transpose(1, 0, 2).reshape(owned, KEY_VALUE_HEADS * HEAD_DIM)
     grad_wv = kv[:, :, 1].transpose(1, 0, 2).reshape(owned, KEY_VALUE_HEADS * HEAD_DIM)
-    small = [ggain[0], gheads[0], gheads[1], grad_ffn_gain]
-    small = [lax.psum_scatter(g, both, scatter_dimension=0, tiled=True) for g in small]
-    grad_router = lax.psum_scatter(grad_router, both, scatter_dimension=0, tiled=True)
     return (
         output[None],
         grad_input[None],
-        small[0],
+        small[:owned],
         grad_wq,
         grad_wk,
         grad_wv,
-        small[1],
-        small[2],
+        small[2 * owned : at - few],
+        small[at - few : at],
         grad_wo,
-        small[3],
-        grad_router,
+        small[owned : 2 * owned],
+        small[at : at + owned * expert_count].reshape(owned, expert_count),
         grad_gate,
         grad_up,
         grad_down,

time: 1360 us -> 773 us (0.57)
  waiting for transfers between devices: 908 us -> 0 us
  Pallas kernels: 121 us -> 685 us
  blocking collectives: 176 us -> 0 us
  other arithmetic: 39.6 us -> 18.3 us
  local copies, waits for them, and re-layouts: 45.5 us -> 29.5 us
  between operations: 16.3 us -> 1.57 us
    pallas_call x0 -> x8, Pallas kernels: none -> 564 us  [the longest x2 168 us: scatter_all(): pl.pallas_call(scatter_all_kernel, out_shape=jax.ShapeDtypeStruct(shape,...]
    reduce_scatter x5 -> x0, waiting for transfers between devices: 487 us -> none  [the longest x1 189 us: tensor_body(): d_back = lax.psum_scatter(d_part, both, scatter_dimension=0, tiled=False)]
    all_gather x6 -> x0, waiting for transfers between devices: 236 us -> none  [the longest x1 118 us: tensor_body(): pay_all = lax.all_gather(payload, both, axis=0)]
    unnamed x15 -> x0, waiting for transfers between devices: 185 us -> none
    unnamed x2 -> x0, blocking collectives: 99.5 us -> none
    all_to_all x1 -> x0, blocking collectives: 40.6 us -> none  [tensor_body(): moved = lax.all_to_all(slabs, 'ctx', split_axis=0, concat_axis=0)]
    all_gather x1 -> x0, blocking collectives: 36 us -> none  [tensor_body(): router_matrix = lax.all_gather(w_router, both, axis=0, tiled=True)]
    concatenate x4 -> x0, other arithmetic: 19.6 us -> none  [the longest x2 9.95 us: natural_order(): return jnp.concatenate([first, second], axis=0)]
  transfers between devices with their start and end apart: 14 -> 0, of which waited for: 10 -> 0; matrix products, arithmetic and copies ran while one was open for 6% -> 0% of each run, Pallas kernels for 0% -> 0%
where the time goes in v2:
time: 773 us; the launch traced here: 764 us
  Pallas kernels  685 us (89%)
  local copies, waits for them, and re-layouts  29.5 us (4%)
  matrix products  29 us (4%)
  other arithmetic  18.3 us (2%)
    pallas_call x2, Pallas kernels, scatter_all(): pl.pallas_call(scatter_all_kernel, out_shape=jax.ShapeDtypeStruct(shape,...  168 us
    pallas_call x2, Pallas kernels, gather_all(): pl.pallas_call(gather_all_kernel, out_shape=jax.ShapeDtypeStruct((32,) +...  159 us
    pallas_call x1, Pallas kernels, scatter_end(): pl.pallas_call(scatter_end_kernel, out_shape=(jax.ShapeDtypeStruct((rows,...  67.7 us
    pallas_call x1, Pallas kernels, expert_compute(): pl.pallas_call(kernel, grid_spec=grid_spec, out_shape=(jax.ShapeDtypeStru...  62.7 us
    pallas_call x1, Pallas kernels, gather_start(): pl.pallas_call(gather_start_kernel, out_shape=(jax.ShapeDtypeStruct((8 *...  61.6 us
    pallas_call x1, Pallas kernels, scatter_rows(): pl.pallas_call(scatter_rows_kernel, out_shape=jax.ShapeDtypeStruct((rows,...  59.8 us
    pallas_call x1, Pallas kernels, gather_rows(): pl.pallas_call(gather_rows_kernel, out_shape=jax.ShapeDtypeStruct((8 * ro...  47.6 us
    pallas_call x1, Pallas kernels, attention_backward(): pl.pallas_call(kernel, out_shape=shapes, in_specs=[VMEM_WHOLE] * 16, out_...  36.6 us

profile of v2, /device:TPU:8, one launch (start us, length us, event | category | flops | bytes accessed | tf_op | source)
XLA Modules:
  0.0 763.8 jit_solution(3671553312353528282)
XLA Ops:
  3.4 2.8 concatenate.64
  8.3 2.0 bitcast_select_fusion.source
  10.3 1.1 fusion.39
  11.6 1.9 fusion.10
  13.5 1.3 pad_maximum_fusion
  14.8 61.6 %gather_start.1 = (bf16[1024,2048]{1,0:T(8,128)(2,1)}, bf16[32,80,768]{2,1,0:T(8,128)(2,1)}, bf16[512,2048]{1,0:T(8,128)(2,1)}) custom-call(bf16[128,2048]{1,0:T(8,128)(2,1)} %bitcast.110, bf16[8,80,768]{2,1,0:T(8,128)(2,1)} %copy-done.4, bf16[128,2048]{1,0:T(8,128)(2,1)} %wo_in.1), custom_call_target="tpu_custom_call" | custom-call | tf_op jit(solution)/shard_map/gather_start/pallas_call | solution.py:1526
  76.4 1.2 slice.138
  77.6 4.0 slice.140
  84.5 22.0 %attention_forward.1 = (bf16[1024,2048]{1,0:T(8,128)(2,1)}, f32[1024,640]{1,0:T(8,128)}, bf16[1024,512]{1,0:T(8,128)(2,1)}, bf16[1024,128]{1,0:T(8,128)(2,1)}, b...) custom-call(bf16[1024,2048]{1,0:T(8,128)(2,1)} %get-tuple-element.40.refs_0_.refs_8_, ...), custom_call_target="tpu_custom_call" | custom-call | tf_op jit(solution)/shard_map/attention_forward/pallas_call | solution.py:643
  106.5 59.8 %scatter_rows.1 = f32[128,2048]{1,0:T(8,128)} custom-call(bf16[1024,2048]{1,0:T(8,128)(2,1)} %get-tuple-element.43.part), custom_call_target="tpu_custom_call" | custom-call | tf_op jit(solution)/shard_map/scatter_rows/pallas_call | solution.py:1420
  166.4 1.5 multiply_reduce_fusion.2
  169.7 76.8 %gather_all.3.refs_2_ = bf16[32,128,2048]{2,1,0:T(8,128)(2,1)} custom-call(bf16[128,2048]{1,0:T(8,128)(2,1)} %bitcast_select_fusion.source), custom_call_target="tpu_custom_call" | custom-call | tf_op jit(solution)/shard_map/gather_all/pallas_call | solution.py:1098
  246.6 82.5 %gather_all.2.refs_1_ = bf16[32,128,2176]{2,1,0:T(8,128)(2,1)} custom-call(bf16[128,2176]{1,0:T(8,128)(2,1)} %concatenate.82.source), custom_call_target="tpu_custom_call" | custom-call | tf_op jit(solution)/shard_map/gather_all/pallas_call | solution.py:1098
  329.0 62.7 %expert_compute.1 = (bf16[32,128,2048]{2,1,0:T(8,128)(2,1)}, bf16[32,128,2176]{2,1,0:T(8,128)(2,1)}, bf16[1536,2048]{1,0:T(8,128)(2,1)}, bf16[1536,2048]{1,0:T(8...) custom-call(s32[1]{0:T(128)} %bitcast.14.refs_0_, ...), custom_call_target="tpu_custom_call" | custom-call | tf_op jit(solution)/shard_map/expert_compute/pallas_call | solution.py:927
  391.7 81.4 %scatter_all.2 = f32[128,2048]{1,0:T(8,128)} custom-call(bf16[32,128,2048]{2,1,0:T(8,128)(2,1)} %get-tuple-element.44.part), custom_call_target="tpu_custom_call" | custom-call | tf_op jit(solution)/shard_map/scatter_all/pallas_call | solution.py:1258
  473.1 86.6 %scatter_all.3 = f32[128,2176]{1,0:T(8,128)} custom-call(bf16[32,128,2176]{2,1,0:T(8,128)(2,1)} %get-tuple-element.45.part), custom_call_target="tpu_custom_call" | custom-call | tf_op jit(solution)/shard_map/scatter_all/pallas_call | solution.py:1258
  559.8 1.1 multiply_reduce_fusion.3
  560.9 2.3 fusion.46
  563.2 2.4 reshape.217
  565.6 2.0 multiply_reduce_fusion
  567.7 1.1 fusion.38.source
  568.8 47.6 %gather_rows.1.refs_0_ = bf16[1024,2048]{1,0:T(8,128)(2,1)} custom-call(bf16[128,2048]{1,0:T(8,128)(2,1)} %fusion.38.source), custom_call_target="tpu_custom_call" | custom-call | tf_op jit(solution)/shard_map/gather_rows/pallas_call | solution.py:1342
  616.5 36.6 %attention_backward.1 = (bf16[512,2048]{1,0:T(8,128)(2,1)}, bf16[2048,768]{1,0:T(8,128)(2,1)}, bf16[1024,2048]{1,0:T(8,128)(2,1)}, f32[1,2048]{1,0:T(1,128)}, f32[8,128]{1,0:T(8,128)}) custom-call(bf16[1024,2048]{1,0:T(8,128)(2,1)} %gather_rows.1.refs_0_, bf16[512,2048]{1,0:T(8,128)(2,1)} %get-tuple-element.42.refs_9_.refs_1_, ...), custom_call_target="tpu_custom_call" | custom-call | tf_op jit(solution)/shard_map/attention_backward/pallas_call | solution.py:796
  654.4 1.4 reduce.11
  656.1 1.1 concatenate.83
  658.1 67.7 %scatter_end.1 = (f32[128,2048]{1,0:T(8,128)}, bf16[8,64,768]{2,1,0:T(8,128)(2,1)}, f32[128,2048]{1,0:T(8,128)}, f32[32,128]{1,0:T(8,128)}) custom-call(bf16[1024,2048]{1,0:T(8,128)(2,1)} %get-tuple-element.52.part, bf16[8,2,2,64,768]{4,3,2,1,0:T(8,128)(2,1)} %bitcast.114, bf16[2,2,128,2048]{3,2,1,0:T(8,128)(2,1)} %bitcast.116, f32[8,2,2,32,128]{4,3,2,1,0:T(8,128)} %bitcast.117), custom_call_target="tpu_custom_call" | custom-call | tf_op jit(solution)/shard_map/scatter_end/pallas_call | solution.py:1655
  725.9 1.5 fusion.3
  727.4 3.4 fusion.7
  736.4 1.1 copy.77
  738.1 10.1 %convolution_bitcast_fusion.2 = f32[1,2048,768]{2,1,0:T(8,128)} fusion(bf16[1536,2048]{1,0:T(8,128)(2,1)} %get-tuple-element.61, bf16[1536,768]{1,0:T(8,128)(2,1)S(1)} %copy-done.10), kind=kOutput, calls=%fused_computation.2 | convolution fusion | flops 4831838208 | bytes 14942208 | tf_op jit(solution)/shard_map/dot_general | solution.py:514
  748.3 7.1 convolution_bitcast_fusion.1
  755.4 7.0 convolution_bitcast_fusion
  (99 shorter events, 19.4 us)
Async XLA Ops:
  1.7 11.8 %copy-start.6 = (s32[1024]{0:T(1024)}, s32[1024]{0:T(1024)S(1)}, u32[]{:S(2)}) copy-start(s32[1024]{0:T(1024)S(1)} %convert_reduce_fusion) | copy-start | bytes 12292
  11.6 3.3 copy-start.4
  84.5 83.5 %copy-start.2 = (bf16[2048,32]{1,0:T(8,128)(2,1)}, bf16[2048,32]{1,0:T(8,128)(2,1)S(1)}, u32[]{:S(2)}) copy-start(bf16[2048,32]{1,0:T(8,128)(2,1)S(1)} %reshape.212) | copy-start | bytes 393220
  106.5 59.8 %copy-start = (bf16[1,128,2048]{2,1,0:T(8,128)(2,1)S(1)}, bf16[1,128,2048]{2,1,0:T(8,128)(2,1)}, u32[]{:S(2)}) copy-start(bf16[1,128,2048]{2,1,0:T(8,128)(2,1)} %param.16) | copy-start | bytes 1572868
  559.7 8.0 %copy-start.1 = (bf16[1,128,2048]{2,1,0:T(8,128)(2,1)S(1)}, bf16[1,128,2048]{2,1,0:T(8,128)(2,1)}, u32[]{:S(2)}) copy-start(bf16[1,128,2048]{2,1,0:T(8,128)(2,1)} %param.17) | copy-start | bytes 1572868
  727.4 3.4 copy-start.7
  730.8 5.2 copy-start.3
  736.1 2.0 copy-start.10
  736.3 11.9 %slice-start.2 = ((s8[6291456]{0:T(1024)(128)(4,1)}), s8[4194304]{0:T(1024)(128)(4,1)S(1)}, s32[]{:S(2)}) async-start(s8[6291456]{0:T(1024)(128)(4,1)} %bitcast.135), calls=%async_computation.2 | async-start | bytes 8388608
  738.1 10.1 %slice-start.3 = ((s8[6291456]{0:T(1024)(128)(4,1)}), s8[2097152]{0:T(1024)(128)(4,1)S(1)}, s32[]{:S(2)}) async-start(s8[6291456]{0:T(1024)(128)(4,1)} %bitcast.135), calls=%async_computation.3 | async-start | bytes 4194304
  738.1 10.1 %copy-start.9 = (bf16[1536,768]{1,0:T(8,128)(2,1)S(1)}, bf16[1536,768]{1,0:T(8,128)(2,1)}, u32[]{:S(2)}) copy-start(bf16[1536,768]{1,0:T(8,128)(2,1)} %get-tuple-element.63) | copy-start | bytes 7077892
  738.1 17.2 %slice-start = ((s8[6291456]{0:T(1024)(128)(4,1)}), s8[4194304]{0:T(1024)(128)(4,1)S(1)}, s32[]{:S(2)}) async-start(s8[6291456]{0:T(1024)(128)(4,1)} %bitcast.133), calls=%async_computation | async-start | bytes 8388608
  748.3 7.1 slice-start.1
  748.3 7.1 copy-start.8
  755.3 7.0 copy-start.5

commit v3 on v2

--- a/solution.py
+++ b/solution.py
@@ -809,138 +809,6 @@
     )(dh, wo, attn, q, k, v, raw, normed, x, w, qg, kg, cosine, sine, segc, segr)
 
 
-def expert_kernel(
-    capacity,
-    expert_ref,
-    pay_ref,
-    dout_ref,
-    wg_ref,
-    wu_ref,
-    wd_ref,
-    outp_ref,
-    dp_ref,
-    x_ref,
-    deo_ref,
-    hid_ref,
-    dgl_ref,
-    dul_ref,
-    d_ref,
-    g_ref,
-    st_ref,
-):
-    sources, tokens, payload = pay_ref.shape
-    width = wg_ref.shape[0]
-    experts = (payload - width) // 4
-    e = expert_ref[0]
-    lane = lax.broadcasted_iota(jnp.int32, (tokens, payload - width), 1)
-    slot_lane = lax.broadcasted_iota(jnp.int32, (tokens, capacity), 1).astype(SINGLE_FLOAT)
-    row_lane = lax.broadcasted_iota(jnp.int32, (capacity, payload - width), 1)
-    is_gate = (row_lane == e) | (row_lane == experts + e)
-    for s in range(sources):
-        rows = slice(s * capacity, (s + 1) * capacity)
-        table = pay_ref[s, :, width:].astype(SINGLE_FLOAT)
-        rank = jnp.sum(jnp.where(lane == 2 * experts + e, table, 0.0), axis=-1, keepdims=True)
-        pick = (rank == slot_lane).astype(BRAIN_FLOAT_TYPE)
-        st_ref[s] = pick
-        chosen = dot_left_transposed(pick, pay_ref[s])
-        x_ref[rows, :] = chosen[:, :width].astype(BRAIN_FLOAT_TYPE)
-        gate = jnp.sum(jnp.where(is_gate, chosen[:, width:], 0.0), axis=-1, keepdims=True)
-        g_ref[rows, :] = gate
-        d_rows = dot_left_transposed(pick, dout_ref[s])
-        d_ref[rows, :] = d_rows.astype(BRAIN_FLOAT_TYPE)
-        deo_ref[rows, :] = (gate * d_rows).astype(BRAIN_FLOAT_TYPE)
-    x = x_ref[...]
-    gate_hidden = dot_rows(x, wg_ref[...])
-    up_hidden = dot_rows(x, wu_ref[...])
-    sigmoid = 1.0 / (1.0 + jnp.exp(-gate_hidden))
-    silu = gate_hidden * sigmoid
-    hidden = (silu * up_hidden).astype(BRAIN_FLOAT_TYPE)
-    hid_ref[...] = hidden
-    d_hidden = dot_right_transposed(deo_ref[...], wd_ref[...])
-    d_gate = (d_hidden * up_hidden * sigmoid * (1.0 + gate_hidden * (1.0 - sigmoid))).astype(
-        BRAIN_FLOAT_TYPE
-    )
-    d_up = (d_hidden * silu).astype(BRAIN_FLOAT_TYPE)
-    dgl_ref[...] = d_gate
-    dul_ref[...] = d_up
-    expert_out = dot_rows(hidden, wd_ref[...]).astype(BRAIN_FLOAT_TYPE)
-    d_copy = (
-        dot_right_transposed(d_gate, wg_ref[...]) + dot_right_transposed(d_up, wu_ref[...])
-    ).astype(BRAIN_FLOAT_TYPE)
-    for s in range(sources):
-        rows = slice(s * capacity, (s + 1) * capacity)
-        pick = st_ref[s]
-        e_rows = expert_out[rows].astype(SINGLE_FLOAT)
-        gate = g_ref[rows, :]
-        d_gate_rows = jnp.sum(
-            d_ref[rows, :].astype(SINGLE_FLOAT) * e_rows, axis=-1, keepdims=True
-        )
-        high = d_gate_rows.astype(BRAIN_FLOAT_TYPE).astype(SINGLE_FLOAT)
-        extra = jnp.where(row_lane == e, high, 0.0) + jnp.where(
-            row_lane == experts + e, d_gate_rows - high, 0.0
-        )
-        outp_ref[s] = dot_rows(pick, (gate * e_rows).astype(BRAIN_FLOAT_TYPE)).astype(
-            BRAIN_FLOAT_TYPE
-        )
-        dp_ref[s, :, :width] = dot_rows(pick, d_copy[rows]).astype(BRAIN_FLOAT_TYPE)
-        dp_ref[s, :, width:] = dot_rows(pick, extra.astype(BRAIN_FLOAT_TYPE)).astype(
-            BRAIN_FLOAT_TYPE
-        )
-
-
-def expert_compute(capacity, step_sources, expert, pay, dout, wg, wu, wd):
-    sources, tokens, payload = pay.shape
-    width, ff = wg.shape
-    low = BRAIN_FLOAT_TYPE
-    rows = step_sources * capacity
-    total = sources * capacity
-    once = pl.Buffered(1)
-    grid_spec = pltpu.PrefetchScalarGridSpec(
-        num_scalar_prefetch=1,
-        grid=(sources // step_sources,),
-        in_specs=[
-            pl.BlockSpec((step_sources, tokens, payload), lambda i, e: (i, 0, 0)),
-            pl.BlockSpec((step_sources, tokens, width), lambda i, e: (i, 0, 0)),
-            pl.BlockSpec((width, ff), lambda i, e: (0, 0), pipeline_mode=once),
-            pl.BlockSpec((width, ff), lambda i, e: (0, 0), pipeline_mode=once),
-            pl.BlockSpec((ff, width), lambda i, e: (0, 0), pipeline_mode=once),
-        ],
-        out_specs=[
-            pl.BlockSpec((step_sources, tokens, width), lambda i, e: (i, 0, 0)),
-            pl.BlockSpec((step_sources, tokens, payload), lambda i, e: (i, 0, 0)),
-            pl.BlockSpec((rows, width), lambda i, e: (i, 0)),
-            pl.BlockSpec((rows, width), lambda i, e: (i, 0)),
-            pl.BlockSpec((rows, ff), lambda i, e: (i, 0)),
-            pl.BlockSpec((rows, ff), lambda i, e: (i, 0)),
-            pl.BlockSpec((rows, ff), lambda i, e: (i, 0)),
-        ],
-        scratch_shapes=[
-            pltpu.VMEM((rows, width), low),
-            pltpu.VMEM((rows, 1), SINGLE_FLOAT),
-            pltpu.VMEM((step_sources, tokens, capacity), low),
-        ],
-    )
-
-    def kernel(*refs):
-        expert_kernel(capacity, *refs)
-
-    return pl.pallas_call(
-        kernel,
-        grid_spec=grid_spec,
-        out_shape=(
-            jax.ShapeDtypeStruct((sources, tokens, width), low),
-            jax.ShapeDtypeStruct((sources, tokens, payload), low),
-            jax.ShapeDtypeStruct((total, width), low),
-            jax.ShapeDtypeStruct((total, width), low),
-            jax.ShapeDtypeStruct((total, ff), low),
-            jax.ShapeDtypeStruct((total, ff), low),
-            jax.ShapeDtypeStruct((total, ff), low),
-        ),
-        compiler_params=compiler_params(),
-        name="expert_compute",
-    )(expert, pay, dout, wg, wu, wd)
-
-
 MESH = pl.DeviceIdType.MESH
 ANYWHERE = pl.BlockSpec(memory_space=pl.ANY)
 LINE = 4
@@ -1171,18 +1039,19 @@
         add_blocks(out, block, up_ref.at[z], down_ref.at[z])
 
 
-def scatter_all_kernel(
-    part,
+def scatter_picked_kernel(
+    rows_in,
+    pick_in,
     out,
+    rows_ref,
+    pick_ref,
     own_ref,
-    sibling_ref,
     corner_ref,
     x_ref,
     y_ref,
     up_ref,
     down_ref,
     load_sems,
-    sibling_sems,
     corner_sems,
     x_sems,
     y_sems,
@@ -1193,47 +1062,32 @@
     z, y, x, k = place()
     order = line_order(z)
     along_x, along_y = device_at(z, y, 1 - x, k), device_at(z, 1 - y, x, k)
-    sibling = device_at(z, y, x, 1 - k)
-    meet(z, y, x, k, (along_x, along_y, sibling))
+    pick_load = pltpu.make_async_copy(pick_in, pick_ref, load_sems.at[16])
+    pick_load.start()
+    turn = [i * 4 + r for r in (3, 1, 2, 0) for i in (3, 2, 1, 0)]
+    loads = {j: pltpu.make_async_copy(rows_in.at[j], rows_ref.at[j], load_sems.at[j]) for j in turn}
+    for j in turn:
+        loads[j].start()
+    meet(z, y, x, k, (along_x, along_y))
     sends = Sends(send_sems)
-    home, on_x, on_y, corner = 0, 1, 2, 3
-    where = {home: (y, x), on_x: (y, 1 - x), on_y: (1 - y, x), corner: (1 - y, 1 - x)}
-    turn = [(i, corner) for i in (3, 2, 1, 0)]
-    for i in (3, 2, 1, 0):
-        turn += [(i, on_x), (i, on_y)]
-    turn += [(i, home) for i in (3, 2, 1, 0)]
-    loads = {}
-    for i, r in turn:
-        j = i * 4 + r
-        dy, dx = where[r]
-        sends.start(
-            part.at[slot_of(order[i], dy, dx, 1 - k)],
-            sibling_ref.at[j],
-            sibling_sems.at[j],
-            sibling,
-        )
-        loads[j] = pltpu.make_async_copy(
-            part.at[slot_of(order[i], dy, dx, k)], own_ref.at[j], load_sems.at[j]
-        )
-        loads[j].start()
+    pick_load.wait()
 
     def gather(i, r, *extra):
         j = i * 4 + r
         loads[j].wait()
-        arrived(sibling_ref.at[j], sibling_sems.at[j], sibling)
-        add_blocks(own_ref.at[j], own_ref.at[j], sibling_ref.at[j], *extra)
+        spread_rows(own_ref.at[j], pick_ref.at[j], rows_ref.at[j], *extra)
         return own_ref.at[j]
 
     for i in (3, 2, 1, 0):
         sends.start(
-            gather(i, corner), corner_ref.at[i], corner_sems.at[i], along_y if i < 2 else along_x
+            gather(i, 3), corner_ref.at[i], corner_sems.at[i], along_y if i < 2 else along_x
         )
 
     def cross(i):
         arrived(corner_ref.at[i], corner_sems.at[i], along_x)
         extra = (corner_ref.at[i],)
-        for_x = gather(i, on_x, *(extra if i < 2 else ()))
-        for_y = gather(i, on_y, *(extra if i >= 2 else ()))
+        for_x = gather(i, 1, *(extra if i < 2 else ()))
+        for_y = gather(i, 2, *(extra if i >= 2 else ()))
         sends.start(for_x, x_ref.at[i], x_sems.at[i], along_x)
         sends.start(for_y, y_ref.at[i], y_sems.at[i], along_y)
 
@@ -1242,32 +1096,34 @@
         arrived(y_ref.at[i], y_sems.at[i], along_y)
         if i > 0:
             cross(i - 1)
-        gather(i, home, x_ref.at[i], y_ref.at[i])
+        gather(i, 0, x_ref.at[i], y_ref.at[i])
 
     cross(3)
     scatter_line(
-        z, y, x, k, order, total, lambda i: own_ref.at[i * 4 + home],
+        z, y, x, k, order, total, lambda i: own_ref.at[i * 4],
         up_ref, down_ref, up_sems, down_sems, sends, out, lambda i: None,
     )
     sends.finish()
 
 
-def scatter_all(part, collective_id, dtype):
-    shape, low = part.shape[1:], part.dtype
+def scatter_picked(rows, pick, collective_id, dtype):
+    slots, width = rows.shape[1:]
+    tokens = pick.shape[2]
+    shape, low = (tokens, width), rows.dtype
     dma = pltpu.SemaphoreType.DMA
     return pl.pallas_call(
-        scatter_all_kernel,
+        scatter_picked_kernel,
         out_shape=jax.ShapeDtypeStruct(shape, dtype),
-        in_specs=[ANYWHERE],
+        in_specs=[ANYWHERE, ANYWHERE],
         out_specs=VMEM_WHOLE,
-        scratch_shapes=[pltpu.VMEM((n,) + shape, low) for n in (16, 16, 4, 4, 4, 4, 4)]
-        + [dma((n,)) for n in (16, 16, 4, 4, 4, 4, 4)]
-        + [dma((40,))],
+        scratch_shapes=[pltpu.VMEM(rows.shape, low), pltpu.VMEM(pick.shape, low)]
+        + [pltpu.VMEM((n,) + shape, low) for n in (16, 4, 4, 4, 4, 4)]
+        + [dma((n,)) for n in (17, 4, 4, 4, 4, 4, 24)],
         compiler_params=pltpu.CompilerParams(
             collective_id=collective_id, has_side_effects=True, vmem_limit_bytes=VMEM_BYTES
         ),
-        name="scatter_all",
-    )(part)
+        name="scatter_picked",
+    )(rows, pick)
 
 
 def halves(ref, z, y):
@@ -1673,6 +1529,427 @@
         ),
         name="scatter_end",
     )(part, gw, gwo, small)
+
+
+GROUPS = 8
+
+
+def order_at(z, i):
+    upper = z // 2
+    inner = (z % 2) * (1 - upper) + (1 - z % 2) * upper
+    along = i * (1 - inner) + inner * ((i + 1) % 3 + 2 * (i // 3))
+    return 3 * upper + (1 - 2 * upper) * along
+
+
+def group_blocks(g):
+    later = ((g + 1) // 4) * (1 - g // 7)
+    g = g * (1 - later) + later * (3 + g % 4)
+    kind, turn = (g + 2) // 4, (g + 2) % 4
+    far, side, near = 1 - (kind + 1) // 2, kind % 2, kind // 2
+    return (
+        (far * (turn - 2) + side * (3 - turn) + near * (3 - 2 * turn), 3 - 2 * kind + near),
+        (far * turn + side * (3 - turn) + near * (2 - 2 * turn), 3 - kind - near),
+    )
+
+
+def spread_rows(target, pick, rows, *terms):
+    step = 4 * HEAD_DIM
+    width = target.shape[1]
+    at = jnp.transpose(pick[...].astype(SINGLE_FLOAT)).astype(BRAIN_FLOAT_TYPE)
+    for start in range(0, width, step):
+        part = slice(start, min(start + step, width))
+        total = dot_rows(at, rows[:, part])
+        for term in terms:
+            total = total + term[:, part].astype(SINGLE_FLOAT)
+        target[:, part] = total.astype(target.dtype)
+
+
+def expert_exchange_kernel(
+    capacity,
+    pay_all,
+    dout_all,
+    wg_in,
+    wu_in,
+    wd_in,
+    back_ref,
+    rows_out,
+    pick_out,
+    x_out,
+    deo_out,
+    hid_out,
+    dgl_out,
+    dul_out,
+    wg_ref,
+    wu_ref,
+    wd_ref,
+    pay_ref,
+    dout_ref,
+    x_ref,
+    deo_ref,
+    hid_ref,
+    dgl_ref,
+    dul_ref,
+    d_ref,
+    g_ref,
+    far_pick_ref,
+    far_d_ref,
+    far_o_ref,
+    near_o_ref,
+    pick_ref,
+    rows_ref,
+    own_ref,
+    corner_ref,
+    x_sum_ref,
+    y_sum_ref,
+    up_ref,
+    down_ref,
+    weight_sems,
+    load_sems,
+    row_sems,
+    near_sems,
+    far_sems,
+    sibling_sems,
+    corner_sems,
+    x_sums,
+    y_sums,
+    up_sems,
+    down_sems,
+    sum_send_sems,
+    pick_sem,
+):
+    z, y, x, k = place()
+    order = line_order(z)
+    along_x, along_y = device_at(z, y, 1 - x, k), device_at(z, 1 - y, x, k)
+    sibling = device_at(z, y, x, 1 - k)
+    weights = [
+        pltpu.make_async_copy(a, b, weight_sems.at[n])
+        for n, (a, b) in enumerate(((wg_in, wg_ref), (wu_in, wu_ref), (wd_in, wd_ref)))
+    ]
+    for copy in weights:
+        copy.start()
+    meet(z, y, x, k, (along_x, along_y, sibling))
+    mine = slot_of(z, y, x, k)
+    width = wg_in.shape[0]
+    _, tokens, payload = pay_all.shape
+    experts = (payload - width) // 4
+    rows = 4 * capacity
+    above, below = device_at(z + 1, y, x, k), device_at(z - 1, y, x, k)
+
+    def far_copies(n, j):
+        half = pl.ds(capacity, capacity)
+        return [
+            remote(a, b, far_sems.at[n, m], sibling_sems.at[m, j], sibling)
+            for m, (a, b) in enumerate(
+                (
+                    (far_pick_ref.at[n], pick_ref.at[j, half, :]),
+                    (far_d_ref.at[n], rows_ref.at[j, half, :]),
+                    (far_o_ref.at[n], rows_out.at[j, half, :]),
+                )
+            )
+        ]
+
+    def gather(i, r, *extra):
+        j = i * 4 + r
+        for copy in far_copies(0, j)[:2]:
+            copy.wait_recv()
+        spread_rows(own_ref.at[j], pick_ref.at[j], rows_ref.at[j], *extra)
+        return own_ref.at[j]
+
+    def sum_send(n, j, target, recv, device):
+        return remote(own_ref.at[j], target, sum_send_sems.at[n], recv, device)
+
+    corner_sends = [
+        sum_send(i, i * 4 + 3, corner_ref.at[i], corner_sems.at[i], along_y if i < 2 else along_x)
+        for i in range(4)
+    ]
+    x_sends = [
+        sum_send(4 + i, i * 4 + 1, x_sum_ref.at[i], x_sums.at[i], along_x) for i in range(4)
+    ]
+    y_sends = [
+        sum_send(8 + i, i * 4 + 2, y_sum_ref.at[i], y_sums.at[i], along_y) for i in range(4)
+    ]
+    line_sends = []
+    for i in (1, 2, 3):
+        chip = order[i]
+        upward = chip > z
+        line_sends.append(
+            (upward, sum_send(12 + i, i * 4, up_ref.at[chip], up_sems.at[chip], above))
+        )
+        line_sends.append(
+            (
+                jnp.logical_not(upward),
+                sum_send(16 + i, i * 4, down_ref.at[chip], down_sems.at[chip], below),
+            )
+        )
+
+    def corners(*which):
+        for i in which:
+            gather(i, 3)
+            corner_sends[i].start()
+
+    def cross(i):
+        arrived(corner_ref.at[i], corner_sems.at[i], along_x)
+        extra = (corner_ref.at[i],)
+        gather(i, 1, *(extra if i < 2 else ()))
+        x_sends[i].start()
+        gather(i, 2, *(extra if i >= 2 else ()))
+        y_sends[i].start()
+
+    def total(i):
+        arrived(x_sum_ref.at[i], x_sums.at[i], along_x)
+        arrived(y_sum_ref.at[i], y_sums.at[i], along_y)
+        gather(i, 0, x_sum_ref.at[i], y_sum_ref.at[i])
+
+    def along(i):
+        total(i)
+        chip, block = order[i], own_ref.at[i * 4]
+        upward = chip > z
+
+        @pl.when(upward & (z > 0))
+        def _():
+            arrived(up_ref.at[chip], up_sems.at[chip], below)
+            add_blocks(block, block, up_ref.at[chip])
+
+        @pl.when(jnp.logical_not(upward) & (z < LINE - 1))
+        def _():
+            arrived(down_ref.at[chip], down_sems.at[chip], above)
+            add_blocks(block, block, down_ref.at[chip])
+
+        for condition, copy in line_sends[2 * i - 2 : 2 * i]:
+            pl.when(condition)(copy.start)
+
+    def sixth():
+        cross(1)
+        along(3)
+
+    def last():
+        cross(0)
+        along(2)
+
+    at_start = {5: lambda: cross(2), 6: sixth, 7: last}
+    at_middle = {1: lambda: corners(2, 0), 2: lambda: corners(3, 1), 3: lambda: cross(3)}
+
+    def at(g, table):
+        for n, work in table.items():
+            pl.when(g == n)(work)
+
+    for copy in weights:
+        copy.wait()
+    slot_row = lax.broadcasted_iota(jnp.int32, (capacity, tokens), 0).astype(SINGLE_FLOAT)
+    row_lane = lax.broadcasted_iota(jnp.int32, (capacity, payload - width), 1)
+    e = mine
+    is_gate = (row_lane == e) | (row_lane == experts + e)
+    rank_lane = (
+        lax.broadcasted_iota(jnp.int32, (8, payload - width), 1) == 2 * experts + e
+    ).astype(BRAIN_FLOAT_TYPE)
+
+    def row_copies(g):
+        out_rows = pl.ds(pl.multiple_of(g * rows, rows), rows)
+        pairs = (
+            (x_ref, x_out), (deo_ref, deo_out), (hid_ref, hid_out), (dgl_ref, dgl_out),
+            (dul_ref, dul_out),
+        )
+        return [
+            pltpu.make_async_copy(a, b.at[out_rows, :], row_sems.at[n])
+            for n, (a, b) in enumerate(pairs)
+        ]
+
+    def blocks_of(g):
+        found = []
+        for lane_k in (k, 1 - k):
+            for i, r in group_blocks(g):
+                dy, dx = r // 2, r % 2
+                slot = slot_of(
+                    order_at(z, i), y + dy * (1 - 2 * y), x + dx * (1 - 2 * x), lane_k
+                )
+                found.append((slot, i * 4 + r))
+        return found
+
+    def near_copies(g):
+        return [
+            pltpu.make_async_copy(
+                near_o_ref.at[n], rows_out.at[blocks_of(g)[n][1], pl.ds(0, capacity), :], near_sems.at[n]
+            )
+            for n in (0, 1)
+        ]
+
+    def settle(g):
+        for copy in row_copies(g) + near_copies(g):
+            copy.wait()
+        for n in (0, 1):
+            for copy in far_copies(n, blocks_of(g)[2 + n][1]):
+                copy.wait_send()
+
+    def load_copies(g):
+        return [
+            (
+                pltpu.make_async_copy(pay_all.at[slot], pay_ref.at[n], load_sems.at[n]),
+                pltpu.make_async_copy(dout_all.at[slot], dout_ref.at[n], load_sems.at[4 + n]),
+            )
+            for n, (slot, _) in enumerate(blocks_of(g))
+        ]
+
+    def load(g):
+        for pair in load_copies(g):
+            for copy in pair:
+                copy.start()
+
+    def step(g, carry):
+        blocks = blocks_of(g)
+        at(g, at_start)
+
+        @pl.when(g > 0)
+        def _():
+            settle(g - 1)
+
+        loads = load_copies(g)
+        for n in range(4):
+            for copy in loads[n]:
+                copy.wait()
+            part = slice(n * capacity, (n + 1) * capacity)
+            rank = dot_right_transposed(rank_lane, pay_ref[n, :, width:])
+            pick = (rank[0:1, :] == slot_row).astype(BRAIN_FLOAT_TYPE)
+            if n < 2:
+                pick_ref[blocks[n][1], 0:capacity, :] = pick
+            else:
+                far_pick_ref[n - 2] = pick
+            chosen = dot_rows(pick, pay_ref[n])
+            x_ref[part, :] = chosen[:, :width].astype(BRAIN_FLOAT_TYPE)
+            gate = jnp.sum(jnp.where(is_gate, chosen[:, width:], 0.0), axis=-1, keepdims=True)
+            g_ref[part, :] = gate
+            d_rows = dot_rows(pick, dout_ref[n])
+            d_ref[part, :] = d_rows.astype(BRAIN_FLOAT_TYPE)
+            deo_ref[part, :] = (gate * d_rows).astype(BRAIN_FLOAT_TYPE)
+
+        @pl.when(g < GROUPS - 1)
+        def _():
+            load(g + 1)
+
+        at(g, at_middle)
+        rows_in = x_ref[...]
+        gate_hidden = dot_rows(rows_in, wg_ref[...])
+        up_hidden = dot_rows(rows_in, wu_ref[...])
+        sigmoid = 1.0 / (1.0 + jnp.exp(-gate_hidden))
+        silu = gate_hidden * sigmoid
+        hidden = (silu * up_hidden).astype(BRAIN_FLOAT_TYPE)
+        hid_ref[...] = hidden
+        d_hidden = dot_right_transposed(deo_ref[...], wd_ref[...])
+        d_gate = (d_hidden * up_hidden * sigmoid * (1.0 + gate_hidden * (1.0 - sigmoid))).astype(
+            BRAIN_FLOAT_TYPE
+        )
+        d_up = (d_hidden * silu).astype(BRAIN_FLOAT_TYPE)
+        dgl_ref[...] = d_gate
+        dul_ref[...] = d_up
+        for copy in row_copies(g):
+            copy.start()
+        expert_out = dot_rows(hidden, wd_ref[...]).astype(BRAIN_FLOAT_TYPE)
+        d_copy = (
+            dot_right_transposed(d_gate, wg_ref[...]) + dot_right_transposed(d_up, wu_ref[...])
+        ).astype(BRAIN_FLOAT_TYPE)
+        for n in (2, 3, 0, 1):
+            j = blocks[n][1]
+            part = slice(n * capacity, (n + 1) * capacity)
+            e_rows = expert_out[part].astype(SINGLE_FLOAT)
+            d_gate_rows = jnp.sum(
+                d_ref[part, :].astype(SINGLE_FLOAT) * e_rows, axis=-1, keepdims=True
+            )
+            high = d_gate_rows.astype(BRAIN_FLOAT_TYPE).astype(SINGLE_FLOAT)
+            extra = jnp.where(row_lane == e, high, 0.0) + jnp.where(
+                row_lane == experts + e, d_gate_rows - high, 0.0
+            )
+            if n >= 2:
+                d_target, o_target = far_d_ref.at[n - 2], far_o_ref.at[n - 2]
+            else:
+                d_target, o_target = rows_ref.at[j, pl.ds(0, capacity), :], near_o_ref.at[n]
+            d_target[:, :width] = d_copy[part]
+            d_target[:, width:] = extra.astype(BRAIN_FLOAT_TYPE)
+            o_target[...] = (g_ref[part, :] * e_rows).astype(BRAIN_FLOAT_TYPE)
+            if n >= 2:
+                for copy in far_copies(n - 2, j):
+                    copy.start()
+        for copy in near_copies(g):
+            copy.start()
+        return carry
+
+    load(0)
+    lax.fori_loop(0, GROUPS, step, 0)
+    along(1)
+    total(0)
+    block = own_ref.at[0]
+
+    @pl.when(z > 0)
+    def _():
+        arrived(up_ref.at[z], up_sems.at[z], below)
+
+    @pl.when(z < LINE - 1)
+    def _():
+        arrived(down_ref.at[z], down_sems.at[z], above)
+
+    @pl.when(z == 0)
+    def _():
+        add_blocks(back_ref, block, down_ref.at[z])
+
+    @pl.when(z == LINE - 1)
+    def _():
+        add_blocks(back_ref, block, up_ref.at[z])
+
+    @pl.when((z > 0) & (z < LINE - 1))
+    def _():
+        add_blocks(back_ref, block, up_ref.at[z], down_ref.at[z])
+
+    settle(GROUPS - 1)
+    keep = pltpu.make_async_copy(pick_ref, pick_out, pick_sem)
+    keep.start()
+    for j in range(16):
+        far_copies(0, j)[2].wait_recv()
+    keep.wait()
+    for copy in corner_sends + x_sends + y_sends:
+        copy.wait_send()
+    for condition, copy in line_sends:
+        pl.when(condition)(copy.wait_send)
+
+
+def expert_exchange(capacity, pay_all, dout_all, wg, wu, wd, collective_id):
+    _, tokens, wide = pay_all.shape
+    width, ff = wg.shape
+    low = BRAIN_FLOAT_TYPE
+    rows = 4 * capacity
+    total = GROUPS * rows
+    dma, vmem = pltpu.SemaphoreType.DMA, pltpu.VMEM
+
+    def kernel(*refs):
+        expert_exchange_kernel(capacity, *refs)
+
+    shape = jax.ShapeDtypeStruct
+    return pl.pallas_call(
+        kernel,
+        out_shape=(
+            shape((tokens, wide), SINGLE_FLOAT),
+            shape((16, 2 * capacity, width), low),
+            shape((16, 2 * capacity, tokens), low),
+            shape((total, width), low),
+            shape((total, width), low),
+            shape((total, ff), low),
+            shape((total, ff), low),
+            shape((total, ff), low),
+        ),
+        in_specs=[ANYWHERE] * 5,
+        out_specs=[VMEM_WHOLE] + [ANYWHERE] * 7,
+        scratch_shapes=[vmem((width, ff), low), vmem((width, ff), low), vmem((ff, width), low)]
+        + [vmem((4, tokens, wide), low), vmem((4, tokens, width), low)]
+        + [vmem((rows, width), low), vmem((rows, width), low)]
+        + [vmem((rows, ff), low)] * 3
+        + [vmem((rows, width), low), vmem((rows, 1), SINGLE_FLOAT)]
+        + [vmem((2, capacity, n), low) for n in (tokens, wide, width, width)]
+        + [vmem((16, 2 * capacity, tokens), low), vmem((16, 2 * capacity, wide), low)]
+        + [vmem((n, tokens, wide), low) for n in (16, 4, 4, 4, 4, 4)]
+        + [dma((3,)), dma((8,)), dma((5,)), dma((2,)), dma((2, 3))]
+        + [dma((3, 16)), dma((4,)), dma((4,)), dma((4,)), dma((4,)), dma((4,)), dma((20,)), dma],
+        compiler_params=pltpu.CompilerParams(
+            collective_id=collective_id, has_side_effects=True, vmem_limit_bytes=VMEM_BYTES
+        ),
+        name="expert_exchange",
+    )(pay_all, dout_all, wg, wu, wd)
 
 
 def natural_order(blocks):
@@ -1777,6 +2054,7 @@
     own_segments = segment_ids(doc_lengths[0], own_places)
     validity = own_segments < doc_lengths.shape[1]
     d_layer = jnp.where(validity[:, None], grad_output[0], 0.0).astype(BRAIN_FLOAT_TYPE)
+    dout_all = gather_all(d_layer, 7)
 
     normed, raw, q, k, v, attn, part = attention_forward(
         slack, x_all, attn_gain[None, :], w_all, qg, kg, cosine, sine, segc, segr, wo_all
@@ -1803,12 +2081,10 @@
         [mixed, gate_high, gate_low, rank, jnp.zeros_like(rank)], axis=1
     )
     pay_all = gather_all(payload, 3)
-    dout_all = gather_all(d_layer, 7)
-    out_part, d_part, x_rows, d_rows, hidden, d_gate, d_up = expert_compute(
-        capacity, 4, me.astype(jnp.int32).reshape(1), pay_all, dout_all, expert_gate[0], expert_up[0], expert_down[0]
-    )
-    d_back = scatter_all(d_part, 4, SINGLE_FLOAT)
-    moe_sum = scatter_all(out_part, 8, SINGLE_FLOAT)
+    d_back, out_rows, out_pick, x_rows, d_rows, hidden, d_gate, d_up = expert_exchange(
+        capacity, pay_all, dout_all, expert_gate[0], expert_up[0], expert_down[0], 4
+    )
+    moe_sum = scatter_picked(out_rows, out_pick, 8, SINGLE_FLOAT)
     output = (hidden_state + moe_sum).astype(BRAIN_FLOAT_TYPE)
     grad_gate = dot_left_transposed(x_rows, d_gate)[None]
     grad_up = dot_left_transposed(x_rows, d_up)[None]

time: 773 us -> 747 us (0.966)
  Pallas kernels: 685 us -> 666 us
    pallas_call x3 -> x2, Pallas kernels: 231 us -> 200 us  [the longest x1 121 us: expert_exchange(): pl.pallas_call(kernel, out_shape=(shape((tokens, wide), SINGLE_FLOAT), sh...]
    pallas_call x2, Pallas kernels: 159 us -> 171 us  [gather_all(): pl.pallas_call(gather_all_kernel, out_shape=jax.ShapeDtypeStruct((32,) +...]
where the time goes in v3:
time: 747 us; the launch traced here: 744 us
  Pallas kernels  666 us (89%)
  local copies, waits for them, and re-layouts  29.4 us (4%)
  matrix products  29 us (4%)
  other arithmetic  18.3 us (2%)
    pallas_call x2, Pallas kernels, gather_all(): pl.pallas_call(gather_all_kernel, out_shape=jax.ShapeDtypeStruct((32,) +...  171 us
    pallas_call x1, Pallas kernels, expert_exchange(): pl.pallas_call(kernel, out_shape=(shape((tokens, wide), SINGLE_FLOAT), sh...  121 us
    pallas_call x1, Pallas kernels, scatter_picked(): pl.pallas_call(scatter_picked_kernel, out_shape=jax.ShapeDtypeStruct(shap...  79.7 us
    pallas_call x1, Pallas kernels, scatter_end(): pl.pallas_call(scatter_end_kernel, out_shape=(jax.ShapeDtypeStruct((rows,...  68.2 us
    pallas_call x1, Pallas kernels, gather_start(): pl.pallas_call(gather_start_kernel, out_shape=(jax.ShapeDtypeStruct((8 *...  61.6 us
    pallas_call x1, Pallas kernels, scatter_rows(): pl.pallas_call(scatter_rows_kernel, out_shape=jax.ShapeDtypeStruct((rows,...  59.8 us
    pallas_call x1, Pallas kernels, gather_rows(): pl.pallas_call(gather_rows_kernel, out_shape=jax.ShapeDtypeStruct((8 * ro...  46.6 us
    pallas_call x1, Pallas kernels, attention_backward(): pl.pallas_call(kernel, out_shape=shapes, in_specs=[VMEM_WHOLE] * 16, out_...  36.8 us

profile of v3, /device:TPU:8, one launch (start us, length us, event | category | flops | bytes accessed | tf_op | source)
XLA Modules:
  0.0 744.0 jit_solution(4576301537900004542)
XLA Ops:
  3.4 2.8 concatenate.64
  7.3 1.0 copy.63.refs_7_.refs_14_
  8.3 2.0 bitcast_select_fusion.source
  10.3 1.1 fusion.39
  11.6 1.9 fusion.10
  13.5 1.3 pad_maximum_fusion
  14.8 61.6 %gather_start.1 = (bf16[1024,2048]{1,0:T(8,128)(2,1)}, bf16[32,80,768]{2,1,0:T(8,128)(2,1)}, bf16[512,2048]{1,0:T(8,128)(2,1)}) custom-call(bf16[128,2048]{1,0:T(8,128)(2,1)} %bitcast.109, bf16[8,80,768]{2,1,0:T(8,128)(2,1)} %copy-done.4, bf16[128,2048]{1,0:T(8,128)(2,1)} %wo_in.1), custom_call_target="tpu_custom_call" | custom-call | tf_op jit(solution)/shard_map/gather_start/pallas_call | solution.py:1382
  76.4 1.2 slice.138
  77.6 3.9 slice.140
  84.4 22.0 %attention_forward.1 = (bf16[1024,2048]{1,0:T(8,128)(2,1)}, f32[1024,640]{1,0:T(8,128)}, bf16[1024,512]{1,0:T(8,128)(2,1)}, bf16[1024,128]{1,0:T(8,128)(2,1)}, b...) custom-call(bf16[1024,2048]{1,0:T(8,128)(2,1)} %get-tuple-element.41.refs_0_.refs_8_, ...), custom_call_target="tpu_custom_call" | custom-call | tf_op jit(solution)/shard_map/attention_forward/pallas_call | solution.py:643
  106.4 59.8 %scatter_rows.1 = f32[128,2048]{1,0:T(8,128)} custom-call(bf16[1024,2048]{1,0:T(8,128)(2,1)} %get-tuple-element.44.part), custom_call_target="tpu_custom_call" | custom-call | tf_op jit(solution)/shard_map/scatter_rows/pallas_call | solution.py:1276
  166.2 1.5 multiply_reduce_fusion.2
  169.6 88.1 %gather_all.3.refs_1_ = bf16[32,128,2048]{2,1,0:T(8,128)(2,1)} custom-call(bf16[128,2048]{1,0:T(8,128)(2,1)} %bitcast_select_fusion.source), custom_call_target="tpu_custom_call" | custom-call | tf_op jit(solution)/shard_map/gather_all/pallas_call | solution.py:966
  257.7 82.6 %gather_all.2.refs_0_ = bf16[32,128,2176]{2,1,0:T(8,128)(2,1)} custom-call(bf16[128,2176]{1,0:T(8,128)(2,1)} %concatenate.82.source), custom_call_target="tpu_custom_call" | custom-call | tf_op jit(solution)/shard_map/gather_all/pallas_call | solution.py:966
  340.4 120.5 %expert_exchange.1 = (f32[128,2176]{1,0:T(8,128)}, bf16[16,96,2048]{2,1,0:T(8,128)(2,1)}, bf16[16,96,128]{2,1,0:T(8,128)(2,1)}, bf16[1536,2048]{1,0:T(8,128)(2,1...) custom-call(bf16[32,128,2176]{2,1,0:T(8,128)(2,1)} %gather_all.2.ref, ...), custom_call_target="tpu_custom_call" | custom-call | tf_op jit(solution)/shard_map/expert_exchange/pallas_call | solution.py:1924
  460.9 79.7 %scatter_picked.1 = f32[128,2048]{1,0:T(8,128)} custom-call(bf16[16,96,2048]{2,1,0:T(8,128)(2,1)} %get-tuple-element.45.rows_in, bf16[16,96,128]{2,1,0:T(8,128)(2,1)} %get-tuple-element.46.pick_in), custom_call_target="tpu_custom_call" | custom-call | tf_op jit(solution)/shard_map/scatter_picked/pallas_call | solution.py:1114
  540.6 1.1 multiply_reduce_fusion.3
  541.8 2.3 fusion.46
  544.1 2.4 reshape.213
  546.5 2.0 multiply_reduce_fusion
  548.6 1.1 fusion.38.source
  549.7 46.6 %gather_rows.1.refs_0_ = bf16[1024,2048]{1,0:T(8,128)(2,1)} custom-call(bf16[128,2048]{1,0:T(8,128)(2,1)} %fusion.38.source), custom_call_target="tpu_custom_call" | custom-call | tf_op jit(solution)/shard_map/gather_rows/pallas_call | solution.py:1198
  596.3 36.8 %attention_backward.1 = (bf16[512,2048]{1,0:T(8,128)(2,1)}, bf16[2048,768]{1,0:T(8,128)(2,1)}, bf16[1024,2048]{1,0:T(8,128)(2,1)}, f32[1,2048]{1,0:T(1,128)}, f32[8,128]{1,0:T(8,128)}) custom-call(bf16[1024,2048]{1,0:T(8,128)(2,1)} %gather_rows.1.refs_0_, bf16[512,2048]{1,0:T(8,128)(2,1)} %get-tuple-element.43.refs_9_.refs_1_, ...), custom_call_target="tpu_custom_call" | custom-call | tf_op jit(solution)/shard_map/attention_backward/pallas_call | solution.py:796
  634.5 1.4 reduce.11
  636.1 1.1 concatenate.83
  638.2 68.2 %scatter_end.1 = (f32[128,2048]{1,0:T(8,128)}, bf16[8,64,768]{2,1,0:T(8,128)(2,1)}, f32[128,2048]{1,0:T(8,128)}, f32[32,128]{1,0:T(8,128)}) custom-call(bf16[1024,2048]{1,0:T(8,128)(2,1)} %get-tuple-element.54.part, bf16[8,2,2,64,768]{4,3,2,1,0:T(8,128)(2,1)} %bitcast.110, bf16[2,2,128,2048]{3,2,1,0:T(8,128)(2,1)} %bitcast.115, f32[8,2,2,32,128]{4,3,2,1,0:T(8,128)} %bitcast.116), custom_call_target="tpu_custom_call" | custom-call | tf_op jit(solution)/shard_map/scatter_end/pallas_call | solution.py:1511
  706.4 1.5 fusion.3
  708.0 3.4 fusion.7
  716.9 1.1 copy.77
  718.7 10.1 %convolution_bitcast_fusion.2 = f32[1,2048,768]{2,1,0:T(8,128)} fusion(bf16[1536,2048]{1,0:T(8,128)(2,1)} %get-tuple-element.63, bf16[1536,768]{1,0:T(8,128)(2,1)S(1)} %copy-done.10), kind=kOutput, calls=%fused_computation.2 | convolution fusion | flops 4831838208 | bytes 14942208 | tf_op jit(solution)/shard_map/dot_general | solution.py:514
  728.8 7.1 convolution_bitcast_fusion.1
  735.9 7.0 convolution_bitcast_fusion
  (98 shorter events, 18.4 us)
Async XLA Ops:
  1.7 11.8 %copy-start.6 = (s32[1024]{0:T(1024)}, s32[1024]{0:T(1024)S(1)}, u32[]{:S(2)}) copy-start(s32[1024]{0:T(1024)S(1)} %convert_reduce_fusion) | copy-start | bytes 12292
  11.6 3.2 copy-start.4
  84.4 83.5 %copy-start.2 = (bf16[2048,32]{1,0:T(8,128)(2,1)}, bf16[2048,32]{1,0:T(8,128)(2,1)S(1)}, u32[]{:S(2)}) copy-start(bf16[2048,32]{1,0:T(8,128)(2,1)S(1)} %reshape.208) | copy-start | bytes 393220
  106.4 59.8 %copy-start = (bf16[1,128,2048]{2,1,0:T(8,128)(2,1)S(1)}, bf16[1,128,2048]{2,1,0:T(8,128)(2,1)}, u32[]{:S(2)}) copy-start(bf16[1,128,2048]{2,1,0:T(8,128)(2,1)} %param.16) | copy-start | bytes 1572868
  540.6 7.9 %copy-start.1 = (bf16[1,128,2048]{2,1,0:T(8,128)(2,1)S(1)}, bf16[1,128,2048]{2,1,0:T(8,128)(2,1)}, u32[]{:S(2)}) copy-start(bf16[1,128,2048]{2,1,0:T(8,128)(2,1)} %param.17) | copy-start | bytes 1572868
  708.0 3.4 copy-start.7
  711.4 5.2 copy-start.3
  716.6 2.0 copy-start.10
  716.9 11.9 %slice-start.2 = ((s8[6291456]{0:T(1024)(128)(4,1)}), s8[4194304]{0:T(1024)(128)(4,1)S(1)}, s32[]{:S(2)}) async-start(s8[6291456]{0:T(1024)(128)(4,1)} %bitcast.134), calls=%async_computation.2 | async-start | bytes 8388608
  718.7 10.1 %slice-start.3 = ((s8[6291456]{0:T(1024)(128)(4,1)}), s8[2097152]{0:T(1024)(128)(4,1)S(1)}, s32[]{:S(2)}) async-start(s8[6291456]{0:T(1024)(128)(4,1)} %bitcast.134), calls=%async_computation.3 | async-start | bytes 4194304
  718.7 10.1 %copy-start.9 = (bf16[1536,768]{1,0:T(8,128)(2,1)S(1)}, bf16[1536,768]{1,0:T(8,128)(2,1)}, u32[]{:S(2)}) copy-start(bf16[1536,768]{1,0:T(8,128)(2,1)} %get-tuple-element.65) | copy-start | bytes 7077892
  718.7 17.2 %slice-start = ((s8[6291456]{0:T(1024)(128)(4,1)}), s8[4194304]{0:T(1024)(128)(4,1)S(1)}, s32[]{:S(2)}) async-start(s8[6291456]{0:T(1024)(128)(4,1)} %bitcast.132), calls=%async_computation | async-start | bytes 8388608
  728.8 7.1 slice-start.1
  728.8 7.1 copy-start.8
  735.9 7.0 copy-start.5

commit v4 on v3

--- a/solution.py
+++ b/solution.py
@@ -544,112 +544,6 @@
     return exponent * (1.0 / jnp.sum(exponent, axis=-1, keepdims=True))
 
 
-def attention_forward_kernel(
-    slack,
-    x_ref,
-    gain_ref,
-    w_ref,
-    qg_ref,
-    kg_ref,
-    cos_ref,
-    sin_ref,
-    segc_ref,
-    segr_ref,
-    wo_ref,
-    normed_ref,
-    raw_ref,
-    q_ref,
-    k_ref,
-    v_ref,
-    attn_ref,
-    part_ref,
-):
-    tokens = x_ref.shape[0]
-    heads = q_ref.shape[1] // HEAD_DIM
-    rows_step = 256
-
-    def project(i, carry):
-        rows = pl.ds(pl.multiple_of(i * rows_step, rows_step), rows_step)
-        x = x_ref[rows, :].astype(SINGLE_FLOAT)
-        inverse = lax.rsqrt(jnp.mean(x * x, axis=-1, keepdims=True) + EPS)
-        normed = (x * inverse * gain_ref[...]).astype(BRAIN_FLOAT_TYPE)
-        normed_ref[rows, :] = normed
-        raw = dot_rows(normed, w_ref[...])
-        raw_ref[rows, :] = raw[:, : (heads + 1) * HEAD_DIM]
-        v_ref[rows, :] = raw[:, (heads + 1) * HEAD_DIM :].astype(BRAIN_FLOAT_TYPE)
-        cosine, sine = cos_ref[rows, :], sin_ref[rows, :]
-        for h in range(heads + 1):
-            part = raw[:, h * HEAD_DIM : (h + 1) * HEAD_DIM]
-            gain = qg_ref[...] if h < heads else kg_ref[...]
-            scaled = (
-                part * lax.rsqrt(jnp.mean(part * part, axis=-1, keepdims=True) + EPS) * gain
-            )
-            turned = scaled * cosine + pltpu.roll(scaled, HEAD_DIM // 2, 1) * sine
-            turned = turned.astype(BRAIN_FLOAT_TYPE)
-            if h < heads:
-                q_ref[rows, h * HEAD_DIM : (h + 1) * HEAD_DIM] = turned
-            else:
-                k_ref[rows, :] = turned
-        return carry
-
-    lax.fori_loop(0, tokens // rows_step, project, 0)
-    tile_rows = 128
-    for tile in range(tokens // tile_rows):
-        first_row = tile * tile_rows
-        rows = slice(first_row, first_row + tile_rows)
-        low, high = key_range(tile, tile_rows, tokens, slack)
-        probs = tile_scores(
-            stacked_heads(q_ref, rows, heads),
-            k_ref,
-            segc_ref,
-            segr_ref,
-            low,
-            high,
-            first_row,
-            tile_rows,
-            heads,
-        )
-        attended = dot_rows(probs.astype(BRAIN_FLOAT_TYPE), v_ref[low:high, :])
-        for h in range(heads):
-            attn_ref[rows, h * HEAD_DIM : (h + 1) * HEAD_DIM] = attended[
-                h * tile_rows : (h + 1) * tile_rows
-            ].astype(BRAIN_FLOAT_TYPE)
-
-    def project_out(i, carry):
-        rows = pl.ds(pl.multiple_of(i * rows_step, rows_step), rows_step)
-        part_ref[rows, :] = dot_rows(attn_ref[rows, :], wo_ref[...]).astype(BRAIN_FLOAT_TYPE)
-        return carry
-
-    lax.fori_loop(0, tokens // rows_step, project_out, 0)
-
-
-def attention_forward(slack, x, gain, w, qg, kg, cosine, sine, segc, segr, wo):
-    tokens, width = x.shape
-    channels = w.shape[1] - 2 * HEAD_DIM
-    low = BRAIN_FLOAT_TYPE
-    shapes = (
-        jax.ShapeDtypeStruct((tokens, width), low),
-        jax.ShapeDtypeStruct((tokens, channels + HEAD_DIM), SINGLE_FLOAT),
-        jax.ShapeDtypeStruct((tokens, channels), low),
-        jax.ShapeDtypeStruct((tokens, HEAD_DIM), low),
-        jax.ShapeDtypeStruct((tokens, HEAD_DIM), low),
-        jax.ShapeDtypeStruct((tokens, channels), low),
-        jax.ShapeDtypeStruct((tokens, width), low),
-    )
-
-    def kernel(*refs):
-        attention_forward_kernel(slack, *refs)
-
-    return pl.pallas_call(
-        kernel,
-        out_shape=shapes,
-        in_specs=[VMEM_WHOLE] * 10,
-        out_specs=[VMEM_WHOLE] * 7,
-        compiler_params=compiler_params(),
-        name="attention_forward",
-    )(x, gain, w, qg, kg, cosine, sine, segc, segr, wo)
-
-
 def head_backward(turned_gradient, part, gain, cosine, sine):
     scaled_gradient = turned_gradient * cosine - (
         pltpu.roll(turned_gradient, HEAD_DIM // 2, 1) * sine
@@ -662,151 +556,6 @@
         unit_gradient - unit * jnp.mean(unit * unit_gradient, axis=-1, keepdims=True)
     )
     return raw_gradient, gain_gradient
-
-
-def attention_backward_kernel(
-    slack,
-    dh_ref,
-    wo_ref,
-    attn_ref,
-    q_ref,
-    k_ref,
-    v_ref,
-    raw_ref,
-    normed_ref,
-    x_ref,
-    w_ref,
-    qg_ref,
-    kg_ref,
-    cos_ref,
-    sin_ref,
-    segc_ref,
-    segr_ref,
-    gwo_ref,
-    gw_ref,
-    dpart_ref,
-    ggain_ref,
-    gheads_ref,
-    da_ref,
-    draw_ref,
-    dk_ref,
-    dv_ref,
-):
-    tokens = x_ref.shape[0]
-    heads = q_ref.shape[1] // HEAD_DIM
-    scale = HEAD_DIM ** (-0.5)
-    rows_step = 256
-
-    def attended_gradient(i, carry):
-        rows = pl.ds(pl.multiple_of(i * rows_step, rows_step), rows_step)
-        da_ref[rows, :] = dot_right_transposed(dh_ref[rows, :], wo_ref[...]).astype(
-            BRAIN_FLOAT_TYPE
-        )
-        return carry
-
-    lax.fori_loop(0, tokens // rows_step, attended_gradient, 0)
-
-    def out_weight(i, carry):
-        columns = pl.ds(pl.multiple_of(i * 512, 512), 512)
-        gwo_ref[:, columns] = dot_left_transposed(attn_ref[...], dh_ref[:, columns]).astype(
-            gwo_ref.dtype
-        )
-        return carry
-
-    lax.fori_loop(0, dh_ref.shape[1] // 512, out_weight, 0)
-    dk_ref[...] = jnp.zeros_like(dk_ref)
-    dv_ref[...] = jnp.zeros_like(dv_ref)
-    query_gain_gradient = jnp.zeros((1, HEAD_DIM), SINGLE_FLOAT)
-    tile_rows = 128
-    for tile in range(tokens // tile_rows):
-        first_row = tile * tile_rows
-        rows = slice(first_row, first_row + tile_rows)
-        low, high = key_range(tile, tile_rows, tokens, slack)
-        q4 = stacked_heads(q_ref, rows, heads)
-        da4 = stacked_heads(da_ref, rows, heads)
-        probs = tile_scores(
-            q4, k_ref, segc_ref, segr_ref, low, high, first_row, tile_rows, heads
-        )
-        d_probs = dot_right_transposed(da4, v_ref[low:high, :])
-        delta = jnp.sum(probs * d_probs, axis=-1, keepdims=True)
-        d_scores = (probs * (d_probs - delta)).astype(BRAIN_FLOAT_TYPE)
-        dq4 = dot_rows(d_scores, k_ref[low:high, :]) * scale
-        dk_ref[low:high, :] += dot_left_transposed(d_scores, q4)
-        dv_ref[low:high, :] += dot_left_transposed(probs.astype(BRAIN_FLOAT_TYPE), da4)
-        for h in range(heads):
-            columns = slice(h * HEAD_DIM, (h + 1) * HEAD_DIM)
-            raw_gradient, gain_gradient = head_backward(
-                dq4[h * tile_rows : (h + 1) * tile_rows],
-                raw_ref[rows, columns],
-                qg_ref[...],
-                cos_ref[rows, :],
-                sin_ref[rows, :],
-            )
-            draw_ref[rows, columns] = raw_gradient.astype(BRAIN_FLOAT_TYPE)
-            query_gain_gradient = query_gain_gradient + gain_gradient
-    key_columns = slice(heads * HEAD_DIM, (heads + 1) * HEAD_DIM)
-    raw_gradient, key_gain_gradient = head_backward(
-        dk_ref[...] * scale, raw_ref[:, key_columns], kg_ref[...], cos_ref[...], sin_ref[...]
-    )
-    draw_ref[:, key_columns] = raw_gradient.astype(BRAIN_FLOAT_TYPE)
-    draw_ref[:, (heads + 1) * HEAD_DIM :] = dv_ref[...].astype(BRAIN_FLOAT_TYPE)
-    gheads_ref[...] = jnp.concatenate(
-        [query_gain_gradient, key_gain_gradient, jnp.zeros((6, HEAD_DIM), SINGLE_FLOAT)], axis=0
-    )
-
-    def projection_weight(i, carry):
-        columns = pl.ds(pl.multiple_of(i * 256, 256), 256)
-        gw_ref[columns, :] = dot_left_transposed(normed_ref[:, columns], draw_ref[...]).astype(
-            gw_ref.dtype
-        )
-        return carry
-
-    lax.fori_loop(0, normed_ref.shape[1] // 256, projection_weight, 0)
-    ggain_ref[...] = jnp.zeros_like(ggain_ref)
-
-    def input_gradient(i, carry):
-        rows = pl.ds(pl.multiple_of(i * rows_step, rows_step), rows_step)
-        d_normed = dot_right_transposed(draw_ref[rows, :], w_ref[...])
-        dpart_ref[rows, :] = d_normed.astype(BRAIN_FLOAT_TYPE)
-        x = x_ref[rows, :].astype(SINGLE_FLOAT)
-        inverse = lax.rsqrt(jnp.mean(x * x, axis=-1, keepdims=True) + EPS)
-        ggain_ref[...] += jnp.sum(d_normed * (x * inverse), axis=0, keepdims=True)
-        return carry
-
-    lax.fori_loop(0, tokens // rows_step, input_gradient, 0)
-
-
-def attention_backward(
-    slack, dh, wo, attn, q, k, v, raw, normed, x, w, qg, kg, cosine, sine, segc, segr
-):
-    tokens, width = x.shape
-    channels = q.shape[1]
-    low = BRAIN_FLOAT_TYPE
-    shapes = (
-        jax.ShapeDtypeStruct((channels, width), low),
-        jax.ShapeDtypeStruct((width, channels + 2 * HEAD_DIM), low),
-        jax.ShapeDtypeStruct((tokens, width), low),
-        jax.ShapeDtypeStruct((1, width), SINGLE_FLOAT),
-        jax.ShapeDtypeStruct((8, HEAD_DIM), SINGLE_FLOAT),
-    )
-
-    def kernel(*refs):
-        attention_backward_kernel(slack, *refs)
-
-    return pl.pallas_call(
-        kernel,
-        out_shape=shapes,
-        in_specs=[VMEM_WHOLE] * 16,
-        out_specs=[VMEM_WHOLE] * 5,
-        scratch_shapes=[
-            pltpu.VMEM((tokens, channels), low),
-            pltpu.VMEM((tokens, channels + 2 * HEAD_DIM), low),
-            pltpu.VMEM((tokens, HEAD_DIM), SINGLE_FLOAT),
-            pltpu.VMEM((tokens, HEAD_DIM), SINGLE_FLOAT),
-        ],
-        compiler_params=compiler_params(),
-        name="attention_backward",
-    )(dh, wo, attn, q, k, v, raw, normed, x, w, qg, kg, cosine, sine, segc, segr)
 
 
 MESH = pl.DeviceIdType.MESH
@@ -897,69 +646,75 @@
     start(block, device_at(z - 1, y, x, k), down)
 
 
-def gather_all_kernel(source, out, local, send_sems, recv_sems):
-    z, y, x, k = place()
-    order = line_order(z)
-    along_x, along_y = device_at(z, y, 1 - x, k), device_at(z, 1 - y, x, k)
-    sibling = device_at(z, y, x, 1 - k)
-    meet(z, y, x, k, (along_x, along_y, sibling))
-    sends = Sends(send_sems)
-    mine = slot_of(z, y, x, k)
-    own = pltpu.make_async_copy(source, out.at[mine], local)
-    own.start()
-
-    def pass_on(slot, device, condition=None):
-        block = source if slot is mine else out.at[slot]
-        sends.start(block, out.at[slot], recv_sems.at[slot], device, condition)
-
-    def wait(slot):
-        arrived(out.at[slot], recv_sems.at[slot], along_x)
-
-    def column(i):
-        slot = mine if i == 0 else slot_of(order[i], y, x, k)
+class BlockGather:
+    def __init__(self, source, out, local, send_sems, recv_sems):
+        self.source, self.out, self.recv_sems = source, out, recv_sems
+        z, y, x, k = self.at = place()
+        self.order = line_order(z)
+        self.along_x, self.along_y = device_at(z, y, 1 - x, k), device_at(z, 1 - y, x, k)
+        self.sibling = device_at(z, y, x, 1 - k)
+        self.sends = Sends(send_sems)
+        self.mine = slot_of(z, y, x, k)
+        self.own = pltpu.make_async_copy(source, out.at[self.mine], local)
+
+    def pass_on(self, slot, device, condition=None):
+        block = self.source if slot is self.mine else self.out.at[slot]
+        self.sends.start(block, self.out.at[slot], self.recv_sems.at[slot], device, condition)
+
+    def wait(self, slot):
+        arrived(self.out.at[slot], self.recv_sems.at[slot], self.along_x)
+
+    def column(self, i):
+        z, y, x, k = self.at
+        slot = self.mine if i == 0 else slot_of(self.order[i], y, x, k)
         if i > 0:
-            wait(slot)
-        along_line(z, y, x, k, slot, i, order, pass_on)
-        pass_on(slot, along_x)
-        pass_on(slot, along_y)
-        pass_on(slot, sibling)
-
-    def from_x(i):
-        slot = slot_of(order[i], y, 1 - x, k)
-        wait(slot)
-        pass_on(slot, sibling)
-        if i == 3:
-            for j in (0, 1):
-                pass_on(slot_of(order[j], y, 1 - x, k), along_y)
-
-    def from_y(i):
-        slot = slot_of(order[i], 1 - y, x, k)
-        wait(slot)
-        pass_on(slot, sibling)
-        if i == 3:
-            for j in (2, 3):
-                pass_on(slot_of(order[j], 1 - y, x, k), along_x)
-
-    def from_corner(i):
-        slot = slot_of(order[i], 1 - y, 1 - x, k)
-        wait(slot)
-        pass_on(slot, sibling)
-
-    column(0)
+            self.wait(slot)
+        along_line(z, y, x, k, slot, i, self.order, self.pass_on)
+        for device in (self.along_x, self.along_y, self.sibling):
+            self.pass_on(slot, device)
+
+    def across(self, i, on_x, on_y):
+        z, y, x, k = self.at
+        return slot_of(self.order[i], 1 - y if on_y else y, 1 - x if on_x else x, k)
+
+    def receive(self, slot):
+        self.wait(slot)
+        self.pass_on(slot, self.sibling)
+
+    def begin(self):
+        meet(*self.at, (self.along_x, self.along_y, self.sibling))
+        self.own.start()
+        self.column(0)
+
+    def advance(self, i):
+        self.column(i)
+        self.receive(self.across(i - 1, True, False))
+        self.receive(self.across(i - 1, False, True))
+
+    def finish(self):
+        self.receive(self.across(3, True, False))
+        for j in (0, 1):
+            self.pass_on(self.across(j, True, False), self.along_y)
+        self.receive(self.across(3, False, True))
+        for j in (2, 3):
+            self.pass_on(self.across(j, False, True), self.along_x)
+        for i in range(4):
+            self.receive(self.across(i, True, True))
+        z, y, x, k = self.at
+        for i in range(4):
+            for dy in (y, 1 - y):
+                for dx in (x, 1 - x):
+                    self.wait(slot_of(self.order[i], dy, dx, 1 - k))
+        self.own.wait()
+        self.sends.finish()
+
+
+def gather_all_kernel(source, out, *semaphores):
+    blocks = BlockGather(source, out, *semaphores)
+    blocks.begin()
     for i in (1, 2, 3):
-        column(i)
-        from_x(i - 1)
-        from_y(i - 1)
-    from_x(3)
-    from_y(3)
-    for i in range(4):
-        from_corner(i)
-    for i in range(4):
-        for dy in (y, 1 - y):
-            for dx in (x, 1 - x):
-                wait(slot_of(order[i], dy, dx, 1 - k))
-    own.wait()
-    sends.finish()
+        blocks.advance(i)
+    blocks.finish()
 
 
 def gather_all(block, collective_id):
@@ -1039,91 +794,91 @@
         add_blocks(out, block, up_ref.at[z], down_ref.at[z])
 
 
-def scatter_picked_kernel(
-    rows_in,
-    pick_in,
-    out,
-    rows_ref,
-    pick_ref,
-    own_ref,
-    corner_ref,
-    x_ref,
-    y_ref,
-    up_ref,
-    down_ref,
-    load_sems,
-    corner_sems,
-    x_sems,
-    y_sems,
-    up_sems,
-    down_sems,
-    send_sems,
-):
-    z, y, x, k = place()
-    order = line_order(z)
-    along_x, along_y = device_at(z, y, 1 - x, k), device_at(z, 1 - y, x, k)
-    pick_load = pltpu.make_async_copy(pick_in, pick_ref, load_sems.at[16])
-    pick_load.start()
-    turn = [i * 4 + r for r in (3, 1, 2, 0) for i in (3, 2, 1, 0)]
-    loads = {j: pltpu.make_async_copy(rows_in.at[j], rows_ref.at[j], load_sems.at[j]) for j in turn}
-    for j in turn:
-        loads[j].start()
-    meet(z, y, x, k, (along_x, along_y))
-    sends = Sends(send_sems)
-    pick_load.wait()
-
-    def gather(i, r, *extra):
+class PickedSums:
+    def __init__(self, rows_in, pick_in, out, scratch):
+        (
+            self.rows_ref,
+            self.pick_ref,
+            self.own_ref,
+            self.corner_ref,
+            self.x_ref,
+            self.y_ref,
+            self.up_ref,
+            self.down_ref,
+            load_sems,
+            self.corner_sems,
+            self.x_sems,
+            self.y_sems,
+            self.up_sems,
+            self.down_sems,
+            send_sems,
+        ) = scratch
+        self.out = out
+        z, y, x, k = self.at = place()
+        self.order = line_order(z)
+        self.along_x, self.along_y = device_at(z, y, 1 - x, k), device_at(z, 1 - y, x, k)
+        self.pick_load = pltpu.make_async_copy(pick_in, self.pick_ref, load_sems.at[16])
+        self.turn = [i * 4 + r for r in (3, 1, 2, 0) for i in (3, 2, 1, 0)]
+        self.loads = {
+            j: pltpu.make_async_copy(rows_in.at[j], self.rows_ref.at[j], load_sems.at[j])
+            for j in self.turn
+        }
+        self.sends = Sends(send_sems)
+
+    def begin(self):
+        self.pick_load.start()
+        for j in self.turn:
+            self.loads[j].start()
+        meet(*self.at, (self.along_x, self.along_y))
+        self.pick_load.wait()
+
+    def gather(self, i, r, *extra):
         j = i * 4 + r
-        loads[j].wait()
-        spread_rows(own_ref.at[j], pick_ref.at[j], rows_ref.at[j], *extra)
-        return own_ref.at[j]
-
-    for i in (3, 2, 1, 0):
-        sends.start(
-            gather(i, 3), corner_ref.at[i], corner_sems.at[i], along_y if i < 2 else along_x
+        self.loads[j].wait()
+        block = self.own_ref.at[j]
+        spread_rows(block, self.pick_ref.at[j], self.rows_ref.at[j], *extra)
+        return block
+
+    def corners(self):
+        for i in (3, 2, 1, 0):
+            self.sends.start(
+                self.gather(i, 3),
+                self.corner_ref.at[i],
+                self.corner_sems.at[i],
+                self.along_y if i < 2 else self.along_x,
+            )
+
+    def cross(self, i):
+        arrived(self.corner_ref.at[i], self.corner_sems.at[i], self.along_x)
+        extra = (self.corner_ref.at[i],)
+        for_x = self.gather(i, 1, *(extra if i < 2 else ()))
+        self.sends.start(for_x, self.x_ref.at[i], self.x_sems.at[i], self.along_x)
+        for_y = self.gather(i, 2, *(extra if i >= 2 else ()))
+        self.sends.start(for_y, self.y_ref.at[i], self.y_sems.at[i], self.along_y)
+
+    def total(self, i):
+        arrived(self.x_ref.at[i], self.x_sems.at[i], self.along_x)
+        arrived(self.y_ref.at[i], self.y_sems.at[i], self.along_y)
+        if i > 0:
+            self.cross(i - 1)
+        self.gather(i, 0, self.x_ref.at[i], self.y_ref.at[i])
+
+    def finish(self, between=lambda i: None):
+        scatter_line(
+            *self.at, self.order, self.total, lambda i: self.own_ref.at[i * 4],
+            self.up_ref, self.down_ref, self.up_sems, self.down_sems, self.sends, self.out,
+            between,
         )
-
-    def cross(i):
-        arrived(corner_ref.at[i], corner_sems.at[i], along_x)
-        extra = (corner_ref.at[i],)
-        for_x = gather(i, 1, *(extra if i < 2 else ()))
-        for_y = gather(i, 2, *(extra if i >= 2 else ()))
-        sends.start(for_x, x_ref.at[i], x_sems.at[i], along_x)
-        sends.start(for_y, y_ref.at[i], y_sems.at[i], along_y)
-
-    def total(i):
-        arrived(x_ref.at[i], x_sems.at[i], along_x)
-        arrived(y_ref.at[i], y_sems.at[i], along_y)
-        if i > 0:
-            cross(i - 1)
-        gather(i, 0, x_ref.at[i], y_ref.at[i])
-
-    cross(3)
-    scatter_line(
-        z, y, x, k, order, total, lambda i: own_ref.at[i * 4],
-        up_ref, down_ref, up_sems, down_sems, sends, out, lambda i: None,
-    )
-    sends.finish()
-
-
-def scatter_picked(rows, pick, collective_id, dtype):
-    slots, width = rows.shape[1:]
-    tokens = pick.shape[2]
-    shape, low = (tokens, width), rows.dtype
-    dma = pltpu.SemaphoreType.DMA
-    return pl.pallas_call(
-        scatter_picked_kernel,
-        out_shape=jax.ShapeDtypeStruct(shape, dtype),
-        in_specs=[ANYWHERE, ANYWHERE],
-        out_specs=VMEM_WHOLE,
-        scratch_shapes=[pltpu.VMEM(rows.shape, low), pltpu.VMEM(pick.shape, low)]
+        self.sends.finish()
+
+
+def picked_scratch(rows, pick):
+    shape, low = (pick.shape[2], rows.shape[2]), rows.dtype
+    return (
+        [pltpu.VMEM(rows.shape, low), pltpu.VMEM(pick.shape, low)]
         + [pltpu.VMEM((n,) + shape, low) for n in (16, 4, 4, 4, 4, 4)]
-        + [dma((n,)) for n in (17, 4, 4, 4, 4, 4, 24)],
-        compiler_params=pltpu.CompilerParams(
-            collective_id=collective_id, has_side_effects=True, vmem_limit_bytes=VMEM_BYTES
-        ),
-        name="scatter_picked",
-    )(rows, pick)
+        + [pltpu.SemaphoreType.DMA((n,)) for n in (17, 4, 4, 4, 4, 4, 24)]
+    )
 
 
 def halves(ref, z, y):
@@ -1529,6 +1284,180 @@
         ),
         name="scatter_end",
     )(part, gw, gwo, small)
+
+
+def forward_gather_kernel(
+    slack,
+    block_in,
+    x_in,
+    slabs_in,
+    wo_in,
+    gain_ref,
+    qg_ref,
+    kg_ref,
+    cos_ref,
+    sin_ref,
+    segc_ref,
+    segr_ref,
+    block_out,
+    normed_out,
+    raw_out,
+    q_out,
+    k_out,
+    v_out,
+    attn_out,
+    part_out,
+    *scratch,
+):
+    (
+        x_ref,
+        w_ref,
+        wo_ref,
+        normed_ref,
+        raw_ref,
+        q_ref,
+        k_ref,
+        v_ref,
+        attn_ref,
+        part_ref,
+        in_sems,
+        out_sems,
+    ) = scratch[:12]
+    tokens, width = x_ref.shape
+    heads = q_ref.shape[1] // HEAD_DIM
+    owned, columns = w_ref.shape[1:]
+    rows_step = 256
+    copies = [
+        pltpu.make_async_copy(s, t, in_sems.at[n])
+        for n, (s, t) in enumerate(
+            ((x_in, x_ref), (slabs_in.at[:, pl.ds(0, owned), :], w_ref), (wo_in, wo_ref))
+        )
+    ]
+    stores = [
+        pltpu.make_async_copy(s, t, out_sems.at[n])
+        for n, (s, t) in enumerate(
+            (
+                (normed_ref, normed_out),
+                (raw_ref, raw_out),
+                (q_ref, q_out),
+                (k_ref, k_out),
+                (v_ref, v_out),
+                (attn_ref, attn_out),
+                (part_ref, part_out),
+            )
+        )
+    ]
+    for copy in copies:
+        copy.start()
+    blocks = BlockGather(block_in, block_out, *scratch[12:])
+    blocks.begin()
+    copies[0].wait()
+    copies[1].wait()
+
+    def project(i, carry):
+        rows = pl.ds(pl.multiple_of(i * rows_step, rows_step), rows_step)
+        x = x_ref[rows, :].astype(SINGLE_FLOAT)
+        inverse = lax.rsqrt(jnp.mean(x * x, axis=-1, keepdims=True) + EPS)
+        normed = (x * inverse * gain_ref[...]).astype(BRAIN_FLOAT_TYPE)
+        normed_ref[rows, :] = normed
+        raw = dot_rows(normed, w_ref[...].reshape(width, columns))
+        raw_ref[rows, :] = raw[:, : (heads + 1) * HEAD_DIM]
+        v_ref[rows, :] = raw[:, (heads + 1) * HEAD_DIM :].astype(BRAIN_FLOAT_TYPE)
+        cosine, sine = cos_ref[rows, :], sin_ref[rows, :]
+        for h in range(heads + 1):
+            part = raw[:, h * HEAD_DIM : (h + 1) * HEAD_DIM]
+            gain = qg_ref[...] if h < heads else kg_ref[...]
+            scaled = (
+                part * lax.rsqrt(jnp.mean(part * part, axis=-1, keepdims=True) + EPS) * gain
+            )
+            turned = scaled * cosine + pltpu.roll(scaled, HEAD_DIM // 2, 1) * sine
+            turned = turned.astype(BRAIN_FLOAT_TYPE)
+            if h < heads:
+                q_ref[rows, h * HEAD_DIM : (h + 1) * HEAD_DIM] = turned
+            else:
+                k_ref[rows, :] = turned
+        return carry
+
+    lax.fori_loop(0, tokens // rows_step, project, 0)
+    for copy in stores[:5]:
+        copy.start()
+    blocks.advance(1)
+    tile_rows = 128
+    for tile in range(tokens // tile_rows):
+        first_row = tile * tile_rows
+        rows = slice(first_row, first_row + tile_rows)
+        low, high = key_range(tile, tile_rows, tokens, slack)
+        probs = tile_scores(
+            stacked_heads(q_ref, rows, heads),
+            k_ref,
+            segc_ref,
+            segr_ref,
+            low,
+            high,
+            first_row,
+            tile_rows,
+            heads,
+        )
+        attended = dot_rows(probs.astype(BRAIN_FLOAT_TYPE), v_ref[low:high, :])
+        for h in range(heads):
+            attn_ref[rows, h * HEAD_DIM : (h + 1) * HEAD_DIM] = attended[
+                h * tile_rows : (h + 1) * tile_rows
+            ].astype(BRAIN_FLOAT_TYPE)
+    stores[5].start()
+    blocks.advance(2)
+    copies[2].wait()
+
+    def project_out(i, carry):
+        rows = pl.ds(pl.multiple_of(i * rows_step, rows_step), rows_step)
+        part_ref[rows, :] = dot_rows(attn_ref[rows, :], wo_ref[...]).astype(BRAIN_FLOAT_TYPE)
+        return carry
+
+    lax.fori_loop(0, tokens // rows_step, project_out, 0)
+    stores[6].start()
+    blocks.advance(3)
+    blocks.finish()
+    for copy in stores:
+        copy.wait()
+
+
+def forward_gather(slack, block, x, slabs, wo, gain, qg, kg, cosine, sine, segc, segr, collective_id):
+    tokens, width = x.shape
+    columns = slabs.shape[2]
+    owned = width // slabs.shape[0]
+    channels = columns - 2 * HEAD_DIM
+    low = BRAIN_FLOAT_TYPE
+    shape, vmem, dma = jax.ShapeDtypeStruct, pltpu.VMEM, pltpu.SemaphoreType.DMA
+    sizes = (
+        ((tokens, width), low),
+        ((tokens, channels + HEAD_DIM), SINGLE_FLOAT),
+        ((tokens, channels), low),
+        ((tokens, HEAD_DIM), low),
+        ((tokens, HEAD_DIM), low),
+        ((tokens, channels), low),
+        ((tokens, width), low),
+    )
+
+    def kernel(*refs):
+        forward_gather_kernel(slack, *refs)
+
+    return pl.pallas_call(
+        kernel,
+        out_shape=[shape((32,) + block.shape, low)] + [shape(*size) for size in sizes],
+        in_specs=[ANYWHERE] * 4 + [VMEM_WHOLE] * 7,
+        out_specs=[ANYWHERE] * 8,
+        scratch_shapes=[
+            vmem((tokens, width), low),
+            vmem((slabs.shape[0], owned, columns), low),
+            vmem(wo.shape, low),
+        ]
+        + [vmem(*size) for size in sizes]
+        + [dma((3,)), dma((7,))]
+        + [dma, dma((40,)), dma((32,))],
+        compiler_params=pltpu.CompilerParams(
+            collective_id=collective_id, has_side_effects=True, vmem_limit_bytes=VMEM_BYTES
+        ),
+        name="forward_gather",
+    )(block, x, slabs, wo, gain, qg, kg, cosine, sine, segc, segr)
 
 
 GROUPS = 8
@@ -1952,6 +1881,272 @@
     )(pay_all, dout_all, wg, wu, wd)
 
 
+def backward_scatter_kernel(
+    slack,
+    rows_in,
+    pick_in,
+    dh_in,
+    wo_in,
+    attn_in,
+    q_in,
+    k_in,
+    v_in,
+    raw_in,
+    normed_in,
+    x_in,
+    w_in,
+    qg_ref,
+    kg_ref,
+    cos_ref,
+    sin_ref,
+    segc_ref,
+    segr_ref,
+    out,
+    gwo_out,
+    gw_out,
+    dpart_out,
+    ggain_ref,
+    gheads_ref,
+    *scratch,
+):
+    (
+        dh_ref,
+        wo_ref,
+        attn_ref,
+        q_ref,
+        k_ref,
+        v_ref,
+        raw_ref,
+        normed_ref,
+        w_ref,
+        x_ref,
+        gwo_ref,
+        gw_ref,
+        da_ref,
+        draw_ref,
+        dk_ref,
+        dv_ref,
+        in_sems,
+        x_load_sems,
+        gwo_sems,
+        gw_sems,
+        dpart_sems,
+    ) = scratch[:21]
+    exchange = PickedSums(rows_in, pick_in, out, scratch[21:])
+    owned, columns = w_ref.shape[1:]
+    w_rows = w_in.at[:, pl.ds(0, owned), :]
+    inputs = (dh_in, wo_in, attn_in, q_in, k_in, v_in, raw_in, normed_in, w_rows)
+    held = (dh_ref, wo_ref, attn_ref, q_ref, k_ref, v_ref, raw_ref, normed_ref, w_ref)
+    copies = [pltpu.make_async_copy(s, t, in_sems.at[n]) for n, (s, t) in enumerate(zip(inputs, held))]
+    tokens = dh_ref.shape[0]
+    heads = q_ref.shape[1] // HEAD_DIM
+    scale = HEAD_DIM ** (-0.5)
+    rows_step = 256
+    row_steps = tokens // rows_step
+
+    def x_load(i):
+        rows = pl.ds(pl.multiple_of(i * rows_step, rows_step), rows_step)
+        return pltpu.make_async_copy(x_in.at[rows, :], x_ref.at[i % 2], x_load_sems.at[i % 2])
+
+    def dpart_store(i):
+        rows = pl.ds(pl.multiple_of(i * rows_step, rows_step), rows_step)
+        return pltpu.make_async_copy(dh_ref.at[rows, :], dpart_out.at[rows, :], dpart_sems.at[i])
+
+    def gwo_store(i):
+        columns = pl.ds(pl.multiple_of(i * 512, 512), 512)
+        return pltpu.make_async_copy(
+            gwo_ref.at[i % 2], gwo_out.at[:, columns], gwo_sems.at[i % 2]
+        )
+
+    def gw_store(i):
+        part = pl.ds(pl.multiple_of(i * 256, 256), 256)
+        return pltpu.make_async_copy(gw_ref.at[i % 2], gw_out.at[part, :], gw_sems.at[i % 2])
+
+    def attended_gradient():
+        def body(i, carry):
+            rows = pl.ds(pl.multiple_of(i * rows_step, rows_step), rows_step)
+            da_ref[rows, :] = dot_right_transposed(dh_ref[rows, :], wo_ref[...]).astype(
+                BRAIN_FLOAT_TYPE
+            )
+            return carry
+
+        for copy in copies[:2]:
+            copy.wait()
+        lax.fori_loop(0, row_steps, body, 0)
+
+    def out_weight():
+        copies[2].wait()
+        for i in range(dh_ref.shape[1] // 512):
+            if i >= 2:
+                gwo_store(i - 2).wait()
+            gwo_ref[i % 2] = dot_left_transposed(
+                attn_ref[...], dh_ref[:, i * 512 : (i + 1) * 512]
+            ).astype(gwo_ref.dtype)
+            gwo_store(i).start()
+
+    tile_rows = 128
+    gains = []
+
+    def tiles(first, last):
+        for tile in range(first, last):
+            first_row = tile * tile_rows
+            rows = slice(first_row, first_row + tile_rows)
+            low, high = key_range(tile, tile_rows, tokens, slack)
+            q4 = stacked_heads(q_ref, rows, heads)
+            da4 = stacked_heads(da_ref, rows, heads)
+            probs = tile_scores(
+                q4, k_ref, segc_ref, segr_ref, low, high, first_row, tile_rows, heads
+            )
+            d_probs = dot_right_transposed(da4, v_ref[low:high, :])
+            delta = jnp.sum(probs * d_probs, axis=-1, keepdims=True)
+            d_scores = (probs * (d_probs - delta)).astype(BRAIN_FLOAT_TYPE)
+            dq4 = dot_rows(d_scores, k_ref[low:high, :]) * scale
+            dk_ref[low:high, :] += dot_left_transposed(d_scores, q4)
+            dv_ref[low:high, :] += dot_left_transposed(probs.astype(BRAIN_FLOAT_TYPE), da4)
+            for h in range(heads):
+                columns = slice(h * HEAD_DIM, (h + 1) * HEAD_DIM)
+                raw_gradient, gain_gradient = head_backward(
+                    dq4[h * tile_rows : (h + 1) * tile_rows],
+                    raw_ref[rows, columns],
+                    qg_ref[...],
+                    cos_ref[rows, :],
+                    sin_ref[rows, :],
+                )
+                draw_ref[rows, columns] = raw_gradient.astype(BRAIN_FLOAT_TYPE)
+                gains.append(gain_gradient)
+
+    def keys():
+        columns = slice(heads * HEAD_DIM, (heads + 1) * HEAD_DIM)
+        raw_gradient, key_gain_gradient = head_backward(
+            dk_ref[...] * scale, raw_ref[:, columns], kg_ref[...], cos_ref[...], sin_ref[...]
+        )
+        draw_ref[:, columns] = raw_gradient.astype(BRAIN_FLOAT_TYPE)
+        draw_ref[:, (heads + 1) * HEAD_DIM :] = dv_ref[...].astype(BRAIN_FLOAT_TYPE)
+        query_gain_gradient = gains[0]
+        for gain in gains[1:]:
+            query_gain_gradient = query_gain_gradient + gain
+        gheads_ref[...] = jnp.concatenate(
+            [query_gain_gradient, key_gain_gradient, jnp.zeros((6, HEAD_DIM), SINGLE_FLOAT)],
+            axis=0,
+        )
+
+    def projection_weight():
+        copies[7].wait()
+        count = normed_ref.shape[1] // 256
+        for i in range(count):
+            if i >= 2:
+                gw_store(i - 2).wait()
+            gw_ref[i % 2] = dot_left_transposed(
+                normed_ref[:, i * 256 : (i + 1) * 256], draw_ref[...]
+            ).astype(gw_ref.dtype)
+            gw_store(i).start()
+
+    def input_gradient():
+        copies[8].wait()
+        ggain_ref[...] = jnp.zeros_like(ggain_ref)
+        for i in range(row_steps):
+            x_load(i).wait()
+            rows = slice(i * rows_step, (i + 1) * rows_step)
+            d_normed = dot_right_transposed(
+                draw_ref[rows, :], w_ref[...].reshape(normed_ref.shape[1], columns)
+            )
+            dh_ref[rows, :] = d_normed.astype(BRAIN_FLOAT_TYPE)
+            dpart_store(i).start()
+            x = x_ref[i % 2].astype(SINGLE_FLOAT)
+            inverse = lax.rsqrt(jnp.mean(x * x, axis=-1, keepdims=True) + EPS)
+            ggain_ref[...] += jnp.sum(d_normed * (x * inverse), axis=0, keepdims=True)
+            if i + 2 < row_steps:
+                x_load(i + 2).start()
+
+    exchange.begin()
+    for copy in copies:
+        copy.start()
+    x_load(0).start()
+    x_load(1).start()
+    dk_ref[...] = jnp.zeros_like(dk_ref)
+    dv_ref[...] = jnp.zeros_like(dv_ref)
+    exchange.corners()
+    attended_gradient()
+    out_weight()
+    for copy in copies[3:7]:
+        copy.wait()
+    tiles(0, 5)
+    exchange.cross(3)
+    tiles(5, 8)
+    keys()
+
+    def between(i):
+        if i == 3:
+            projection_weight()
+        elif i == 2:
+            input_gradient()
+
+    exchange.finish(between)
+    for i in (2, 3):
+        gwo_store(i).wait()
+    for i in (6, 7):
+        gw_store(i).wait()
+    for i in range(row_steps):
+        dpart_store(i).wait()
+
+
+def backward_scatter(
+    slack, rows, pick, dh, wo, attn, q, k, v, raw, normed, x, w, qg, kg, cosine, sine, segc, segr,
+    collective_id,
+):
+    tokens, width = x.shape
+    channels = q.shape[1]
+    columns = channels + 2 * HEAD_DIM
+    low = BRAIN_FLOAT_TYPE
+    shape, vmem, dma = jax.ShapeDtypeStruct, pltpu.VMEM, pltpu.SemaphoreType.DMA
+    shapes = (
+        shape((pick.shape[2], width), SINGLE_FLOAT),
+        shape((channels, width), low),
+        shape((width, columns), low),
+        shape((tokens, width), low),
+        shape((1, width), SINGLE_FLOAT),
+        shape((8, HEAD_DIM), SINGLE_FLOAT),
+    )
+
+    def kernel(*refs):
+        backward_scatter_kernel(slack, *refs)
+
+    return pl.pallas_call(
+        kernel,
+        out_shape=shapes,
+        in_specs=[ANYWHERE] * 12 + [VMEM_WHOLE] * 6,
+        out_specs=[VMEM_WHOLE] + [ANYWHERE] * 3 + [VMEM_WHOLE] * 2,
+        scratch_shapes=[
+            vmem((tokens, width), low),
+            vmem((channels, width), low),
+            vmem((tokens, channels), low),
+            vmem((tokens, channels), low),
+            vmem((tokens, HEAD_DIM), low),
+            vmem((tokens, HEAD_DIM), low),
+            vmem((tokens, channels + HEAD_DIM), SINGLE_FLOAT),
+            vmem((tokens, width), low),
+            vmem((w.shape[0], width // w.shape[0], columns), low),
+            vmem((2, 256, width), low),
+            vmem((2, channels, 512), low),
+            vmem((2, 256, columns), low),
+            vmem((tokens, channels), low),
+            vmem((tokens, columns), low),
+            vmem((tokens, HEAD_DIM), SINGLE_FLOAT),
+            vmem((tokens, HEAD_DIM), SINGLE_FLOAT),
+            dma((9,)),
+            dma((2,)),
+            dma((2,)),
+            dma((2,)),
+            dma((4,)),
+        ]
+        + picked_scratch(rows, pick),
+        compiler_params=pltpu.CompilerParams(
+            collective_id=collective_id, has_side_effects=True, vmem_limit_bytes=VMEM_BYTES
+        ),
+        name="backward_scatter",
+    )(rows, pick, dh, wo, attn, q, k, v, raw, normed, x, w, qg, kg, cosine, sine, segc, segr)
+
+
 def natural_order(blocks):
     count, rows, width = blocks.shape
     half = rows // 2
@@ -2025,7 +2220,6 @@
         slabs.append(jnp.concatenate([slab, small], axis=0))
     owned, few = width // device_count, query_norm.shape[0]
     x_all, slabs, wo_all = gather_start(inputs[0], jnp.stack(slabs), w_out, 1)
-    w_all = slabs[:, :owned].reshape(width, columns)
     small = slabs[:, owned:].reshape(device_count, 16 * columns)
     attn_gain = small[:, :owned].reshape(width).astype(SINGLE_FLOAT)
     ffn_gain = small[:, owned : 2 * owned].reshape(width).astype(SINGLE_FLOAT)
@@ -2054,10 +2248,9 @@
     own_segments = segment_ids(doc_lengths[0], own_places)
     validity = own_segments < doc_lengths.shape[1]
     d_layer = jnp.where(validity[:, None], grad_output[0], 0.0).astype(BRAIN_FLOAT_TYPE)
-    dout_all = gather_all(d_layer, 7)
-
-    normed, raw, q, k, v, attn, part = attention_forward(
-        slack, x_all, attn_gain[None, :], w_all, qg, kg, cosine, sine, segc, segr, wo_all
+
+    dout_all, normed, raw, q, k, v, attn, part = forward_gather(
+        slack, d_layer, x_all, slabs, wo_all, attn_gain[None, :], qg, kg, cosine, sine, segc, segr, 7
     )
     branch = scatter_rows(part, 2)
     layer_in = inputs[0].astype(SINGLE_FLOAT)
@@ -2084,8 +2277,6 @@
     d_back, out_rows, out_pick, x_rows, d_rows, hidden, d_gate, d_up = expert_exchange(
         capacity, pay_all, dout_all, expert_gate[0], expert_up[0], expert_down[0], 4
     )
-    moe_sum = scatter_picked(out_rows, out_pick, 8, SINGLE_FLOAT)
-    output = (hidden_state + moe_sum).astype(BRAIN_FLOAT_TYPE)
     grad_gate = dot_left_transposed(x_rows, d_gate)[None]
     grad_up = dot_left_transposed(x_rows, d_up)[None]
     grad_down = dot_left_transposed(hidden, d_rows)[None]
@@ -2102,9 +2293,10 @@
     d_state = d_layer.astype(SINGLE_FLOAT) + d_state_norm
     d_state_low = d_state.astype(BRAIN_FLOAT_TYPE)
     dh_all = gather_rows(d_state_low, 5)
-    gwo, gw, dpart, ggain, gheads = attention_backward(
-        slack, dh_all, wo_all, attn, q, k, v, raw, normed, x_all, w_all, qg, kg, cosine, sine, segc, segr
-    )
+    moe_sum, gwo, gw, dpart, ggain, gheads = backward_scatter(
+        slack, out_rows, out_pick, dh_all, wo_all, attn, q, k, v, raw, normed, x_all, slabs, qg, kg, cosine, sine, segc, segr, 8
+    )
+    output = (hidden_state + moe_sum).astype(BRAIN_FLOAT_TYPE)
     blocks = (ctx_count, ws_count // 2, 2)
     small = jnp.concatenate(
         [

time: 747 us -> 687 us (0.920)
  Pallas kernels: 666 us -> 603 us
    pallas_call x2 -> x1, Pallas kernels: 171 us -> 79.5 us  [gather_all(): pl.pallas_call(gather_all_kernel, out_shape=jax.ShapeDtypeStruct((32,) +...]
    pallas_call x3 -> x2, Pallas kernels: 139 us -> 168 us  [the longest x1 86 us: forward_gather(): pl.pallas_call(kernel, out_shape=[shape((32,) + block.shape, low)] + [sha...]
where the time goes in v4:
time: 687 us; the launch traced here: 678 us
  Pallas kernels  603 us (88%)
  matrix products  29 us (4%)
  local copies, waits for them, and re-layouts  25.5 us (4%)
  other arithmetic  18.3 us (3%)
    pallas_call x1, Pallas kernels, expert_exchange(): pl.pallas_call(kernel, out_shape=(shape((tokens, wide), SINGLE_FLOAT), sh...  122 us
    pallas_call x1, Pallas kernels, forward_gather(): pl.pallas_call(kernel, out_shape=[shape((32,) + block.shape, low)] + [sha...  86 us
    pallas_call x1, Pallas kernels, backward_scatter(): pl.pallas_call(kernel, out_shape=shapes, in_specs=[ANYWHERE] * 12 + [VMEM...  82.2 us
    pallas_call x1, Pallas kernels, gather_all(): pl.pallas_call(gather_all_kernel, out_shape=jax.ShapeDtypeStruct((32,) +...  79.5 us
    pallas_call x1, Pallas kernels, scatter_end(): pl.pallas_call(scatter_end_kernel, out_shape=(jax.ShapeDtypeStruct((rows,...  64.8 us
    pallas_call x1, Pallas kernels, gather_start(): pl.pallas_call(gather_start_kernel, out_shape=(jax.ShapeDtypeStruct((8 *...  61.6 us
    pallas_call x1, Pallas kernels, scatter_rows(): pl.pallas_call(scatter_rows_kernel, out_shape=jax.ShapeDtypeStruct((rows,...  55.8 us
    pallas_call x1, Pallas kernels, gather_rows(): pl.pallas_call(gather_rows_kernel, out_shape=jax.ShapeDtypeStruct((8 * ro...  51.7 us

profile of v4, /device:TPU:8, one launch (start us, length us, event | category | flops | bytes accessed | tf_op | source)
XLA Modules:
  0.0 677.8 jit_solution(9541475897146325359)
XLA Ops:
  3.4 2.8 concatenate.64
  7.3 1.0 copy.63.refs_9_.refs_16_
  8.3 1.9 bitcast_select_fusion.refs_0_
  10.3 1.1 fusion.39
  11.6 1.9 fusion.10
  13.5 1.3 pad_maximum_fusion
  14.8 61.6 %gather_start.1 = (bf16[1024,2048]{1,0:T(8,128)(2,1)}, bf16[32,80,768]{2,1,0:T(8,128)(2,1)}, bf16[512,2048]{1,0:T(8,128)(2,1)}) custom-call(bf16[128,2048]{1,0:T(8,128)(2,1)} %bitcast.106, bf16[8,80,768]{2,1,0:T(8,128)(2,1)} %copy-done.4, bf16[128,2048]{1,0:T(8,128)(2,1)} %wo_in.1), custom_call_target="tpu_custom_call" | custom-call | tf_op jit(solution)/shard_map/gather_start/pallas_call | solution.py:1137
  76.4 1.2 slice.135
  80.5 86.0 %forward_gather.1 = (bf16[32,128,2048]{2,1,0:T(8,128)(2,1)}, bf16[1024,2048]{1,0:T(8,128)(2,1)}, f32[1024,640]{1,0:T(8,128)}, bf16[1024,512]{1,0:T(8,128)(2,1)},...) custom-call(bf16[128,2048]{1,0:T(8,128)(2,1)} %bitcast_select_fusion, ...), custom_call_target="tpu_custom_call" | custom-call | tf_op jit(solution)/shard_map/forward_gather/pallas_call | solution.py:1443
  166.5 55.8 %scatter_rows.1 = f32[128,2048]{1,0:T(8,128)} custom-call(bf16[1024,2048]{1,0:T(8,128)(2,1)} %get-tuple-element.46.part), custom_call_target="tpu_custom_call" | custom-call | tf_op jit(solution)/shard_map/scatter_rows/pallas_call | solution.py:1031
  222.3 1.5 multiply_reduce_fusion.2
  224.7 1.0 concatenate.82.source
  225.7 79.5 %gather_all.1.refs_0_ = bf16[32,128,2176]{2,1,0:T(8,128)(2,1)} custom-call(bf16[128,2176]{1,0:T(8,128)(2,1)} %concatenate.82.source), custom_call_target="tpu_custom_call" | custom-call | tf_op jit(solution)/shard_map/gather_all/pallas_call | solution.py:721
  305.2 121.9 %expert_exchange.1 = (f32[128,2176]{1,0:T(8,128)}, bf16[16,96,2048]{2,1,0:T(8,128)(2,1)}, bf16[16,96,128]{2,1,0:T(8,128)(2,1)}, bf16[1536,2048]{1,0:T(8,128)(2,1...) custom-call(bf16[32,128,2176]{2,1,0:T(8,128)(2,1)} %gather_all.1.ref, ...), custom_call_target="tpu_custom_call" | custom-call | tf_op jit(solution)/shard_map/expert_exchange/pallas_call | solution.py:1853
  427.1 1.1 multiply_reduce_fusion.3
  428.2 2.3 fusion.46
  430.6 2.4 reshape.209
  433.0 2.0 multiply_reduce_fusion
  435.1 1.1 fusion.38.source
  436.2 51.7 %gather_rows.1.refs_2_ = bf16[1024,2048]{1,0:T(8,128)(2,1)} custom-call(bf16[128,2048]{1,0:T(8,128)(2,1)} %fusion.38.source), custom_call_target="tpu_custom_call" | custom-call | tf_op jit(solution)/shard_map/gather_rows/pallas_call | solution.py:953
  487.9 82.2 %backward_scatter.1 = (f32[128,2048]{1,0:T(8,128)}, bf16[512,2048]{1,0:T(8,128)(2,1)}, bf16[2048,768]{1,0:T(8,128)(2,1)}, bf16[1024,2048]{1,0:T(8,128)(2,1)}, f32[1,2048]{1,0:T(1,128)}, /*index=5*/f32[8,128]{1,0:T(8,128)}) custom-call(bf16[16,96,2048]{2,1,0:T(8,128)(2,1)} %get-tuple-element.48.refs_0_, bf16[16,96,128]{2,1,0:T(8,128)(2,1)} %get-tuple-element.49.refs_1_, ...), custom_call_target="tpu_custom_call" | custom-call | tf_op jit(solution)/shard_map/backward_scatter/pallas_call | solution.py:2114
  571.4 1.4 reduce.11
  573.0 1.1 concatenate.83
  575.1 64.8 %scatter_end.1 = (f32[128,2048]{1,0:T(8,128)}, bf16[8,64,768]{2,1,0:T(8,128)(2,1)}, f32[128,2048]{1,0:T(8,128)}, f32[32,128]{1,0:T(8,128)}) custom-call(bf16[1024,2048]{1,0:T(8,128)(2,1)} %get-tuple-element.58.part, bf16[8,2,2,64,768]{4,3,2,1,0:T(8,128)(2,1)} %bitcast.107, bf16[2,2,128,2048]{3,2,1,0:T(8,128)(2,1)} %bitcast.112, f32[8,2,2,32,128]{4,3,2,1,0:T(8,128)} %bitcast.113), custom_call_target="tpu_custom_call" | custom-call | tf_op jit(solution)/shard_map/scatter_end/pallas_call | solution.py:1266
  639.9 1.5 fusion.3
  641.4 3.4 fusion.7
  646.8 1.0 slice.162
  650.3 1.1 copy.77
  652.1 10.1 %convolution_bitcast_fusion.2 = f32[1,2048,768]{2,1,0:T(8,128)} fusion(bf16[1536,2048]{1,0:T(8,128)(2,1)} %get-tuple-element.67, bf16[1536,768]{1,0:T(8,128)(2,1)S(1)} %copy-done.10), kind=kOutput, calls=%fused_computation.2 | convolution fusion | flops 4831838208 | bytes 14942208 | tf_op jit(solution)/shard_map/dot_general | solution.py:514
  662.3 7.1 %convolution_bitcast_fusion.1 = f32[1,2048,768]{2,1,0:T(8,128)} fusion(bf16[1536,2048]{1,0:T(8,128)(2,1)S(1)} %bitcast.132, bf16[1536,768]{1,0:T(8,128)(2,1)S(1)} %copy-done.9), kind=kOutput, calls=%fused_computation.1 | convolution fusion | flops 4831838208 | bytes 14942208 | tf_op jit(solution)/shard_map/dot_general | solution.py:514
  669.4 7.0 %convolution_bitcast_fusion = f32[1,768,2048]{2,1,0:T(8,128)} fusion(bf16[1536,768]{1,0:T(8,128)(2,1)S(1)} %copy-done.8, bf16[1536,2048]{1,0:T(8,128)(2,1)S(1)} %bitcast.130), kind=kOutput, calls=%fused_computation | convolution fusion | flops 4831838208 | bytes 14942208 | tf_op jit(solution)/shard_map/dot_general | solution.py:514
  676.3 1.0 copy.94
  (95 shorter events, 15.5 us)
Async XLA Ops:
  1.7 11.8 %copy-start.6 = (s32[1024]{0:T(1024)}, s32[1024]{0:T(1024)S(1)}, u32[]{:S(2)}) copy-start(s32[1024]{0:T(1024)S(1)} %convert_reduce_fusion) | copy-start | bytes 12292
  11.5 3.2 copy-start.4
  80.5 143.5 %copy-start.2 = (bf16[2048,32]{1,0:T(8,128)(2,1)}, bf16[2048,32]{1,0:T(8,128)(2,1)S(1)}, u32[]{:S(2)}) copy-start(bf16[2048,32]{1,0:T(8,128)(2,1)S(1)} %reshape.204) | copy-start | bytes 393220
  166.5 55.8 %copy-start = (bf16[1,128,2048]{2,1,0:T(8,128)(2,1)S(1)}, bf16[1,128,2048]{2,1,0:T(8,128)(2,1)}, u32[]{:S(2)}) copy-start(bf16[1,128,2048]{2,1,0:T(8,128)(2,1)} %param.16) | copy-start | bytes 1572868
  427.1 8.0 %copy-start.1 = (bf16[1,128,2048]{2,1,0:T(8,128)(2,1)S(1)}, bf16[1,128,2048]{2,1,0:T(8,128)(2,1)}, u32[]{:S(2)}) copy-start(bf16[1,128,2048]{2,1,0:T(8,128)(2,1)} %param.17) | copy-start | bytes 1572868
  641.4 3.4 copy-start.7
  644.8 5.2 copy-start.3
  650.1 2.0 copy-start.10
  650.3 11.9 %slice-start.2 = ((s8[6291456]{0:T(1024)(128)(4,1)}), s8[4194304]{0:T(1024)(128)(4,1)S(1)}, s32[]{:S(2)}) async-start(s8[6291456]{0:T(1024)(128)(4,1)} %bitcast.131), calls=%async_computation.2 | async-start | bytes 8388608
  652.1 10.1 %slice-start.3 = ((s8[6291456]{0:T(1024)(128)(4,1)}), s8[2097152]{0:T(1024)(128)(4,1)S(1)}, s32[]{:S(2)}) async-start(s8[6291456]{0:T(1024)(128)(4,1)} %bitcast.131), calls=%async_computation.3 | async-start | bytes 4194304
  652.1 10.1 %copy-start.9 = (bf16[1536,768]{1,0:T(8,128)(2,1)S(1)}, bf16[1536,768]{1,0:T(8,128)(2,1)}, u32[]{:S(2)}) copy-start(bf16[1536,768]{1,0:T(8,128)(2,1)} %get-tuple-element.69) | copy-start | bytes 7077892
  652.1 17.2 %slice-start = ((s8[6291456]{0:T(1024)(128)(4,1)}), s8[4194304]{0:T(1024)(128)(4,1)S(1)}, s32[]{:S(2)}) async-start(s8[6291456]{0:T(1024)(128)(4,1)} %bitcast.129), calls=%async_computation | async-start | bytes 8388608
  662.3 7.1 %slice-start.1 = ((s8[6291456]{0:T(1024)(128)(4,1)}), s8[2097152]{0:T(1024)(128)(4,1)S(1)}, s32[]{:S(2)}) async-start(s8[6291456]{0:T(1024)(128)(4,1)} %bitcast.129), calls=%async_computation.1 | async-start | bytes 4194304
  662.3 7.1 %copy-start.8 = (bf16[1536,768]{1,0:T(8,128)(2,1)S(1)}, bf16[1536,768]{1,0:T(8,128)(2,1)}, u32[]{:S(2)}) copy-start(bf16[1536,768]{1,0:T(8,128)(2,1)} %get-tuple-element.70) | copy-start | bytes 7077892
  669.3 7.0 %copy-start.5 = (f32[128,2048]{1,0:T(8,128)S(1)}, f32[128,2048]{1,0:T(8,128)}, u32[]{:S(2)}) copy-start(f32[128,2048]{1,0:T(8,128)} %get-tuple-element.199) | copy-start | bytes 3145732

commit v5 on v4

--- a/solution.py
+++ b/solution.py
@@ -664,12 +664,23 @@
     def wait(self, slot):
         arrived(self.out.at[slot], self.recv_sems.at[slot], self.along_x)
 
+    def line(self, i):
+        z, y, x, k = self.at
+        slot = slot_of(self.order[i], y, x, k)
+        if i > 1:
+            pl.when((z > 0) & (z < LINE - 1))(lambda: self.wait(slot))
+        along_line(z, y, x, k, slot, i, self.order, self.pass_on)
+
     def column(self, i):
         z, y, x, k = self.at
         slot = self.mine if i == 0 else slot_of(self.order[i], y, x, k)
-        if i > 0:
+        if i == 0:
+            along_line(z, y, x, k, slot, i, self.order, self.pass_on)
+        elif i == 1:
             self.wait(slot)
-        along_line(z, y, x, k, slot, i, self.order, self.pass_on)
+            self.line(1)
+        else:
+            pl.when((z == 0) | (z == LINE - 1))(lambda: self.wait(slot))
         for device in (self.along_x, self.along_y, self.sibling):
             self.pass_on(slot, device)
 
@@ -688,49 +699,35 @@
 
     def advance(self, i):
         self.column(i)
+        if i < 3:
+            self.line(i + 1)
         self.receive(self.across(i - 1, True, False))
         self.receive(self.across(i - 1, False, True))
 
-    def finish(self):
+    def turn(self):
         self.receive(self.across(3, True, False))
         for j in (0, 1):
             self.pass_on(self.across(j, True, False), self.along_y)
         self.receive(self.across(3, False, True))
         for j in (2, 3):
             self.pass_on(self.across(j, False, True), self.along_x)
+
+    def last(self, waited=()):
         for i in range(4):
             self.receive(self.across(i, True, True))
         z, y, x, k = self.at
         for i in range(4):
-            for dy in (y, 1 - y):
-                for dx in (x, 1 - x):
-                    self.wait(slot_of(self.order[i], dy, dx, 1 - k))
+            for dy, dx in ((0, 0), (0, 1), (1, 0), (1, 1)):
+                if (dy, dx) not in waited:
+                    self.wait(
+                        slot_of(self.order[i], 1 - y if dy else y, 1 - x if dx else x, 1 - k)
+                    )
+        self.sends.finish()
+
+    def finish(self):
+        self.turn()
+        self.last()
         self.own.wait()
-        self.sends.finish()
-
-
-def gather_all_kernel(source, out, *semaphores):
-    blocks = BlockGather(source, out, *semaphores)
-    blocks.begin()
-    for i in (1, 2, 3):
-        blocks.advance(i)
-    blocks.finish()
-
-
-def gather_all(block, collective_id):
-    return pl.pallas_call(
-        gather_all_kernel,
-        out_shape=jax.ShapeDtypeStruct((32,) + block.shape, block.dtype),
-        in_specs=[ANYWHERE],
-        out_specs=ANYWHERE,
-        scratch_shapes=[
-            pltpu.SemaphoreType.DMA,
-            pltpu.SemaphoreType.DMA((40,)),
-            pltpu.SemaphoreType.DMA((32,)),
-        ],
-        compiler_params=pltpu.CompilerParams(collective_id=collective_id, has_side_effects=True),
-        name="gather_all",
-    )(block)
 
 
 def add_blocks(target, *terms):
@@ -906,12 +903,10 @@
         for copy in self.own:
             copy.start()
 
-    def column(self, i):
+    def send(self, i, along, across):
         z, y, x, k = self.at
         chip = self.order[i]
         pieces = halves(self.out, chip, y)
-        if i > 0:
-            self.wait(chip, y)
         for n in (0, 1):
             block = split_rows(self.source)[n] if i == 0 else pieces[n]
             recv = self.semaphores.at[n, chip * 2 + y]
@@ -919,8 +914,23 @@
             def start(_, device, condition=None):
                 self.sends.start(block, pieces[n], recv, device, condition)
 
-            along_line(z, y, x, k, None, i, self.order, start)
-            start(None, self.along_y)
+            if along:
+                along_line(z, y, x, k, None, i, self.order, start)
+            if across:
+                start(None, self.along_y)
+
+    def line(self, i):
+        z, y = self.at[:2]
+        pl.when((z > 0) & (z < LINE - 1))(lambda: self.wait(self.order[i], y))
+        self.send(i, True, False)
+
+    def column(self, i):
+        z, y = self.at[:2]
+        if i == 1:
+            self.wait(self.order[i], y)
+        elif i > 1:
+            pl.when((z == 0) | (z == LINE - 1))(lambda: self.wait(self.order[i], y))
+        self.send(i, i < 2, True)
 
     def wait(self, chip, y):
         for n, piece in enumerate(halves(self.out, chip, y)):
@@ -934,31 +944,121 @@
             copy.wait()
 
 
-def gather_rows_kernel(source, out, local_sems, send_sems, recv_sems):
+def gather_rows_kernel(
+    source,
+    x_late,
+    x_early,
+    d_in,
+    hidden_late,
+    hidden_early,
+    d_gate_in,
+    d_up_in,
+    out,
+    gate_out,
+    up_out,
+    down_out,
+    x_ref,
+    d_ref,
+    hidden_ref,
+    d_gate_ref,
+    d_up_ref,
+    gate_ref,
+    up_ref,
+    down_ref,
+    load_sems,
+    store_sems,
+    local_sems,
+    send_sems,
+    recv_sems,
+):
     at = place()
     z, y, x, k = at
     along_y = device_at(z, 1 - y, x, k)
+    late, early = x_late.shape[0], x_early.shape[0]
+    loads = [
+        pltpu.make_async_copy(a, b, load_sems.at[n])
+        for n, (a, b) in enumerate(
+            (
+                (x_late, x_ref.at[pl.ds(0, late), :]),
+                (x_early, x_ref.at[pl.ds(late, early), :]),
+                (d_gate_in, d_gate_ref),
+                (d_up_in, d_up_ref),
+                (hidden_late, hidden_ref.at[pl.ds(0, late), :]),
+                (hidden_early, hidden_ref.at[pl.ds(late, early), :]),
+                (d_in, d_ref),
+            )
+        )
+    ]
+    stores = [
+        pltpu.make_async_copy(a, b, store_sems.at[n])
+        for n, (a, b) in enumerate(
+            ((gate_ref, gate_out), (up_ref, up_out), (down_ref, down_out))
+        )
+    ]
     meet(z, y, x, k, (along_y,))
     sends = Sends(send_sems)
     rows = RowGather(source, out, sends, local_sems, recv_sems, at, line_order(z), along_y)
-    for i in range(4):
-        rows.column(i)
+    rows.column(0)
+    for copy in loads:
+        copy.start()
+
+    def inward(i, carry):
+        part = pl.ds(pl.multiple_of(i * 256, 256), 256)
+        left = x_ref[:, part]
+        gate_ref[part, :] = dot_left_transposed(left, d_gate_ref[...]).astype(gate_ref.dtype)
+        up_ref[part, :] = dot_left_transposed(left, d_up_ref[...]).astype(up_ref.dtype)
+        return carry
+
+    def outward(i, carry):
+        part = pl.ds(pl.multiple_of(i * 256, 256), 256)
+        down_ref[part, :] = dot_left_transposed(hidden_ref[:, part], d_ref[...]).astype(
+            down_ref.dtype
+        )
+        return carry
+
+    steps = x_ref.shape[1] // 256
+    for copy in loads[:4]:
+        copy.wait()
+    lax.fori_loop(0, 3, inward, 0)
+    rows.column(1)
+    rows.line(2)
+    lax.fori_loop(3, steps, inward, 0)
+    for copy in stores[:2]:
+        copy.start()
+    rows.column(2)
+    rows.line(3)
+    for copy in loads[4:]:
+        copy.wait()
+    lax.fori_loop(0, hidden_ref.shape[1] // 256, outward, 0)
+    stores[2].start()
+    rows.column(3)
     rows.finish()
+    for copy in stores:
+        copy.wait()
     sends.finish()
 
 
-def gather_rows(block, collective_id):
+def gather_rows(block, x_rows, d_rows, hidden, d_gate, d_up, collective_id):
     rows, width = block.shape
-    dma = pltpu.SemaphoreType.DMA
+    ff, low = d_up.shape[1], block.dtype
+    slots = d_up.shape[0]
+    shape, vmem, dma = jax.ShapeDtypeStruct, pltpu.VMEM, pltpu.SemaphoreType.DMA
+    inputs = (*x_rows, d_rows, *hidden, d_gate, d_up)
+    held = ((slots, width), (slots, width), (slots, ff), (slots, ff), (slots, ff))
+    grads = ((width, ff), (width, ff), (ff, width))
     return pl.pallas_call(
         gather_rows_kernel,
-        out_shape=jax.ShapeDtypeStruct((8 * rows, width), block.dtype),
-        in_specs=[ANYWHERE],
-        out_specs=ANYWHERE,
-        scratch_shapes=[dma((2,)), dma((24,)), dma((2, 8))],
-        compiler_params=pltpu.CompilerParams(collective_id=collective_id, has_side_effects=True),
+        out_shape=[shape((8 * rows, width), low)] + [shape(size, low) for size in grads],
+        in_specs=[ANYWHERE] * 8,
+        out_specs=[ANYWHERE] * 4,
+        scratch_shapes=[vmem(size, low) for size in held]
+        + [vmem(size, low) for size in grads]
+        + [dma((7,)), dma((3,)), dma((2,)), dma((24,)), dma((2, 8))],
+        compiler_params=pltpu.CompilerParams(
+            collective_id=collective_id, has_side_effects=True, vmem_limit_bytes=VMEM_BYTES
+        ),
         name="gather_rows",
-    )(block)
+    )(block, *inputs)
 
 
 class RowScatter:
@@ -1116,7 +1216,9 @@
             pass_on(take((c + 8 - t) % 8, beside), sibling)
 
     rows.column(1)
+    rows.line(2)
     rows.column(2)
+    rows.line(3)
     onward()
     rows.column(3)
     across()
@@ -1493,6 +1595,193 @@
         target[:, part] = total.astype(target.dtype)
 
 
+def blocks_at(at, g):
+    z, y, x, k = at
+    found = []
+    for lane in (k, 1 - k):
+        for i, r in group_blocks(g):
+            dy, dx = r // 2, r % 2
+            slot = slot_of(order_at(z, i), y + dy * (1 - 2 * y), x + dx * (1 - 2 * x), lane)
+            found.append((slot, i * 4 + r))
+    return found
+
+
+def rank_mask(experts, e, extra):
+    lane = lax.broadcasted_iota(jnp.int32, (8, extra), 1)
+    return (lane == 2 * experts + e).astype(BRAIN_FLOAT_TYPE)
+
+
+def picked(mask, pay, width, capacity):
+    rank = dot_right_transposed(mask, pay[:, width:])
+    slots = lax.broadcasted_iota(jnp.int32, (capacity, pay.shape[0]), 0).astype(SINGLE_FLOAT)
+    return (rank[0:1, :] == slots).astype(BRAIN_FLOAT_TYPE)
+
+
+def early_step(n):
+    late = n // 3
+    return (1 - late) * (7 - n) + late * (3 + (n + 1) % 2 - n // 5)
+
+
+def gather_forward_kernel(
+    capacity,
+    payload_in,
+    dout_all,
+    wg_in,
+    wu_in,
+    wd_in,
+    pay_all,
+    x_out,
+    d_out,
+    extra_out,
+    gh_out,
+    uh_out,
+    hid_out,
+    eo_out,
+    pick_out,
+    wg_ref,
+    wu_ref,
+    wd_ref,
+    pay_ref,
+    dout_ref,
+    x_ref,
+    d_ref,
+    extra_ref,
+    gh_ref,
+    uh_ref,
+    hid_ref,
+    eo_ref,
+    pick_ref,
+    weight_sems,
+    load_sems,
+    store_sems,
+    local_sem,
+    send_sems,
+    recv_sems,
+):
+    blocks = BlockGather(payload_in, pay_all, local_sem, send_sems, recv_sems)
+    blocks.begin()
+    weights = [
+        pltpu.make_async_copy(a, b, weight_sems.at[n])
+        for n, (a, b) in enumerate(((wg_in, wg_ref), (wu_in, wu_ref), (wd_in, wd_ref)))
+    ]
+    for copy in weights:
+        copy.start()
+    width = wg_in.shape[0]
+    tokens, payload = payload_in.shape
+    experts = (payload - width) // 4
+    rows = 4 * capacity
+    mask = rank_mask(experts, blocks.mine, payload - width)
+
+    def stores(n):
+        g = early_step(n) - 2
+        part = pl.ds(pl.multiple_of(g * rows, rows), rows)
+        pairs = (
+            (x_ref, x_out), (d_ref, d_out), (extra_ref, extra_out), (gh_ref, gh_out),
+            (uh_ref, uh_out), (hid_ref, hid_out), (eo_ref, eo_out),
+        )
+        return [
+            pltpu.make_async_copy(a, b.at[part, :], store_sems.at[m])
+            for m, (a, b) in enumerate(pairs)
+        ] + [pltpu.make_async_copy(pick_ref, pick_out.at[g], store_sems.at[7])]
+
+    def group(n, carry):
+        found = blocks_at(blocks.at, early_step(n))
+        for slot, _ in found[2:]:
+            blocks.wait(slot)
+        loads = [
+            (
+                pltpu.make_async_copy(pay_all.at[slot], pay_ref.at[m], load_sems.at[m]),
+                pltpu.make_async_copy(dout_all.at[slot], dout_ref.at[m], load_sems.at[4 + m]),
+            )
+            for m, (slot, _) in enumerate(found)
+        ]
+        for pair in loads:
+            for copy in pair:
+                copy.start()
+
+        @pl.when(n > 0)
+        def _():
+            for copy in stores(n - 1):
+                copy.wait()
+
+        for m in range(4):
+            for copy in loads[m]:
+                copy.wait()
+            part = slice(m * capacity, (m + 1) * capacity)
+            pick = picked(mask, pay_ref.at[m], width, capacity)
+            pick_ref[m] = pick
+            chosen = dot_rows(pick, pay_ref[m]).astype(BRAIN_FLOAT_TYPE)
+            x_ref[part, :] = chosen[:, :width]
+            extra_ref[part, :] = chosen[:, width:]
+            d_ref[part, :] = dot_rows(pick, dout_ref[m]).astype(BRAIN_FLOAT_TYPE)
+        forward_rows(x_ref, wg_ref, wu_ref, wd_ref, gh_ref, uh_ref, hid_ref, eo_ref)
+        for copy in stores(n):
+            copy.start()
+        return carry
+
+    blocks.advance(1)
+    blocks.own.wait()
+    for copy in weights:
+        copy.wait()
+    lax.fori_loop(0, 1, group, 0)
+    blocks.advance(2)
+    lax.fori_loop(1, 2, group, 0)
+    blocks.advance(3)
+    lax.fori_loop(2, 3, group, 0)
+    blocks.turn()
+    lax.fori_loop(3, GROUPS - 2, group, 0)
+    blocks.last(((0, 0), (0, 1), (1, 0)))
+    for copy in stores(5):
+        copy.wait()
+
+
+def forward_rows(x_ref, wg_ref, wu_ref, wd_ref, gh_ref, uh_ref, hid_ref, eo_ref):
+    x = x_ref[...]
+    gate_hidden = dot_rows(x, wg_ref[...])
+    up_hidden = dot_rows(x, wu_ref[...])
+    gh_ref[...] = gate_hidden
+    uh_ref[...] = up_hidden
+    sigmoid = 1.0 / (1.0 + jnp.exp(-gate_hidden))
+    hidden = (gate_hidden * sigmoid * up_hidden).astype(BRAIN_FLOAT_TYPE)
+    hid_ref[...] = hidden
+    eo_ref[...] = dot_rows(hidden, wd_ref[...]).astype(BRAIN_FLOAT_TYPE)
+
+
+def gather_forward(capacity, payload, dout_all, wg, wu, wd, collective_id):
+    tokens, wide = payload.shape
+    width, ff = wg.shape
+    low = BRAIN_FLOAT_TYPE
+    rows = 4 * capacity
+    early = (GROUPS - 2) * rows
+    shape, vmem, dma = jax.ShapeDtypeStruct, pltpu.VMEM, pltpu.SemaphoreType.DMA
+    extra = wide - width
+    sizes = (
+        (width, low), (width, low), (extra, low), (ff, SINGLE_FLOAT), (ff, SINGLE_FLOAT),
+        (ff, low), (width, low),
+    )
+
+    def kernel(*refs):
+        gather_forward_kernel(capacity, *refs)
+
+    return pl.pallas_call(
+        kernel,
+        out_shape=[shape((32, tokens, wide), low)]
+        + [shape((early, n), dtype) for n, dtype in sizes]
+        + [shape((GROUPS - 2, 4, capacity, tokens), low)],
+        in_specs=[ANYWHERE] * 5,
+        out_specs=[ANYWHERE] * 9,
+        scratch_shapes=[vmem((width, ff), low), vmem((width, ff), low), vmem((ff, width), low)]
+        + [vmem((4, tokens, wide), low), vmem((4, tokens, width), low)]
+        + [vmem((rows, n), dtype) for n, dtype in sizes]
+        + [vmem((4, capacity, tokens), low)]
+        + [dma((3,)), dma((8,)), dma((8,)), dma, dma((40,)), dma((32,))],
+        compiler_params=pltpu.CompilerParams(
+            collective_id=collective_id, has_side_effects=True, vmem_limit_bytes=VMEM_BYTES
+        ),
+        name="gather_forward",
+    )(payload, dout_all, wg, wu, wd)
+
+
 def expert_exchange_kernel(
     capacity,
     pay_all,
@@ -1500,12 +1789,18 @@
     wg_in,
     wu_in,
     wd_in,
+    d_early,
+    extra_early,
+    gh_early,
+    uh_early,
+    eo_early,
+    pick_early,
     back_ref,
     rows_out,
     pick_out,
     x_out,
+    hid_out,
     deo_out,
-    hid_out,
     dgl_out,
     dul_out,
     wg_ref,
@@ -1514,12 +1809,15 @@
     pay_ref,
     dout_ref,
     x_ref,
+    hid_ref,
     deo_ref,
-    hid_ref,
     dgl_ref,
     dul_ref,
     d_ref,
-    g_ref,
+    extra_ref,
+    gh_ref,
+    uh_ref,
+    eo_ref,
     far_pick_ref,
     far_d_ref,
     far_o_ref,
@@ -1534,6 +1832,7 @@
     down_ref,
     weight_sems,
     load_sems,
+    early_sems,
     row_sems,
     near_sems,
     far_sems,
@@ -1564,13 +1863,13 @@
     rows = 4 * capacity
     above, below = device_at(z + 1, y, x, k), device_at(z - 1, y, x, k)
 
-    def far_copies(n, j):
+    def far_copies(n, j, side):
         half = pl.ds(capacity, capacity)
         return [
             remote(a, b, far_sems.at[n, m], sibling_sems.at[m, j], sibling)
             for m, (a, b) in enumerate(
                 (
-                    (far_pick_ref.at[n], pick_ref.at[j, half, :]),
+                    (far_pick_ref.at[side, n], pick_ref.at[j, half, :]),
                     (far_d_ref.at[n], rows_ref.at[j, half, :]),
                     (far_o_ref.at[n], rows_out.at[j, half, :]),
                 )
@@ -1579,7 +1878,7 @@
 
     def gather(i, r, *extra):
         j = i * 4 + r
-        for copy in far_copies(0, j)[:2]:
+        for copy in far_copies(0, j, 0)[:2]:
             copy.wait_recv()
         spread_rows(own_ref.at[j], pick_ref.at[j], rows_ref.at[j], *extra)
         return own_ref.at[j]
@@ -1655,8 +1954,8 @@
         cross(0)
         along(2)
 
-    at_start = {5: lambda: cross(2), 6: sixth, 7: last}
-    at_middle = {1: lambda: corners(2, 0), 2: lambda: corners(3, 1), 3: lambda: cross(3)}
+    at_start = {4: lambda: cross(3), 5: lambda: cross(2), 6: sixth, 7: last}
+    at_middle = {1: lambda: corners(2, 0), 2: lambda: corners(3, 1)}
 
     def at(g, table):
         for n, work in table.items():
@@ -1664,40 +1963,34 @@
 
     for copy in weights:
         copy.wait()
-    slot_row = lax.broadcasted_iota(jnp.int32, (capacity, tokens), 0).astype(SINGLE_FLOAT)
     row_lane = lax.broadcasted_iota(jnp.int32, (capacity, payload - width), 1)
     e = mine
-    is_gate = (row_lane == e) | (row_lane == experts + e)
-    rank_lane = (
-        lax.broadcasted_iota(jnp.int32, (8, payload - width), 1) == 2 * experts + e
-    ).astype(BRAIN_FLOAT_TYPE)
+    all_lane = lax.broadcasted_iota(jnp.int32, (rows, payload - width), 1)
+    is_gate = (all_lane == e) | (all_lane == experts + e)
+    mask = rank_mask(experts, e, payload - width)
+    at_here = (z, y, x, k)
 
     def row_copies(g):
-        out_rows = pl.ds(pl.multiple_of(g * rows, rows), rows)
-        pairs = (
-            (x_ref, x_out), (deo_ref, deo_out), (hid_ref, hid_out), (dgl_ref, dgl_out),
-            (dul_ref, dul_out),
-        )
+        part = pl.ds(pl.multiple_of(g * rows, rows), rows)
+        pairs = ((deo_ref, deo_out), (dgl_ref, dgl_out), (dul_ref, dul_out))
         return [
-            pltpu.make_async_copy(a, b.at[out_rows, :], row_sems.at[n])
+            pltpu.make_async_copy(a, b.at[part, :], row_sems.at[n])
             for n, (a, b) in enumerate(pairs)
         ]
 
-    def blocks_of(g):
-        found = []
-        for lane_k in (k, 1 - k):
-            for i, r in group_blocks(g):
-                dy, dx = r // 2, r % 2
-                slot = slot_of(
-                    order_at(z, i), y + dy * (1 - 2 * y), x + dx * (1 - 2 * x), lane_k
-                )
-                found.append((slot, i * 4 + r))
-        return found
+    def late_copies(g):
+        part = pl.ds(pl.multiple_of(g * rows, rows), rows)
+        return [
+            pltpu.make_async_copy(a, b.at[part, :], row_sems.at[3 + n])
+            for n, (a, b) in enumerate(((x_ref, x_out), (hid_ref, hid_out)))
+        ]
 
     def near_copies(g):
         return [
             pltpu.make_async_copy(
-                near_o_ref.at[n], rows_out.at[blocks_of(g)[n][1], pl.ds(0, capacity), :], near_sems.at[n]
+                near_o_ref.at[n],
+                rows_out.at[blocks_at(at_here, g)[n][1], pl.ds(0, capacity), :],
+                near_sems.at[n],
             )
             for n in (0, 1)
         ]
@@ -1706,62 +1999,96 @@
         for copy in row_copies(g) + near_copies(g):
             copy.wait()
         for n in (0, 1):
-            for copy in far_copies(n, blocks_of(g)[2 + n][1]):
+            for copy in far_copies(n, blocks_at(at_here, g)[2 + n][1], g % 2):
                 copy.wait_send()
 
     def load_copies(g):
-        return [
-            (
-                pltpu.make_async_copy(pay_all.at[slot], pay_ref.at[n], load_sems.at[n]),
-                pltpu.make_async_copy(dout_all.at[slot], dout_ref.at[n], load_sems.at[4 + n]),
+        copies = []
+        for n, (slot, _) in enumerate(blocks_at(at_here, g)):
+            copies.append(pltpu.make_async_copy(pay_all.at[slot], pay_ref.at[n], load_sems.at[n]))
+            copies.append(
+                pltpu.make_async_copy(dout_all.at[slot], dout_ref.at[n], load_sems.at[4 + n])
             )
-            for n, (slot, _) in enumerate(blocks_of(g))
+        return copies
+
+    def early_copies(g):
+        side, at = g % 2, g - 2
+        part = pl.ds(pl.multiple_of(at * rows, rows), rows)
+        pairs = (
+            (d_early, d_ref), (extra_early, extra_ref), (gh_early, gh_ref), (uh_early, uh_ref),
+            (eo_early, eo_ref),
+        )
+        copies = [
+            pltpu.make_async_copy(a.at[part, :], b.at[side], early_sems.at[side, n])
+            for n, (a, b) in enumerate(pairs)
         ]
-
-    def load(g):
-        for pair in load_copies(g):
-            for copy in pair:
-                copy.start()
+        for n, (_, j) in enumerate(blocks_at(at_here, g)):
+            target = pick_ref.at[j, pl.ds(0, capacity), :] if n < 2 else far_pick_ref.at[side, n - 2]
+            copies.append(
+                pltpu.make_async_copy(pick_early.at[at, n], target, early_sems.at[side, 5 + n])
+            )
+        return copies
 
     def step(g, carry):
-        blocks = blocks_of(g)
+        blocks = blocks_at(at_here, g)
+        side = g % 2
         at(g, at_start)
 
         @pl.when(g > 0)
         def _():
             settle(g - 1)
 
-        loads = load_copies(g)
-        for n in range(4):
-            for copy in loads[n]:
+        @pl.when((g > 0) & (g < GROUPS - 1))
+        def _():
+            for copy in early_copies(g + 1):
+                copy.start()
+
+        @pl.when(g < 2)
+        def _():
+            @pl.when(g == 1)
+            def _():
+                for copy in late_copies(g - 1):
+                    copy.wait()
+
+            for copy in load_copies(g):
                 copy.wait()
-            part = slice(n * capacity, (n + 1) * capacity)
-            rank = dot_right_transposed(rank_lane, pay_ref[n, :, width:])
-            pick = (rank[0:1, :] == slot_row).astype(BRAIN_FLOAT_TYPE)
-            if n < 2:
-                pick_ref[blocks[n][1], 0:capacity, :] = pick
-            else:
-                far_pick_ref[n - 2] = pick
-            chosen = dot_rows(pick, pay_ref[n])
-            x_ref[part, :] = chosen[:, :width].astype(BRAIN_FLOAT_TYPE)
-            gate = jnp.sum(jnp.where(is_gate, chosen[:, width:], 0.0), axis=-1, keepdims=True)
-            g_ref[part, :] = gate
-            d_rows = dot_rows(pick, dout_ref[n])
-            d_ref[part, :] = d_rows.astype(BRAIN_FLOAT_TYPE)
-            deo_ref[part, :] = (gate * d_rows).astype(BRAIN_FLOAT_TYPE)
-
-        @pl.when(g < GROUPS - 1)
+            for n in range(4):
+                part = slice(n * capacity, (n + 1) * capacity)
+                pick = picked(mask, pay_ref.at[n], width, capacity)
+                if n < 2:
+                    pick_ref[blocks[n][1], 0:capacity, :] = pick
+                else:
+                    far_pick_ref[side, n - 2] = pick
+                chosen = dot_rows(pick, pay_ref[n]).astype(BRAIN_FLOAT_TYPE)
+                x_ref[part, :] = chosen[:, :width]
+                extra_ref[side, part, :] = chosen[:, width:]
+                d_ref[side, part, :] = dot_rows(pick, dout_ref[n]).astype(BRAIN_FLOAT_TYPE)
+
+            @pl.when(g == 0)
+            def _():
+                for copy in load_copies(g + 1):
+                    copy.start()
+
+            forward_rows(
+                x_ref, wg_ref, wu_ref, wd_ref, gh_ref.at[side], uh_ref.at[side], hid_ref,
+                eo_ref.at[side],
+            )
+            for copy in late_copies(g):
+                copy.start()
+
+        @pl.when(g >= 2)
         def _():
-            load(g + 1)
+            for copy in early_copies(g):
+                copy.wait()
 
         at(g, at_middle)
-        rows_in = x_ref[...]
-        gate_hidden = dot_rows(rows_in, wg_ref[...])
-        up_hidden = dot_rows(rows_in, wu_ref[...])
+        gates = jnp.sum(
+            jnp.where(is_gate, extra_ref[side].astype(SINGLE_FLOAT), 0.0), axis=-1, keepdims=True
+        )
+        deo_ref[...] = (gates * d_ref[side].astype(SINGLE_FLOAT)).astype(BRAIN_FLOAT_TYPE)
+        gate_hidden, up_hidden = gh_ref[side], uh_ref[side]
         sigmoid = 1.0 / (1.0 + jnp.exp(-gate_hidden))
         silu = gate_hidden * sigmoid
-        hidden = (silu * up_hidden).astype(BRAIN_FLOAT_TYPE)
-        hid_ref[...] = hidden
         d_hidden = dot_right_transposed(deo_ref[...], wd_ref[...])
         d_gate = (d_hidden * up_hidden * sigmoid * (1.0 + gate_hidden * (1.0 - sigmoid))).astype(
             BRAIN_FLOAT_TYPE
@@ -1771,16 +2098,15 @@
         dul_ref[...] = d_up
         for copy in row_copies(g):
             copy.start()
-        expert_out = dot_rows(hidden, wd_ref[...]).astype(BRAIN_FLOAT_TYPE)
         d_copy = (
             dot_right_transposed(d_gate, wg_ref[...]) + dot_right_transposed(d_up, wu_ref[...])
         ).astype(BRAIN_FLOAT_TYPE)
         for n in (2, 3, 0, 1):
             j = blocks[n][1]
             part = slice(n * capacity, (n + 1) * capacity)
-            e_rows = expert_out[part].astype(SINGLE_FLOAT)
+            e_rows = eo_ref[side, part, :].astype(SINGLE_FLOAT)
             d_gate_rows = jnp.sum(
-                d_ref[part, :].astype(SINGLE_FLOAT) * e_rows, axis=-1, keepdims=True
+                d_ref[side, part, :].astype(SINGLE_FLOAT) * e_rows, axis=-1, keepdims=True
             )
             high = d_gate_rows.astype(BRAIN_FLOAT_TYPE).astype(SINGLE_FLOAT)
             extra = jnp.where(row_lane == e, high, 0.0) + jnp.where(
@@ -1792,15 +2118,16 @@
                 d_target, o_target = rows_ref.at[j, pl.ds(0, capacity), :], near_o_ref.at[n]
             d_target[:, :width] = d_copy[part]
             d_target[:, width:] = extra.astype(BRAIN_FLOAT_TYPE)
-            o_target[...] = (g_ref[part, :] * e_rows).astype(BRAIN_FLOAT_TYPE)
+            o_target[...] = (gates[part] * e_rows).astype(BRAIN_FLOAT_TYPE)
             if n >= 2:
-                for copy in far_copies(n - 2, j):
+                for copy in far_copies(n - 2, j, side):
                     copy.start()
         for copy in near_copies(g):
             copy.start()
         return carry
 
-    load(0)
+    for copy in load_copies(0):
+        copy.start()
     lax.fori_loop(0, GROUPS, step, 0)
     along(1)
     total(0)
@@ -1827,10 +2154,12 @@
         add_blocks(back_ref, block, up_ref.at[z], down_ref.at[z])
 
     settle(GROUPS - 1)
+    for copy in late_copies(1):
+        copy.wait()
     keep = pltpu.make_async_copy(pick_ref, pick_out, pick_sem)
     keep.start()
     for j in range(16):
-        far_copies(0, j)[2].wait_recv()
+        far_copies(0, j, 0)[2].wait_recv()
     keep.wait()
     for copy in corner_sends + x_sends + y_sends:
         copy.wait_send()
@@ -1838,7 +2167,7 @@
         pl.when(condition)(copy.wait_send)
 
 
-def expert_exchange(capacity, pay_all, dout_all, wg, wu, wd, collective_id):
+def expert_exchange(capacity, pay_all, dout_all, wg, wu, wd, early, collective_id):
     _, tokens, wide = pay_all.shape
     width, ff = wg.shape
     low = BRAIN_FLOAT_TYPE
@@ -1856,29 +2185,30 @@
             shape((tokens, wide), SINGLE_FLOAT),
             shape((16, 2 * capacity, width), low),
             shape((16, 2 * capacity, tokens), low),
-            shape((total, width), low),
+            shape((2 * rows, width), low),
+            shape((2 * rows, ff), low),
             shape((total, width), low),
             shape((total, ff), low),
             shape((total, ff), low),
-            shape((total, ff), low),
         ),
-        in_specs=[ANYWHERE] * 5,
+        in_specs=[ANYWHERE] * 11,
         out_specs=[VMEM_WHOLE] + [ANYWHERE] * 7,
         scratch_shapes=[vmem((width, ff), low), vmem((width, ff), low), vmem((ff, width), low)]
         + [vmem((4, tokens, wide), low), vmem((4, tokens, width), low)]
-        + [vmem((rows, width), low), vmem((rows, width), low)]
-        + [vmem((rows, ff), low)] * 3
-        + [vmem((rows, width), low), vmem((rows, 1), SINGLE_FLOAT)]
-        + [vmem((2, capacity, n), low) for n in (tokens, wide, width, width)]
+        + [vmem((rows, n), low) for n in (width, ff, width, ff, ff)]
+        + [vmem((2, rows, width), low), vmem((2, rows, wide - width), low)]
+        + [vmem((2, rows, ff), SINGLE_FLOAT)] * 2
+        + [vmem((2, rows, width), low), vmem((2, 2, capacity, tokens), low)]
+        + [vmem((2, capacity, n), low) for n in (wide, width, width)]
         + [vmem((16, 2 * capacity, tokens), low), vmem((16, 2 * capacity, wide), low)]
         + [vmem((n, tokens, wide), low) for n in (16, 4, 4, 4, 4, 4)]
-        + [dma((3,)), dma((8,)), dma((5,)), dma((2,)), dma((2, 3))]
+        + [dma((3,)), dma((8,)), dma((2, 9)), dma((5,)), dma((2,)), dma((2, 3))]
         + [dma((3, 16)), dma((4,)), dma((4,)), dma((4,)), dma((4,)), dma((4,)), dma((20,)), dma],
         compiler_params=pltpu.CompilerParams(
             collective_id=collective_id, has_side_effects=True, vmem_limit_bytes=VMEM_BYTES
         ),
         name="expert_exchange",
-    )(pay_all, dout_all, wg, wu, wd)
+    )(pay_all, dout_all, wg, wu, wd, *early)
 
 
 def backward_scatter_kernel(
@@ -2273,14 +2603,14 @@
     payload = jnp.concatenate(
         [mixed, gate_high, gate_low, rank, jnp.zeros_like(rank)], axis=1
     )
-    pay_all = gather_all(payload, 3)
-    d_back, out_rows, out_pick, x_rows, d_rows, hidden, d_gate, d_up = expert_exchange(
-        capacity, pay_all, dout_all, expert_gate[0], expert_up[0], expert_down[0], 4
-    )
-    grad_gate = dot_left_transposed(x_rows, d_gate)[None]
-    grad_up = dot_left_transposed(x_rows, d_up)[None]
-    grad_down = dot_left_transposed(hidden, d_rows)[None]
-
+    experts = (expert_gate[0], expert_up[0], expert_down[0])
+    pay_all, x_early, d_early, extra_early, gh_early, uh_early, hid_early, eo_early, pick_early = (
+        gather_forward(capacity, payload, dout_all, *experts, 3)
+    )
+    early = (d_early, extra_early, gh_early, uh_early, eo_early, pick_early)
+    d_back, out_rows, out_pick, x_late, hid_late, d_rows, d_gate, d_up = expert_exchange(
+        capacity, pay_all, dout_all, *experts, early, 4
+    )
     table = d_back[:, width:]
     d_gates = table[:, :expert_count] + table[:, expert_count : 2 * expert_count]
     d_chosen = gates * (d_gates - jnp.sum(gates * d_gates, axis=-1, keepdims=True))
@@ -2292,7 +2622,12 @@
     d_state_norm, grad_ffn_gain = norm_backward(d_mixed, hidden_state, ffn_gain)
     d_state = d_layer.astype(SINGLE_FLOAT) + d_state_norm
     d_state_low = d_state.astype(BRAIN_FLOAT_TYPE)
-    dh_all = gather_rows(d_state_low, 5)
+    dh_all, grad_gate, grad_up, grad_down = gather_rows(
+        d_state_low, (x_late, x_early), d_rows, (hid_late, hid_early), d_gate, d_up, 5
+    )
+    grad_gate, grad_up, grad_down = (
+        grad[None].astype(SINGLE_FLOAT) for grad in (grad_gate, grad_up, grad_down)
+    )
     moe_sum, gwo, gw, dpart, ggain, gheads = backward_scatter(
         slack, out_rows, out_pick, dh_all, wo_all, attn, q, k, v, raw, normed, x_all, slabs, qg, kg, cosine, sine, segc, segr, 8
     )

time: 687 us -> 662 us (0.964)
  matrix products: 29 us -> 4.88 us
  other arithmetic: 18.3 us -> 28.2 us
    dot_general x4 -> x1, matrix products: 26.5 us -> 2.31 us  [dot_left_transposed(): lax.dot_general(left, right, (((0,), (0,)), ((), ())), preferred_element_...]
    convert_element_type x0 -> x3, other arithmetic: none -> 9.93 us  [tensor_body(): grad[None].astype(SINGLE_FLOAT)]
    pallas_call x1, Pallas kernels: 61.6 us -> 70.9 us  [gather_start(): pl.pallas_call(gather_start_kernel, out_shape=(jax.ShapeDtypeStruct((8 *...]
    pallas_call x1, Pallas kernels: 86 us -> 76.7 us  [forward_gather(): pl.pallas_call(kernel, out_shape=[shape((32,) + block.shape, low)] + [sha...]
    pallas_call x1, Pallas kernels: 122 us -> 114 us  [expert_exchange(): pl.pallas_call(kernel, out_shape=(shape((tokens, wide), SINGLE_FLOAT), sh...]
where the time goes in v5:
time: 662 us; the launch traced here: 657 us
  Pallas kernels  597 us (90%)
  other arithmetic  28.2 us (4%)
  local copies, waits for them, and re-layouts  25.7 us (4%)
    pallas_call x1, Pallas kernels, expert_exchange(): pl.pallas_call(kernel, out_shape=(shape((tokens, wide), SINGLE_FLOAT), sh...  114 us
    pallas_call x1, Pallas kernels, gather_forward(): pl.pallas_call(kernel, out_shape=[shape((32, tokens, wide), low)] + [shap...  80.5 us
    pallas_call x1, Pallas kernels, backward_scatter(): pl.pallas_call(kernel, out_shape=shapes, in_specs=[ANYWHERE] * 12 + [VMEM...  79.7 us
    pallas_call x1, Pallas kernels, forward_gather(): pl.pallas_call(kernel, out_shape=[shape((32,) + block.shape, low)] + [sha...  76.7 us
    pallas_call x1, Pallas kernels, gather_start(): pl.pallas_call(gather_start_kernel, out_shape=(jax.ShapeDtypeStruct((8 *...  70.9 us
    pallas_call x1, Pallas kernels, scatter_end(): pl.pallas_call(scatter_end_kernel, out_shape=(jax.ShapeDtypeStruct((rows,...  65.1 us
    pallas_call x1, Pallas kernels, scatter_rows(): pl.pallas_call(scatter_rows_kernel, out_shape=jax.ShapeDtypeStruct((rows,...  59.1 us
    pallas_call x1, Pallas kernels, gather_rows(): pl.pallas_call(gather_rows_kernel, out_shape=[shape((8 * rows, width), lo...  50.6 us

profile of v5, /device:TPU:8, one launch (start us, length us, event | category | flops | bytes accessed | tf_op | source)
XLA Modules:
  0.0 657.2 jit_solution(690354729502409409)
XLA Ops:
  3.4 2.8 concatenate.64
  7.3 1.0 copy.63.refs_9_.refs_16_
  8.3 1.9 bitcast_select_fusion.refs_0_
  10.3 1.1 fusion.39
  11.6 1.9 fusion.10
  13.5 1.3 pad_maximum_fusion
  14.8 70.9 %gather_start.1 = (bf16[1024,2048]{1,0:T(8,128)(2,1)}, bf16[32,80,768]{2,1,0:T(8,128)(2,1)}, bf16[512,2048]{1,0:T(8,128)(2,1)}) custom-call(bf16[128,2048]{1,0:T(8,128)(2,1)} %bitcast.109, bf16[8,80,768]{2,1,0:T(8,128)(2,1)} %copy-done.7, bf16[128,2048]{1,0:T(8,128)(2,1)} %wo_in.1), custom_call_target="tpu_custom_call" | custom-call | tf_op jit(solution)/shard_map/gather_start/pallas_call | solution.py:1239
  85.7 1.2 slice.135
  89.8 76.7 %forward_gather.1 = (bf16[32,128,2048]{2,1,0:T(8,128)(2,1)}, bf16[1024,2048]{1,0:T(8,128)(2,1)}, f32[1024,640]{1,0:T(8,128)}, bf16[1024,512]{1,0:T(8,128)(2,1)},...) custom-call(bf16[128,2048]{1,0:T(8,128)(2,1)} %bitcast_select_fusion, ...), custom_call_target="tpu_custom_call" | custom-call | tf_op jit(solution)/shard_map/forward_gather/pallas_call | solution.py:1545
  166.5 59.1 %scatter_rows.1 = f32[128,2048]{1,0:T(8,128)} custom-call(bf16[1024,2048]{1,0:T(8,128)(2,1)} %get-tuple-element.59.part), custom_call_target="tpu_custom_call" | custom-call | tf_op jit(solution)/shard_map/scatter_rows/pallas_call | solution.py:1131
  225.6 1.5 multiply_reduce_fusion.2
  228.1 1.0 concatenate.82.refs_0_
  229.0 80.5 %gather_forward.1 = (bf16[32,128,2176]{2,1,0:T(8,128)(2,1)}, bf16[1152,2048]{1,0:T(8,128)(2,1)}, bf16[1152,2048]{1,0:T(8,128)(2,1)}, bf16[1152,128]{1,0:T(8,128)...) custom-call(bf16[128,2176]{1,0:T(8,128)(2,1)} %concatenate.82.refs_0, ...), custom_call_target="tpu_custom_call" | custom-call | tf_op jit(solution)/shard_map/gather_forward/pallas_call | solution.py:1766
  309.5 114.4 %expert_exchange.1 = (f32[128,2176]{1,0:T(8,128)}, bf16[16,96,2048]{2,1,0:T(8,128)(2,1)}, bf16[16,96,128]{2,1,0:T(8,128)(2,1)}, bf16[384,2048]{1,0:T(8,128)(2,1)...) custom-call(bf16[32,128,2176]{2,1,0:T(8,128)(2,1)} %get-tuple-elemen, ...), custom_call_target="tpu_custom_call" | custom-call | tf_op jit(solution)/shard_map/expert_exchange/pallas_call | solution.py:2182
  424.0 1.1 multiply_reduce_fusion.3
  425.1 2.3 fusion.46
  427.4 2.4 reshape.215
  429.9 2.0 multiply_reduce_fusion
  431.9 1.1 fusion.38.source
  433.1 50.6 %gather_rows.1 = (bf16[1024,2048]{1,0:T(8,128)(2,1)}, bf16[2048,768]{1,0:T(8,128)(2,1)}, bf16[2048,768]{1,0:T(8,128)(2,1)}, bf16[768,2048]{1,0:T(8,128)(2,1)}) custom-call(bf16[128,2048]{1,0:T(8,128)(2,1)} %fusion.38.source, bf16[384,2048]{1,0:T(8,128)(2,1)} %get-tuple-element.71.x_late, bf16[1152,2048]{1,0:T(8,128)(2,1)} %get-tuple-element.72.x_early, ...), custom_call_target="tpu_custom_call" | custom-call | tf_op jit(solution)/shard_map/gather_rows/pallas_call | solution.py:1049
  483.7 79.7 %backward_scatter.1 = (f32[128,2048]{1,0:T(8,128)}, bf16[512,2048]{1,0:T(8,128)(2,1)}, bf16[2048,768]{1,0:T(8,128)(2,1)}, bf16[1024,2048]{1,0:T(8,128)(2,1)}, f32[1,2048]{1,0:T(1,128)}, /*index=5*/f32[8,128]{1,0:T(8,128)}) custom-call(bf16[16,96,2048]{2,1,0:T(8,128)(2,1)} %get-tuple-element.68.refs_0_, bf16[16,96,128]{2,1,0:T(8,128)(2,1)} %get-tuple-element.69.refs_1_, ...), custom_call_target="tpu_custom_call" | custom-call | tf_op jit(solution)/shard_map/backward_scatter/pallas_call | solution.py:2444
  564.7 1.4 reduce.11
  566.4 1.1 concatenate.83
  568.4 65.1 %scatter_end.1 = (f32[128,2048]{1,0:T(8,128)}, bf16[8,64,768]{2,1,0:T(8,128)(2,1)}, f32[128,2048]{1,0:T(8,128)}, f32[32,128]{1,0:T(8,128)}) custom-call(bf16[1024,2048]{1,0:T(8,128)(2,1)} %get-tuple-element.86.part, bf16[8,2,2,64,768]{4,3,2,1,0:T(8,128)(2,1)} %bitcast.110, bf16[2,2,128,2048]{3,2,1,0:T(8,128)(2,1)} %bitcast.112, f32[8,2,2,32,128]{4,3,2,1,0:T(8,128)} %bitcast.113), custom_call_target="tpu_custom_call" | custom-call | tf_op jit(solution)/shard_map/scatter_end/pallas_call | solution.py:1368
  633.6 1.5 fusion.3
  635.1 3.4 fusion.7
  640.6 1.0 slice.162
  644.1 1.1 copy.77
  646.1 3.2 bitcast_convert_fusion.2
  649.3 3.2 bitcast_convert_fusion.1
  652.4 3.6 bitcast_convert_fusion
  656.0 1.0 copy.94
  (85 shorter events, 15.7 us)
Async XLA Ops:
  1.7 11.8 %copy-start.9 = (s32[1024]{0:T(1024)}, s32[1024]{0:T(1024)S(1)}, u32[]{:S(2)}) copy-start(s32[1024]{0:T(1024)S(1)} %convert_reduce_fusion) | copy-start | bytes 12292
  11.5 3.2 copy-start.7
  89.8 137.5 %copy-start.2 = (bf16[2048,32]{1,0:T(8,128)(2,1)}, bf16[2048,32]{1,0:T(8,128)(2,1)S(1)}, u32[]{:S(2)}) copy-start(bf16[2048,32]{1,0:T(8,128)(2,1)S(1)} %reshape.210) | copy-start | bytes 393220
  166.5 59.1 %copy-start = (bf16[1,128,2048]{2,1,0:T(8,128)(2,1)S(1)}, bf16[1,128,2048]{2,1,0:T(8,128)(2,1)}, u32[]{:S(2)}) copy-start(bf16[1,128,2048]{2,1,0:T(8,128)(2,1)} %param.16) | copy-start | bytes 1572868
  424.0 8.0 %copy-start.1 = (bf16[1,128,2048]{2,1,0:T(8,128)(2,1)S(1)}, bf16[1,128,2048]{2,1,0:T(8,128)(2,1)}, u32[]{:S(2)}) copy-start(bf16[1,128,2048]{2,1,0:T(8,128)(2,1)} %param.17) | copy-start | bytes 1572868
  635.1 3.4 copy-start.10
  638.6 5.2 copy-start.6
  643.8 2.3 copy-start.5
  646.1 3.2 copy-start.4
  649.2 3.2 copy-start.3
  652.4 3.6 copy-start.8

commit v6 on v5

--- a/solution.py
+++ b/solution.py
@@ -1954,8 +1954,14 @@
         cross(0)
         along(2)
 
-    at_start = {4: lambda: cross(3), 5: lambda: cross(2), 6: sixth, 7: last}
-    at_middle = {1: lambda: corners(2, 0), 2: lambda: corners(3, 1)}
+    at_start = {
+        1: lambda: corners(2, 0),
+        2: lambda: corners(3, 1),
+        4: lambda: cross(3),
+        5: lambda: cross(2),
+        6: sixth,
+        7: last,
+    }
 
     def at(g, table):
         for n, work in table.items():
@@ -2081,7 +2087,6 @@
             for copy in early_copies(g):
                 copy.wait()
 
-        at(g, at_middle)
         gates = jnp.sum(
             jnp.where(is_gate, extra_ref[side].astype(SINGLE_FLOAT), 0.0), axis=-1, keepdims=True
         )

time: 662 us -> 659 us (level)
  no operation moved by 1% of the time
where the time goes in v6:
time: 659 us; the launch traced here: 655 us
  Pallas kernels  595 us (90%)
  other arithmetic  28.2 us (4%)
  local copies, waits for them, and re-layouts  25.7 us (4%)
    pallas_call x1, Pallas kernels, expert_exchange(): pl.pallas_call(kernel, out_shape=(shape((tokens, wide), SINGLE_FLOAT), sh...  112 us
    pallas_call x1, Pallas kernels, gather_forward(): pl.pallas_call(kernel, out_shape=[shape((32, tokens, wide), low)] + [shap...  80.5 us
    pallas_call x1, Pallas kernels, backward_scatter(): pl.pallas_call(kernel, out_shape=shapes, in_specs=[ANYWHERE] * 12 + [VMEM...  79.8 us
    pallas_call x1, Pallas kernels, forward_gather(): pl.pallas_call(kernel, out_shape=[shape((32,) + block.shape, low)] + [sha...  76.7 us
    pallas_call x1, Pallas kernels, gather_start(): pl.pallas_call(gather_start_kernel, out_shape=(jax.ShapeDtypeStruct((8 *...  70.9 us
    pallas_call x1, Pallas kernels, scatter_end(): pl.pallas_call(scatter_end_kernel, out_shape=(jax.ShapeDtypeStruct((rows,...  65.5 us
    pallas_call x1, Pallas kernels, scatter_rows(): pl.pallas_call(scatter_rows_kernel, out_shape=jax.ShapeDtypeStruct((rows,...  59.1 us
    pallas_call x1, Pallas kernels, gather_rows(): pl.pallas_call(gather_rows_kernel, out_shape=[shape((8 * rows, width), lo...  50.7 us

profile of v6, /device:TPU:8, one launch (start us, length us, event | category | flops | bytes accessed | tf_op | source)
XLA Modules:
  0.0 655.0 jit_solution(15765978983838785534)
XLA Ops:
  3.4 2.8 concatenate.64
  7.3 1.0 copy.63.refs_9_.refs_16_
  8.3 1.9 bitcast_select_fusion.refs_0_
  10.3 1.1 fusion.39
  11.6 1.9 fusion.10
  13.5 1.3 pad_maximum_fusion
  14.8 70.9 %gather_start.1 = (bf16[1024,2048]{1,0:T(8,128)(2,1)}, bf16[32,80,768]{2,1,0:T(8,128)(2,1)}, bf16[512,2048]{1,0:T(8,128)(2,1)}) custom-call(bf16[128,2048]{1,0:T(8,128)(2,1)} %bitcast.109, bf16[8,80,768]{2,1,0:T(8,128)(2,1)} %copy-done.7, bf16[128,2048]{1,0:T(8,128)(2,1)} %wo_in.1), custom_call_target="tpu_custom_call" | custom-call | tf_op jit(solution)/shard_map/gather_start/pallas_call | solution.py:1239
  85.7 1.2 slice.135
  89.8 76.7 %forward_gather.1 = (bf16[32,128,2048]{2,1,0:T(8,128)(2,1)}, bf16[1024,2048]{1,0:T(8,128)(2,1)}, f32[1024,640]{1,0:T(8,128)}, bf16[1024,512]{1,0:T(8,128)(2,1)},...) custom-call(bf16[128,2048]{1,0:T(8,128)(2,1)} %bitcast_select_fusion, ...), custom_call_target="tpu_custom_call" | custom-call | tf_op jit(solution)/shard_map/forward_gather/pallas_call | solution.py:1545
  166.5 59.1 %scatter_rows.1 = f32[128,2048]{1,0:T(8,128)} custom-call(bf16[1024,2048]{1,0:T(8,128)(2,1)} %get-tuple-element.59.part), custom_call_target="tpu_custom_call" | custom-call | tf_op jit(solution)/shard_map/scatter_rows/pallas_call | solution.py:1131
  225.6 1.5 multiply_reduce_fusion.2
  228.1 1.0 concatenate.82.refs_0_
  229.0 80.5 %gather_forward.1 = (bf16[32,128,2176]{2,1,0:T(8,128)(2,1)}, bf16[1152,2048]{1,0:T(8,128)(2,1)}, bf16[1152,2048]{1,0:T(8,128)(2,1)}, bf16[1152,128]{1,0:T(8,128)...) custom-call(bf16[128,2176]{1,0:T(8,128)(2,1)} %concatenate.82.refs_0, ...), custom_call_target="tpu_custom_call" | custom-call | tf_op jit(solution)/shard_map/gather_forward/pallas_call | solution.py:1766
  309.5 111.8 %expert_exchange.1 = (f32[128,2176]{1,0:T(8,128)}, bf16[16,96,2048]{2,1,0:T(8,128)(2,1)}, bf16[16,96,128]{2,1,0:T(8,128)(2,1)}, bf16[384,2048]{1,0:T(8,128)(2,1)...) custom-call(bf16[32,128,2176]{2,1,0:T(8,128)(2,1)} %get-tuple-elemen, ...), custom_call_target="tpu_custom_call" | custom-call | tf_op jit(solution)/shard_map/expert_exchange/pallas_call | solution.py:2187
  421.4 1.1 multiply_reduce_fusion.3
  422.5 2.3 fusion.46
  424.8 2.4 reshape.215
  427.2 2.0 multiply_reduce_fusion
  429.3 1.1 fusion.38.source
  430.5 50.7 %gather_rows.1 = (bf16[1024,2048]{1,0:T(8,128)(2,1)}, bf16[2048,768]{1,0:T(8,128)(2,1)}, bf16[2048,768]{1,0:T(8,128)(2,1)}, bf16[768,2048]{1,0:T(8,128)(2,1)}) custom-call(bf16[128,2048]{1,0:T(8,128)(2,1)} %fusion.38.source, bf16[384,2048]{1,0:T(8,128)(2,1)} %get-tuple-element.71.x_late, bf16[1152,2048]{1,0:T(8,128)(2,1)} %get-tuple-element.72.x_early, ...), custom_call_target="tpu_custom_call" | custom-call | tf_op jit(solution)/shard_map/gather_rows/pallas_call | solution.py:1049
  481.1 79.8 %backward_scatter.1 = (f32[128,2048]{1,0:T(8,128)}, bf16[512,2048]{1,0:T(8,128)(2,1)}, bf16[2048,768]{1,0:T(8,128)(2,1)}, bf16[1024,2048]{1,0:T(8,128)(2,1)}, f32[1,2048]{1,0:T(1,128)}, /*index=5*/f32[8,128]{1,0:T(8,128)}) custom-call(bf16[16,96,2048]{2,1,0:T(8,128)(2,1)} %get-tuple-element.68.refs_0_, bf16[16,96,128]{2,1,0:T(8,128)(2,1)} %get-tuple-element.69.refs_1_, ...), custom_call_target="tpu_custom_call" | custom-call | tf_op jit(solution)/shard_map/backward_scatter/pallas_call | solution.py:2449
  562.2 1.4 reduce.11
  563.9 1.1 concatenate.83
  566.0 65.5 %scatter_end.1 = (f32[128,2048]{1,0:T(8,128)}, bf16[8,64,768]{2,1,0:T(8,128)(2,1)}, f32[128,2048]{1,0:T(8,128)}, f32[32,128]{1,0:T(8,128)}) custom-call(bf16[1024,2048]{1,0:T(8,128)(2,1)} %get-tuple-element.86.part, bf16[8,2,2,64,768]{4,3,2,1,0:T(8,128)(2,1)} %bitcast.110, bf16[2,2,128,2048]{3,2,1,0:T(8,128)(2,1)} %bitcast.112, f32[8,2,2,32,128]{4,3,2,1,0:T(8,128)} %bitcast.113), custom_call_target="tpu_custom_call" | custom-call | tf_op jit(solution)/shard_map/scatter_end/pallas_call | solution.py:1368
  631.4 1.5 fusion.3
  633.0 3.4 fusion.7
  638.4 1.0 slice.162
  641.9 1.1 copy.77
  643.9 3.2 bitcast_convert_fusion.2
  647.1 3.2 bitcast_convert_fusion.1
  650.3 3.6 bitcast_convert_fusion
  653.8 1.0 copy.94
  (85 shorter events, 15.7 us)
Async XLA Ops:
  1.7 11.8 %copy-start.9 = (s32[1024]{0:T(1024)}, s32[1024]{0:T(1024)S(1)}, u32[]{:S(2)}) copy-start(s32[1024]{0:T(1024)S(1)} %convert_reduce_fusion) | copy-start | bytes 12292
  11.5 3.2 copy-start.7
  89.8 137.5 %copy-start.2 = (bf16[2048,32]{1,0:T(8,128)(2,1)}, bf16[2048,32]{1,0:T(8,128)(2,1)S(1)}, u32[]{:S(2)}) copy-start(bf16[2048,32]{1,0:T(8,128)(2,1)S(1)} %reshape.210) | copy-start | bytes 393220
  166.5 59.1 %copy-start = (bf16[1,128,2048]{2,1,0:T(8,128)(2,1)S(1)}, bf16[1,128,2048]{2,1,0:T(8,128)(2,1)}, u32[]{:S(2)}) copy-start(bf16[1,128,2048]{2,1,0:T(8,128)(2,1)} %param.16) | copy-start | bytes 1572868
  421.3 8.0 %copy-start.1 = (bf16[1,128,2048]{2,1,0:T(8,128)(2,1)S(1)}, bf16[1,128,2048]{2,1,0:T(8,128)(2,1)}, u32[]{:S(2)}) copy-start(bf16[1,128,2048]{2,1,0:T(8,128)(2,1)} %param.17) | copy-start | bytes 1572868
  633.0 3.4 copy-start.10
  636.4 5.2 copy-start.6
  641.6 2.3 copy-start.5
  643.9 3.2 copy-start.4
  647.1 3.2 copy-start.3
  650.3 3.6 copy-start.8
